TPU v7x, 32 devices: a whole 2x2x4 slice. The times are simulated.
32 devices in a mesh: img: 8 (over z, x), row: 4 (over y, core).
Axes of the slice: x: 2, y: 2, z: 4, core: 2. Of those that a mesh axis runs over, the one named last changes fastest.
Arguments:
- feature_map: bfloat16 [448, 24, 16, 1024], P('img', 'row'), may hold values from -6 to 6
- image_group: int32 [448], P('img'), may hold values from 0 to 2, as said below
- row_counts: int32 [448, 4], P('img', 'row'), may hold values from 1 to 6, as said below
- reduce_weight: bfloat16 [1024, 256], replicated, may hold values from -0.1875 to 0.1875
- gain_first: float32 [256], replicated, may hold values from 0.25 to 1.75
- shift_first: float32 [256], replicated, may hold values from -0.5 to 0.5
- split_weight: bfloat16 [3, 3, 128, 512], replicated, may hold values from -0.1875 to 0.1875
- gain_second: float32 [512], replicated, may hold values from 0.25 to 1.75
- shift_second: float32 [512], replicated, may hold values from -0.5 to 0.5
- attn_down: bfloat16 [256, 128], replicated, may hold values from -0.375 to 0.375
- gain_attend: float32 [128], replicated, may hold values from 0.25 to 1.75
- shift_attend: float32 [128], replicated, may hold values from -0.5 to 0.5
- attn_up: bfloat16 [128, 512], replicated, may hold values from -0.5 to 0.5
- attn_bias: float32 [512], replicated, may hold values from -1 to 1
- expand_weight: bfloat16 [256, 1024], replicated, may hold values from -0.375 to 0.375
- gain_third: float32 [1024], replicated, may hold values from 0.25 to 1.75
- shift_third: float32 [1024], replicated, may hold values from -0.5 to 0.5
- cotangent: bfloat16 [448, 24, 16, 1024], P('img', 'row'), may hold values from -6 to 6
Outputs:
- block_out: bfloat16 [448, 24, 16, 1024], P('img', 'row')
- grad_input: bfloat16 [448, 24, 16, 1024], P('img', 'row')
- grad_reduce: float32 [1024, 256], P('row')
- grad_split: float32 [3, 3, 128, 512], P(None, None, 'row')
- grad_expand: float32 [256, 1024], P('row')
- grad_down: float32 [256, 128], replicated
- grad_up: float32 [128, 512], replicated
- grad_bias: float32 [512], replicated
- grad_gain_first: float32 [256], replicated
- grad_shift_first: float32 [256], replicated
- grad_gain_second: float32 [512], replicated
- grad_shift_second: float32 [512], replicated
- grad_gain_attend: float32 [128], replicated
- grad_shift_attend: float32 [128], replicated
- grad_gain_third: float32 [1024], replicated
- grad_shift_third: float32 [1024], replicated
Inputs may be any that keep to these rules, and one draw needn't show every extreme that they name: Image i is 12 + 2 * image_group[i] rows tall and as wide; image 0 is of group 2. `row_counts`: for each image the counts over the 4 devices of row sum to its height; every device holds at least one row of every image; some image has 6 rows on one device.
All inputs are finite; a program needn't handle non-finite values.
Results may differ from a plain program's by a relative error of at most 0.0081.
Values may be sent and summed in bfloat16 or wider, within the bound.
A program may use at most 512 MiB of HBM per device.

v0:
```python
import jax
import jax.numpy as jnp
from jax import lax
from jax.sharding import PartitionSpec as P

HIGH = lax.Precision.HIGHEST
EPS = 1e-05


def with_halo(cells, sides, width):
    for axis, dim in sides:
        count = lax.axis_size(axis)
        ends = count - 1
        head = lax.slice_in_dim(cells, 0, width, axis=dim)
        tail = lax.slice_in_dim(cells, cells.shape[dim] - width, cells.shape[dim], axis=dim)
        cells = jnp.concatenate(
            [
                lax.ppermute(tail, axis, [(i, (i + 1) % count) for i in range(ends)]),
                cells,
                lax.ppermute(head, axis, [((i + 1) % count, i) for i in range(ends)]),
            ],
            axis=dim,
        )
    return cells


def pixel_total(values):
    partial_sums = lax.psum(values, "row")
    return lax.psum(partial_sums, "img")


def image_total(values):
    return lax.psum((values[0], values[1]), "img")


def row_total(values):
    return lax.psum(values, "row")


def edge_swap(edges):
    return with_halo(edges, (("row", 1),), 1)


def swish_slope(values):
    sigmoid = jax.nn.sigmoid(values)
    return sigmoid * (1.0 + values * (1.0 - sigmoid))


def norm_stats(values, weight_mask):
    weighted = values * weight_mask
    return (jnp.sum(weighted, axis=0), jnp.sum(weighted * values, axis=0))


def norm_apply(values, weight_mask, count, totals, gain, shift):
    center = totals[0] / count
    spread = totals[1] / count - center * center
    factor = lax.rsqrt(spread + EPS)
    normed = (values - center) * factor
    return (normed, factor, (normed * gain + shift) * weight_mask)


def norm_back(upstream, normed, factor, weight_mask, count, gain, totals):
    return gain * factor * (upstream - totals[0] / count - normed * totals[1] / count) * weight_mask


def gather_taps(source, slots, columns):
    taps = []
    for row_step in range(3):
        for col_step in range(3):
            taps.append(source[:, row_step : row_step + slots, col_step : col_step + columns, :])
    return jnp.concatenate(taps, axis=-1)


def body(
    feature_map,
    image_group,
    row_counts,
    reduce_weight,
    gain_first,
    shift_first,
    split_weight,
    gain_second,
    shift_second,
    attn_down,
    gain_attend,
    shift_attend,
    attn_up,
    attn_bias,
    expand_weight,
    gain_third,
    shift_third,
    cotangent,
):
    images, slots, columns, channels = feature_map.shape
    middle = reduce_weight.shape[1]
    half = middle // 2
    pixels = images * slots * columns
    height = 12 + 2 * image_group
    counts = row_counts[:, 0]
    row_index = jnp.arange(slots, dtype=jnp.int32)
    col_index = jnp.arange(columns, dtype=jnp.int32)
    image_index = jnp.arange(images, dtype=jnp.int32)
    validity = (
        (row_index[None, :, None] < counts[:, None, None])
        & (col_index[None, None, :] < height[:, None, None])
    ).astype(jnp.float32)
    weight_mask = validity.reshape(pixels, 1)
    inputs = feature_map.reshape(pixels, channels)
    first_pre = jnp.dot(inputs, reduce_weight, preferred_element_type=jnp.float32)
    first_sum, first_square = norm_stats(first_pre, weight_mask)
    first_sum, first_square, count = pixel_total((first_sum, first_square, jnp.sum(weight_mask)))
    first_norm, first_factor, first_out = norm_apply(
        first_pre, weight_mask, count, (first_sum, first_square), gain_first, shift_first
    )
    first_act = jax.nn.silu(first_out).astype(jnp.bfloat16).reshape(images, slots, columns, middle)
    edges = jnp.stack([first_act[:, 0], first_act[image_index, counts - 1]], axis=1)
    haloed = edge_swap(edges)
    above = haloed[:, 0]
    below = haloed[:, 3]
    extended = jnp.concatenate([above[:, None], first_act, jnp.zeros_like(above)[:, None]], axis=1)
    ext_rows = jnp.arange(slots + 2, dtype=jnp.int32)
    below_pick = (ext_rows[None, :] == (counts + 1)[:, None])[:, :, None, None]
    extended = jnp.where(below_pick, below[:, None], extended)
    extended = jnp.pad(extended, ((0, 0), (0, 0), (1, 1), (0, 0)))
    kernel = split_weight.reshape(9 * half, 2 * middle)
    taps_zero = gather_taps(extended[..., :half], slots, columns).reshape(pixels, 9 * half)
    taps_one = gather_taps(extended[..., half:], slots, columns).reshape(pixels, 9 * half)
    second_pre = jnp.concatenate(
        [
            jnp.dot(taps_zero, kernel[:, :middle], preferred_element_type=jnp.float32),
            jnp.dot(taps_one, kernel[:, middle:], preferred_element_type=jnp.float32),
        ],
        axis=1,
    )
    second_totals = pixel_total(norm_stats(second_pre, weight_mask))
    second_norm, second_factor, second_out = norm_apply(
        second_pre, weight_mask, count, second_totals, gain_second, shift_second
    )
    second_act = jax.nn.silu(second_out)
    per_image = second_act.reshape(images, slots * columns, 2 * middle)
    part_zero = per_image[..., :middle]
    part_one = per_image[..., middle:]
    area = (height * height).astype(jnp.float32)[:, None]
    pooled = row_total(jnp.sum(part_zero + part_one, axis=1)) / area
    down_float = attn_down.astype(jnp.float32)
    up_float = attn_up.astype(jnp.float32)
    squeeze = jnp.dot(pooled, down_float, precision=HIGH)
    attend_totals = image_total((jnp.sum(squeeze, axis=0), jnp.sum(squeeze * squeeze, axis=0)))
    image_count = jnp.float32(images * lax.axis_size("img"))
    attend_norm, attend_factor, attend_out = norm_apply(
        squeeze, 1.0, image_count, attend_totals, gain_attend, shift_attend
    )
    attend = jax.nn.silu(attend_out)
    logits = jnp.dot(attend, up_float, precision=HIGH) + attn_bias
    weights = jax.nn.softmax(logits.reshape(images, 2, middle), axis=1)
    mixed = weights[:, 0, None, :] * part_zero + weights[:, 1, None, :] * part_one
    mixed = mixed.astype(jnp.bfloat16).reshape(pixels, middle)
    third_pre = jnp.dot(mixed, expand_weight, preferred_element_type=jnp.float32)
    third_totals = pixel_total(norm_stats(third_pre, weight_mask))
    third_norm, third_factor, third_out = norm_apply(
        third_pre, weight_mask, count, third_totals, gain_third, shift_third
    )
    summed = third_out + inputs.astype(jnp.float32)
    block_out = (
        (jax.nn.silu(summed) * weight_mask)
        .astype(jnp.bfloat16)
        .reshape(images, slots, columns, channels)
    )
    upstream = cotangent.astype(jnp.float32).reshape(pixels, channels) * weight_mask
    summed_grad = upstream * swish_slope(summed)
    third_back = pixel_total(
        (jnp.sum(summed_grad, axis=0), jnp.sum(summed_grad * third_norm, axis=0))
    )
    third_grad = norm_back(
        summed_grad, third_norm, third_factor, weight_mask, count, gain_third, third_back
    ).astype(jnp.bfloat16)
    expand_part = jnp.einsum("pm,pc->mc", mixed, third_grad, preferred_element_type=jnp.float32)
    mixed_grad = jnp.einsum(
        "pc,mc->pm", third_grad, expand_weight, preferred_element_type=jnp.float32
    )
    mixed_rows = mixed_grad.reshape(images, slots * columns, middle)
    weight_part = jnp.concatenate(
        [jnp.sum(mixed_rows * part_zero, axis=1), jnp.sum(mixed_rows * part_one, axis=1)], axis=1
    )
    weight_grad = row_total(weight_part).reshape(images, 2, middle)
    logit_grad = weights * (weight_grad - jnp.sum(weights * weight_grad, axis=1, keepdims=True))
    logit_grad = logit_grad.reshape(images, 2 * middle)
    up_part = jnp.einsum("ik,ij->kj", attend, logit_grad, precision=HIGH)
    bias_part = jnp.sum(logit_grad, axis=0)
    attend_grad = jnp.einsum("ij,kj->ik", logit_grad, up_float, precision=HIGH) * swish_slope(
        attend_out
    )
    attend_back = image_total(
        (jnp.sum(attend_grad, axis=0), jnp.sum(attend_grad * attend_norm, axis=0))
    )
    squeeze_grad = norm_back(
        attend_grad, attend_norm, attend_factor, 1.0, image_count, gain_attend, attend_back
    )
    down_part = jnp.einsum("im,ik->mk", pooled, squeeze_grad, precision=HIGH)
    pooled_grad = jnp.einsum("ik,mk->im", squeeze_grad, down_float, precision=HIGH) / area
    act_rows = jnp.concatenate(
        [
            weights[:, 0, None, :] * mixed_rows + pooled_grad[:, None, :],
            weights[:, 1, None, :] * mixed_rows + pooled_grad[:, None, :],
        ],
        axis=2,
    )
    second_up = act_rows.reshape(pixels, 2 * middle) * swish_slope(second_out) * weight_mask
    second_back = pixel_total(
        (jnp.sum(second_up, axis=0), jnp.sum(second_up * second_norm, axis=0))
    )
    second_grad = norm_back(
        second_up, second_norm, second_factor, weight_mask, count, gain_second, second_back
    ).astype(jnp.bfloat16)
    grad_zero = second_grad[:, :middle]
    grad_one = second_grad[:, middle:]
    split_part = jnp.concatenate(
        [
            jnp.einsum("pk,pj->kj", taps_zero, grad_zero, preferred_element_type=jnp.float32),
            jnp.einsum("pk,pj->kj", taps_one, grad_one, preferred_element_type=jnp.float32),
        ],
        axis=1,
    ).reshape(3, 3, half, 2 * middle)
    taps_back_zero = jnp.einsum(
        "pj,kj->pk", grad_zero, kernel[:, :middle], preferred_element_type=jnp.float32
    )
    taps_back_one = jnp.einsum(
        "pj,kj->pk", grad_one, kernel[:, middle:], preferred_element_type=jnp.float32
    )
    taps_back = jnp.concatenate(
        [
            taps_back_zero.reshape(images, slots, columns, 9, half),
            taps_back_one.reshape(images, slots, columns, 9, half),
        ],
        axis=4,
    )
    ext_grad = jnp.zeros((images, slots + 2, columns + 2, middle), jnp.float32)
    for row_step in range(3):
        for col_step in range(3):
            ext_grad = ext_grad + jnp.pad(
                taps_back[:, :, :, 3 * row_step + col_step, :],
                ((0, 0), (row_step, 2 - row_step), (col_step, 2 - col_step), (0, 0)),
            )
    ext_grad = ext_grad[:, :, 1 : columns + 1]
    act_grad = ext_grad[:, 1 : slots + 1]
    edge_back = jnp.stack([ext_grad[:, 0], ext_grad[image_index, counts + 1]], axis=1)
    returned = with_halo(edge_back.astype(jnp.bfloat16), (("row", 1),), 1).astype(edge_back.dtype)
    first_pick = (row_index == 0)[None, :, None, None]
    last_pick = (row_index[None, :] == (counts - 1)[:, None])[:, :, None, None]
    act_grad = act_grad + jnp.where(first_pick, returned[:, 0][:, None], 0.0)
    act_grad = act_grad + jnp.where(last_pick, returned[:, 3][:, None], 0.0)
    first_up = act_grad.reshape(pixels, middle) * swish_slope(first_out) * weight_mask
    first_back = pixel_total((jnp.sum(first_up, axis=0), jnp.sum(first_up * first_norm, axis=0)))
    first_grad = norm_back(
        first_up, first_norm, first_factor, weight_mask, count, gain_first, first_back
    ).astype(jnp.bfloat16)
    reduce_part = jnp.einsum("pc,pm->cm", inputs, first_grad, preferred_element_type=jnp.float32)
    input_grad = summed_grad + jnp.einsum(
        "pm,cm->pc", first_grad, reduce_weight, preferred_element_type=jnp.float32
    )
    grad_input = (
        (input_grad * weight_mask).astype(jnp.bfloat16).reshape(images, slots, columns, channels)
    )
    reduce_whole, split_whole, expand_whole = lax.psum(
        (reduce_part, split_part, expand_part), ("img", "row")
    )
    place = lax.axis_index("row")
    parts = lax.axis_size("row")
    grad_reduce = lax.dynamic_slice_in_dim(
        reduce_whole, place * (channels // parts), channels // parts, 0
    )
    grad_split = lax.dynamic_slice_in_dim(split_whole, place * (half // parts), half // parts, 2)
    grad_expand = lax.dynamic_slice_in_dim(
        expand_whole, place * (middle // parts), middle // parts, 0
    )
    grad_down, grad_up, grad_bias = lax.psum((down_part, up_part, bias_part), "img")
    return (
        block_out,
        grad_input,
        grad_reduce,
        grad_split,
        grad_expand,
        grad_down,
        grad_up,
        grad_bias,
        first_back[1],
        first_back[0],
        second_back[1],
        second_back[0],
        attend_back[1],
        attend_back[0],
        third_back[1],
        third_back[0],
    )


def solution(mesh):
    in_specs = (
        P("img", "row", None, None),
        P("img"),
        P("img", "row"),
        P(),
        P(),
        P(),
        P(),
        P(),
        P(),
        P(),
        P(),
        P(),
        P(),
        P(),
        P(),
        P(),
        P(),
        P("img", "row", None, None),
    )
    out_specs = (
        P("img", "row", None, None),
        P("img", "row", None, None),
        P("row", None),
        P(None, None, "row", None),
        P("row", None),
        P(),
        P(),
        P(),
        P(),
        P(),
        P(),
        P(),
        P(),
        P(),
        P(),
        P(),
    )
    return jax.shard_map(body, mesh=mesh, in_specs=in_specs, out_specs=out_specs, check_vma=False)
```

profile of v0, /device:TPU:0, one launch (start us, length us, event | category | flops | bytes accessed | tf_op | source)
XLA Modules:
  0.0 1062.4 jit_solution(9835809862918239662)
XLA Ops:
  17.6 9.0 all-reduce.25
  26.6 22.3 %all-reduce.18 = (f32[256]{0:T(256)S(1)}, f32[]{:T(128)}, f32[256]{0:T(256)S(1)}) all-reduce(f32[256]{0:T(256)S(1)} %get-tuple-element.99, f32[]{:T(128)} %get-tuple-element.100, f32[256]{0:T(256)S(1)} %get-tuple-element.101), channel_id=1, replica_groups=mesh['img'=8,'row'=4] {'img'}, use_global_device_ids=true, to_apply=%region_2.0 | all-reduce | flops 513 | bytes 4104 | tf_op jit(solution)/shard_map/psum | solution.py:29
  81.0 11.3 %fusion.36 = f32[5376,256]{1,0:T(8,128)S(1)} fusion(bf16[5376,1152]{1,0:T(8,128)(2,1)} %bitcast.171, bf16[1152,512]{1,0:T(8,128)(2,1)S(1)} %bitcast.158), kind=kOutput, calls=%fused_computation.112 | convolution fusion | flops 3170893824 | bytes 18481152 | tf_op jit(solution)/shard_map/dot_general | solution.py:130
  98.8 9.4 all-reduce.24
  108.3 17.1 %all-reduce.17 = (f32[512]{0:T(512)S(1)}, f32[512]{0:T(512)S(1)}) all-reduce(f32[512]{0:T(512)S(1)} %get-tuple-element.97, f32[512]{0:T(512)S(1)} %get-tuple-element.98), channel_id=1, replica_groups=mesh['img'=8,'row'=4] {'img'}, use_global_device_ids=true, to_apply=%region_14.15 | all-reduce | flops 1024 | bytes 8192 | tf_op jit(solution)/shard_map/psum | solution.py:29
  138.6 10.7 %psum.276 = f32[56,256]{1,0:T(8,128)S(1)} all-reduce(f32[56,256]{1,0:T(8,128)S(1)} %add_reduce_fusion), channel_id=1, replica_groups=mesh['img'=8,'row'=4] {'row'}, use_global_device_ids=true, to_apply=%region_16.17 | all-reduce | flops 14336 | bytes 114688 | tf_op jit(solution)/shard_map/psum | solution.py:37
  149.6 19.6 %all-reduce.16 = (f32[128]{0:T(128)S(1)}, f32[128]{0:T(128)S(1)}) all-reduce(f32[128]{0:T(128)S(1)} %get-tuple-element.65, f32[128]{0:T(128)S(1)} %get-tuple-element.64), channel_id=1, replica_groups=mesh['img'=8,'row'=4] {'img'}, use_global_device_ids=true, to_apply=%region_20.21 | all-reduce | flops 256 | bytes 2048 | tf_op jit(solution)/shard_map/psum | solution.py:33
  177.1 9.3 fusion.1
  192.9 18.1 %all-reduce.15 = (f32[1024]{0:T(1024)}, f32[1024]{0:T(1024)S(1)}) all-reduce(f32[1024]{0:T(1024)S(1)} %get-tuple-element.95, f32[1024]{0:T(1024)} %get-tuple-element.96), channel_id=1, replica_groups=mesh['img'=8,'row'=4] {'img'}, use_global_device_ids=true, to_apply=%region_25.26 | all-reduce | flops 2048 | bytes 16384 | tf_op jit(solution)/shard_map/psum | solution.py:29
  213.6 33.5 %fusion.54 = (f32[1024]{0:T(1024)S(1)}, f32[1024]{0:T(1024)}, f32[5376,1024]{1,0:T(8,128)}, bf16[5376,1024]{1,0:T(8,128)(2,1)}) fusion(f32[1024]{0:T(1024)S(1)} %add_rsqrt_fusion, f32[5376,1024]{1,0:T(8,128)} %get-tuple-element.144, f32[1024]{0:T(1024)S(1)} %get-tuple-element.112, bf16[56,6,16,1024]{3,2,1,0:T(8,128)(2,1)} %param.18, f32[1024]{0:T(1024)} %param.34, ...), kind=kLoop, calls=%fused_computation.180 | loop fusion | flops 126613504 | bytes 77116416 | tf_op jit(solution)/shard_map/reduce_sum | solution.py:172
  253.6 20.1 %all-reduce.14 = (f32[1024]{0:T(1024)S(1)}, f32[1024]{0:T(1024)}) all-reduce(f32[1024]{0:T(1024)} %get-tuple-element.93, f32[1024]{0:T(1024)} %get-tuple-element.94), channel_id=1, replica_groups=mesh['img'=8,'row'=4] {'img'}, use_global_device_ids=true, to_apply=%region_34.35 | all-reduce | flops 2048 | bytes 16384 | tf_op jit(solution)/shard_map/psum | solution.py:29
  275.1 16.4 %multiply_convert_fusion.1 = bf16[5376,1024]{1,0:T(8,128)(2,1)S(1)} fusion(f32[5376,1024]{1,0:T(8,128)} %get-tuple-element.113, f32[5376,1024]{1,0:T(8,128)} %get-tuple-element.144, f32[]{:T(128)} %get-tuple-element.85, f32[1024]{0:T(1024)S(1)} %get-tuple-element.162, f32[1024]{0:T(1024)S(1)} %broadcast_divide_fusion.3, f32[1024]{0:T(1024)} %get-tuple-element.111, ...), kind=kLoop, calls=%fused_computation.9 | loop fusion | flops 49545216 | bytes 55092228 | tf_op jit(solution)/shard_map/convert_element_type | solution.py:176
  303.8 8.3 fusion.68
  312.2 19.6 %all-reduce.30.cloned.1.call-done = f32[56,512]{1,0:T(8,128)} async-done(((f32[56,512]{1,0:T(8,128)}), f32[56,512]{1,0:T(8,128)}) %all-reduce.30.cloned.1.call-update) | async-done | bytes 114704 | tf_op jit(solution)/shard_map/psum | solution.py:37
  334.8 21.4 %all-reduce.13 = (f32[128]{0:T(128)S(1)}, f32[128]{0:T(128)S(1)}) all-reduce(f32[128]{0:T(128)S(1)} %get-tuple-element.63, f32[128]{0:T(128)S(1)} %get-tuple-element.62), channel_id=1, replica_groups=mesh['img'=8,'row'=4] {'img'}, use_global_device_ids=true, to_apply=%region_42.43 | all-reduce | flops 256 | bytes 2048 | tf_op jit(solution)/shard_map/psum | solution.py:33
  361.5 11.9 %fusion.55 = (f32[512]{0:T(512)S(1)}, f32[512]{0:T(512)S(1)}, f32[5376,512]{1,0:T(8,128)}) fusion(f32[512]{0:T(512)S(1)} %get-tuple-element.109, f32[512]{0:T(512)S(1)} %get-tuple-element.132, f32[5376,256]{1,0:T(8,128)} %copy-done.4, f32[5376,256]{1,0:T(8,128)S(1)} %bitcast.118, f32[5376]{0:T(1024)S(1)} %reshape.292, f32[512]{0:T(512)S(1)} %copy-done.44, ...), kind=kLoop, calls=%fused_computation.181 | loop fusion | flops 52296704 | bytes 33063936 | tf_op jit(solution)/shard_map/reduce_sum | solution.py:210
  379.1 17.3 %all-reduce.12 = (f32[512]{0:T(512)S(1)}, f32[512]{0:T(512)S(1)}) all-reduce(f32[512]{0:T(512)S(1)} %get-tuple-element.91, f32[512]{0:T(512)S(1)} %get-tuple-element.92), channel_id=1, replica_groups=mesh['img'=8,'row'=4] {'img'}, use_global_device_ids=true, to_apply=%region_48.49 | all-reduce | flops 1024 | bytes 8192 | tf_op jit(solution)/shard_map/psum | solution.py:29
  397.1 9.5 multiply_convert_fusion.3
  406.7 10.0 fusion.16
  416.7 10.1 fusion.14
  426.8 10.1 fusion.18
  436.9 31.1 %reshape.287 = f32[56,6,16,9,128]{4,3,2,1,0:T(8,128)} reshape(f32[5376,1152]{1,0:T(8,128)} %fusion.18) | data formatting | bytes 49545216 | tf_op jit(solution)/shard_map/reshape | solution.py:232
  468.0 31.2 %reshape.288 = f32[56,6,16,9,128]{4,3,2,1,0:T(8,128)} reshape(f32[5376,1152]{1,0:T(8,128)} %fusion.14) | data formatting | bytes 49545216 | tf_op jit(solution)/shard_map/reshape | solution.py:233
  499.2 31.3 %constant_dynamic-update-slice_fusion.1 = f32[56,6,16,9,256]{4,3,2,1,0:T(8,128)} fusion(f32[56,6,16,9,128]{4,3,2,1,0:T(8,128)} %reshape.287), kind=kLoop, calls=%fused_computation.129 | loop fusion | bytes 68812800
  530.5 31.3 %constant_dynamic-update-slice_fusion = f32[56,6,16,9,256]{4,3,2,1,0:T(8,128)} fusion(f32[56,6,16,9,256]{4,3,2,1,0:T(8,128)} %constant_dynamic-update-slice_fusion.1, f32[56,6,16,9,128]{4,3,2,1,0:T(8,128)} %reshape.288), kind=kLoop, calls=%fused_computation.128 | loop fusion | bytes 88080384 | tf_op jit(solution)/shard_map/concatenate | solution.py:230
  561.8 139.0 %fusion.65 = (f32[56,6,16,1,256]{4,3,2,1,0:T(1,128)}, f32[56,6,16,1,256]{4,3,2,1,0:T(1,128)}, f32[56,6,16,1,256]{4,3,2,1,0:T(1,128)}, f32[56,6,16,1,256]{4,3,2,1...) fusion(f32[56,6,16,9,256]{4,3,2,1,0:T(8,128)} %constant_dynamic, ...), kind=kLoop, calls=%fused_computation.188 | loop fusion | bytes 99090432 | tf_op jit(solution)/shard_map/slice | solution.py:241
  737.6 17.1 %pad_add_fusion = f32[56,8,18,256]{3,2,1,0:T(8,128)S(1)} fusion(f32[56,6,16,256]{3,2,1,0:T(8,128)} %bitcast.147, f32[56,6,16,256]{3,2,1,0:T(8,128)} %bitcast.148, f32[56,6,16,256]{3,2,1,0:T(8,128)} %bitcast.131, f32[56,6,16,256]{3,2,1,0:T(8,128)} %bitcast.134, f32[56,6,16,256]{3,2,1,0:T(8,128)} %bitcast.137, f32[56,6,16,256]{3,2,1,0:T(8,128)} %bitcast.140, ...), kind=kLoop, calls=%fused_computation.26 | loop fusion | flops 16515072 | bytes 57802752 | tf_op jit(solution)/shard_map/add | solution.py:240
  769.6 9.1 fusion.12
  800.9 19.7 %all-reduce.11 = (f32[256]{0:T(256)S(1)}, f32[256]{0:T(256)S(1)}, f32[512]{0:T(512)}) all-reduce(f32[256]{0:T(256)S(1)} %get-tuple-element.89, f32[256]{0:T(256)S(1)} %get-tuple-element.90, f32[512]{0:T(512)S(1)} %copy-done.55), channel_id=1, replica_groups=mesh['img'=8,'row'=4] {'img'}, use_global_device_ids=true, to_apply=%region_54.55 | all-reduce | flops 1024 | bytes 8192 | tf_op jit(solution)/shard_map/psum | solution.py:29
  838.4 13.5 %multiply_convert_fusion = bf16[5376,1024]{1,0:T(8,128)(2,1)} fusion(f32[5376,1024]{1,0:T(8,128)} %get-tuple-element.113, bf16[5376,256]{1,0:T(8,128)(2,1)S(1)} %multiply_convert_fusion.4, bf16[1024,256]{1,0:T(8,128)(2,1)} %param.21, f32[5376]{0:T(1024)S(1)} %copy-done.10), kind=kOutput, calls=%fused_computation.8 | convolution fusion | flops 2835087360 | bytes 36328448 | tf_op jit(solution)/shard_map/pm,cm->pc/dot_general | solution.py:258
  851.9 126.1 %all-reduce.32.cloned.1.call-done = (f32[1024,256]{0,1:T(8,128)}, f32[3,3,128,512]{3,2,1,0:T(8,128)}, f32[256,1024]{1,0:T(8,128)}) async-done(((f32[1024,256]{0,1:T(8,128)}, f32[3,3,128,512]{3,2,1,0:T(8,128)}, f32[256,1024]{1,0:T(8,128)}), (f32[1024,256]{0,1:T(8,128)}, f32[3,3,128,512]{3,2,1,0:T(8,128)}, f32[256,1024]{1,0:T(8,128)})) %all-reduce.32.cloned.1.call-update) | async-done | bytes 4456464 | tf_op jit(solution)/shard_map/psum | solution.py:264
  983.4 69.1 %all-reduce.34.cloned.1.call-done = (f32[256,128]{1,0:T(8,128)}, f32[128,512]{1,0:T(8,128)}) async-done(((f32[256,128]{1,0:T(8,128)}, f32[128,512]{1,0:T(8,128)}), (f32[256,128]{1,0:T(8,128)}, f32[128,512]{1,0:T(8,128)})) %all-reduce.34.cloned.1.call-update) | async-done | bytes 393232 | tf_op jit(solution)/shard_map/psum | solution.py:276
  (323 shorter events, 213.7 us)
Async XLA Ops:
  7.2 169.9 %copy-start = (bf16[256,1024]{1,0:T(8,128)(2,1)S(1)}, bf16[256,1024]{1,0:T(8,128)(2,1)}, u32[]{:S(2)}) copy-start(bf16[256,1024]{1,0:T(8,128)(2,1)} %param.32) | copy-start | bytes 1572868
  7.2 324.6 %all-reduce.30.cloned.1.call-start = ((), (), s32[]{:S(2)}) async-start(), calls=%async_computation | async-start | bytes 229376 | tf_op jit(solution)/shard_map/psum | solution.py:37
  8.6 140.7 %copy-start.73 = (f32[56]{0:T(128)}, f32[56]{0:T(128)S(1)}, u32[]{:S(2)}) copy-start(f32[56]{0:T(128)S(1)} %get-tuple-element.140) | copy-start | bytes 676
  9.5 387.6 %copy-start.9 = (f32[5376]{0:T(1024)}, f32[5376]{0:T(1024)S(1)}, u32[]{:S(2)}) copy-start(f32[5376]{0:T(1024)S(1)} %reshape.292) | copy-start | bytes 64516
  9.5 39.4 %copy-start.41 = (f32[256]{0:T(256)S(1)}, f32[256]{0:T(256)}, u32[]{:S(2)}) copy-start(f32[256]{0:T(256)} %param.22) | copy-start | bytes 3076
  9.5 40.7 %copy-start.61 = (f32[256]{0:T(256)S(1)}, f32[256]{0:T(256)}, u32[]{:S(2)}) copy-start(f32[256]{0:T(256)} %param.23) | copy-start | bytes 3076
  17.6 38.9 %copy-start.69 = (s32[56,1]{0,1:T(1,128)S(1)}, s32[56,1]{0,1:T(1,128)}, u32[]{:S(2)}) copy-start(s32[56,1]{0,1:T(1,128)} %param.20) | copy-start | bytes 676
  55.2 8.7 collective-permute-start
  58.7 5.3 collective-permute-start.1
  137.6 31.6 %copy-start.45 = (f32[128]{0:T(128)S(1)}, f32[128]{0:T(128)}, u32[]{:S(2)}) copy-start(f32[128]{0:T(128)} %param.28) | copy-start | bytes 1540
  137.6 32.1 %copy-start.17 = (bf16[128,512]{1,0:T(8,128)(2,1)S(1)}, bf16[128,512]{1,0:T(8,128)(2,1)}, u32[]{:S(2)}) copy-start(bf16[128,512]{1,0:T(8,128)(2,1)} %param.30) | copy-start | bytes 393220
  137.6 32.1 %copy-start.56 = (f32[128]{0:T(128)S(1)}, f32[128]{0:T(128)}, u32[]{:S(2)}) copy-start(f32[128]{0:T(128)} %param.29) | copy-start | bytes 1540
  137.6 32.1 %copy-start.63 = (f32[512]{0:T(512)S(1)}, f32[512]{0:T(512)}, u32[]{:S(2)}) copy-start(f32[512]{0:T(512)} %param.31) | copy-start | bytes 6148
  177.1 33.9 %copy-start.36 = (f32[1024]{0:T(1024)S(1)}, f32[1024]{0:T(1024)}, u32[]{:S(2)}) copy-start(f32[1024]{0:T(1024)} %param.33) | copy-start | bytes 12292
  303.7 30.8 %copy-start.18 = (bf16[128,512]{1,0:T(8,128)(2,1)S(1)}, bf16[128,512]{1,0:T(8,128)(2,1)}, u32[]{:S(2)}) copy-start(bf16[128,512]{1,0:T(8,128)(2,1)} %param.30) | copy-start | bytes 393220
  303.7 30.8 %copy-start.26 = (f32[56,128]{1,0:T(8,128)S(1)}, f32[56,128]{1,0:T(8,128)}, u32[]{:S(2)}) copy-start(f32[56,128]{1,0:T(8,128)} %copy-done.25) | copy-start | bytes 86020
  303.7 30.8 %copy-start.46 = (f32[128]{0:T(128)S(1)}, f32[128]{0:T(128)}, u32[]{:S(2)}) copy-start(f32[128]{0:T(128)} %param.28) | copy-start | bytes 1540
  303.7 30.8 %copy-start.49 = (f32[128]{0:T(128)S(1)}, f32[128]{0:T(128)}, u32[]{:S(2)}) copy-start(f32[128]{0:T(128)} %copy-done.48) | copy-start | bytes 1540
  303.7 30.8 %copy-start.52 = (f32[128]{0:T(128)S(1)}, f32[128]{0:T(128)}, u32[]{:S(2)}) copy-start(f32[128]{0:T(128)} %copy-done.51) | copy-start | bytes 1540
  303.7 30.8 %copy-start.57 = (f32[128]{0:T(128)S(1)}, f32[128]{0:T(128)}, u32[]{:S(2)}) copy-start(f32[128]{0:T(128)} %param.29) | copy-start | bytes 1540
  303.7 52.9 %copy-start.70 = (f32[128]{0:T(128)S(1)}, f32[128]{0:T(128)}, u32[]{:S(2)}) copy-start(f32[128]{0:T(128)} %get-tuple-element.133) | copy-start | bytes 1540
  303.7 52.9 %copy-start.74 = (f32[56]{0:T(128)S(1)}, f32[56]{0:T(128)}, u32[]{:S(2)}) copy-start(f32[56]{0:T(128)} %copy-done.73) | copy-start | bytes 676
  303.7 54.0 %copy-start.20 = (f32[56,256]{1,0:T(8,128)S(1)}, f32[56,256]{1,0:T(8,128)}, u32[]{:S(2)}) copy-start(f32[56,256]{1,0:T(8,128)} %copy-done.19) | copy-start | bytes 172036
  303.8 54.0 %copy-start.22 = (f32[56,256]{1,0:T(8,128)S(1)}, f32[56,256]{1,0:T(8,128)}, u32[]{:S(2)}) copy-start(f32[56,256]{1,0:T(8,128)} %copy-done.21) | copy-start | bytes 172036
  303.8 674.2 %all-reduce.32.cloned.1.call-start = ((), (), s32[]{:S(2)}) async-start(), calls=%async_computation.1 | async-start | bytes 8912896 | tf_op jit(solution)/shard_map/psum | solution.py:264
  312.2 49.2 %slice-start = ((s8[5505024]{0:T(1024)(128)(4,1)}), s8[1310720]{0:T(1024)(128)(4,1)S(1)}, s32[]{:S(2)}) async-start(s8[5505024]{0:T(1024)(128)(4,1)} %bitcast.117), calls=%async_computation.3 | async-start | bytes 2621440
  361.5 35.6 %copy-start.54 = (f32[512]{0:T(512)S(1)}, f32[512]{0:T(512)}, u32[]{:S(2)}) copy-start(f32[512]{0:T(512)} %get-tuple-element.108) | copy-start | bytes 6148
  762.0 21.4 %collective-permute-start.3 = (bf16[56,1,16,256]{3,2,1,0:T(8,128)(2,1)S(1)}, bf16[56,1,16,256]{3,2,1,0:T(8,128)(2,1)S(1)}, u32[]{:S(2)}, u32[]{:S(2)}) collective-permute-start(bf16[56,1,16,256]{3,2,1,0:T(8,128)(2,1)S(1)} %slice.298), channel_id=1, source_target_pairs={{1,0},{2,1},{3,2},{5,4},{6,5},{7,6},{9,8},{10,9},{11,10},{13,12},{... | collective-permute-start | bytes 1376264 | tf_op jit(solution)/shard_map/ppermute | solution.py:20
  766.2 17.3 %collective-permute-start.2 = (bf16[56,1,16,256]{3,2,1,0:T(8,128)(2,1)S(1)}, bf16[56,1,16,256]{3,2,1,0:T(8,128)(2,1)S(1)}, u32[]{:S(2)}, u32[]{:S(2)}) collective-permute-start(bf16[56,1,16,256]{3,2,1,0:T(8,128)(2,1)S(1)} %bitcast.156), channel_id=1, source_target_pairs={{0,1},{1,2},{2,3},{4,5},{5,6},{6,7},{8,9},{9,10},{10,11},{12,13},{... | collective-permute-start | bytes 1376264 | tf_op jit(solution)/shard_map/ppermute | solution.py:18
  788.3 33.0 %copy-start.60 = (f32[256]{0:T(256)S(1)}, f32[256]{0:T(256)}, u32[]{:S(2)}) copy-start(f32[256]{0:T(256)} %get-tuple-element.102) | copy-start | bytes 3076
  835.7 216.7 %all-reduce.34.cloned.1.call-start = ((), (), s32[]{:S(2)}) async-start(), calls=%async_computation.2 | async-start | bytes 786432 | tf_op jit(solution)/shard_map/psum | solution.py:276
  838.4 217.3 %copy-start.1 = (bf16[256,1024]{1,0:T(8,128)(2,1)S(1)}, bf16[256,1024]{1,0:T(8,128)(2,1)}, u32[]{:S(2)}) copy-start(bf16[256,1024]{1,0:T(8,128)(2,1)} %param.32) | copy-start | bytes 1572868
  (74 other events, 662.7 us)
Sparse Core Ops, SparseCore 0:
  303.8 27.9 all-reduce.29
  835.8 142.1 all-reduce.31
  982.4 70.0 all-reduce.33
where the time goes:
time: 1070 us; the launch traced here: 1060 us
  local copies, waits for them, and re-layouts  348 us (33%)
  waiting for transfers between devices  215 us (20%)
  blocking collectives  211 us (20%)
  other arithmetic  154 us (14%)
  matrix products  109 us (10%)
  between operations  15.5 us (1%)
    slice x1, local copies, waits for them, and re-layouts, body(): taps_back[:, :, :, 3 * row_step + col_step, :]  139 us
    psum x1, waiting for transfers between devices, body(): lax.psum((reduce_part, split_part, expand_part), ('img', 'row'))  126 us
    psum x6, blocking collectives, pixel_total(): return lax.psum(partial_sums, 'img')  115 us
    unnamed x230, local copies, waits for them, and re-layouts  95.3 us
    psum x1, waiting for transfers between devices, body(): lax.psum((down_part, up_part, bias_part), 'img')  69.1 us
    psum x6, blocking collectives, pixel_total(): partial_sums = lax.psum(values, 'row')  44.5 us
    psum x2, blocking collectives, image_total(): return lax.psum((values[0], values[1]), 'img')  40.9 us
    reduce_sum x1, other arithmetic, body(): jnp.sum(summed_grad, axis=0)  33.5 us
  transfers between devices with their start and end apart: 7, of which 3 were waited for; matrix products, arithmetic and copies ran while one was open for 5% of the time, Pallas kernels for 0%

commit v1 on v0

v1 whole, which is shorter than its diff:
```python
import functools

import jax
import jax.numpy as jnp
from jax import lax
from jax.experimental import pallas as pl
from jax.experimental.pallas import tpu as pltpu
from jax.sharding import PartitionSpec as P

MESH = pl.DeviceIdType.MESH
HIGH = lax.Precision.HIGHEST
F32 = jnp.float32
BF16 = jnp.bfloat16
EPS = 1e-05
GROUP = 8
ANY = pl.BlockSpec(memory_space=pl.ANY)
VMEM = pl.BlockSpec(memory_space=pltpu.VMEM)
SMEM = pl.BlockSpec(memory_space=pltpu.SMEM)


def dot(a, b, dims, precision=None):
    return lax.dot_general(
        a, b, (dims, ((), ())), preferred_element_type=F32, precision=precision
    )


def mm(a, b, precision=None):
    return dot(a, b, ((1,), (0,)), precision)


def mm_nt(a, b, precision=None):
    return dot(a, b, ((1,), (1,)), precision)


def mm_tn(a, b, precision=None):
    return dot(a, b, ((0,), (0,)), precision)


def mm_terms(product, a, b, terms):
    total = None
    for _ in range(terms):
        part = a.astype(BF16)
        a = a - part.astype(F32)
        value = product(part, b)
        total = value if total is None else total + value
    return total


def sigmoid(v):
    return 0.5 * jnp.tanh(0.5 * v) + 0.5


def swish_slope(v):
    s = sigmoid(v)
    return s * (1.0 + v * (1.0 - s))


def wide(mask, times):
    return jnp.concatenate([mask] * times, axis=1)


def fold(v):
    return jnp.sum(v.reshape(v.shape[0] // 8, 8, v.shape[1]), axis=0)


def row_sum(v):
    return jnp.sum(v, axis=0, keepdims=True)


class Links:
    def __init__(self, n_img, n_row):
        self.ni, self.nr = n_img, n_row
        self.i, self.r = lax.axis_index("img"), lax.axis_index("row")

    def greet(self):
        bar = pltpu.get_barrier_semaphore()

        def go(k, c):
            pl.semaphore_signal(
                bar, inc=1, device_id=self.peer(k), device_id_type=MESH
            )
            return c

        lax.fori_loop(1, self.ni * self.nr, go, 0)

    def met(self):
        pl.semaphore_wait(pltpu.get_barrier_semaphore(), self.ni * self.nr - 1)

    def peer(self, k):
        return (lax.rem(self.i + k // self.nr, self.ni), lax.rem(self.r + k % self.nr, self.nr))

    def copy(self, buf, send, recv, me, k, target):
        return pltpu.make_async_remote_copy(
            src_ref=buf.at[me],
            dst_ref=buf.at[me],
            send_sem=send.at[k],
            recv_sem=recv.at[k],
            device_id=target,
            device_id_type=MESH,
        )

    def all_me(self):
        return self.i * self.nr + self.r

    def all_start(self, buf, sems):
        def go(k, c):
            self.copy(buf, sems.at[0], sems.at[1], self.all_me(), k, self.peer(k)).start()
            return c

        lax.fori_loop(1, self.ni * self.nr, go, 0)

    def all_wait(self, buf, sems):
        def go(k, c):
            self.copy(buf, sems.at[0], sems.at[1], self.all_me(), k, self.peer(k)).wait()
            return c

        lax.fori_loop(1, self.ni * self.nr, go, 0)
        return jnp.sum(buf[...], axis=0)

    def row_copies(self, buf, sems):
        return [
            self.copy(buf, sems.at[0], sems.at[1], self.r, k, (self.i, lax.rem(self.r + k, self.nr)))
            for k in range(1, self.nr)
        ]

    def img_copy(self, buf, sems, k):
        return self.copy(
            buf, sems.at[0], sems.at[1], self.i, k, (lax.rem(self.i + k, self.ni), self.r)
        )

    def row_total(self, buf, sems):
        copies = self.row_copies(buf, sems)
        for c in copies:
            c.start()
        for c in copies:
            c.wait()
        return jnp.sum(buf[...], axis=0)

    def img_total(self, buf, sems):
        def go(k, c):
            self.img_copy(buf, sems, k).start()
            return c

        def end(k, c):
            self.img_copy(buf, sems, k).wait()
            return c

        lax.fori_loop(1, self.ni, go, 0)
        lax.fori_loop(1, self.ni, end, 0)
        return jnp.sum(buf[...], axis=0)


def norm_terms(total, square, count, gain, shift):
    mean = total / count
    factor = lax.rsqrt(square / count - mean * mean + EPS)
    scale = gain * factor
    return mean, factor, scale, shift - mean * scale


def norm_back_terms(mean, factor, scale, count, s0, s1):
    slope = scale * factor * (s1 / count)
    return slope, scale * (s0 / count) - slope * mean


def forward_kernel(
    n_img,
    n_row,
    counts,
    heights,
    x_hbm,
    area,
    wr,
    g1,
    h1,
    ws,
    g2,
    h2,
    down,
    g_at,
    h_at,
    up,
    bias,
    we,
    g3,
    h3,
    fp_hbm,
    a3_hbm,
    sp_hbm,
    pd_hbm,
    mx_hbm,
    mk_hbm,
    v1,
    v2,
    v3,
    v_at,
    at_norm,
    at_out,
    w0,
    w1,
    pooled,
    gw,
    mixed_sum,
    fp,
    sp,
    pp,
    pd,
    mx,
    mk,
    xbuf,
    a3,
    acc1,
    acc2,
    gram,
    bottom,
    above,
    below,
    buf1,
    buf2,
    rbuf3,
    ibuf3,
    rbuf4,
    ibuf4,
    xsem,
    osem,
    a3sem,
    hsem,
    sem1,
    sem2,
    rsem3,
    isem3,
    rsem4,
    isem4,
):
    images, slots, cols, ch = x_hbm.shape
    mid = wr.shape[1]
    half = mid // 2
    blocks = images // GROUP
    cells = slots * cols
    links = Links(n_img, n_row)
    r = links.r
    links.greet()

    def x_copy(b, slot):
        return pltpu.make_async_copy(
            x_hbm.at[pl.ds(b * GROUP, GROUP)], xbuf.at[slot], xsem.at[slot]
        )

    x_copy(0, 0).start()

    def first(b, c):
        slot = lax.rem(b, 2)

        @pl.when(b + 1 < blocks)
        def _():
            x_copy(b + 1, 1 - slot).start()

        x_copy(b, slot).wait()
        pre = mm(xbuf[slot].reshape(GROUP * cells, ch), wr[...])
        fp[pl.ds(b * GROUP, GROUP)] = pre.reshape(GROUP, slots, cols, mid)
        return c

    lax.fori_loop(0, blocks, first, 0)
    out_fp = pltpu.make_async_copy(fp, fp_hbm, osem.at[0])
    out_fp.start()
    acc1[...] = jnp.zeros_like(acc1)

    def first_sums(i, c):
        count, height = counts[i], heights[i]
        rows = lax.broadcasted_iota(jnp.int32, (slots, cols, 128), 0)
        columns = lax.broadcasted_iota(jnp.int32, (slots, cols, 128), 1)
        m = jnp.where((rows < count) & (columns < height), 1.0, 0.0).astype(F32)
        mk[i] = m
        m = m.reshape(cells, 128)
        v = fp[i].reshape(cells, mid)
        w = v * wide(m, mid // 128)
        acc1[0] += fold(w)
        acc1[1] += fold(w * v)
        acc1[2, :, 0:128] += fold(m)
        bottom[i] = fp[i, jnp.maximum(count - 1, 0)]
        return c

    lax.fori_loop(0, images, first_sums, 0)
    out_mk = pltpu.make_async_copy(mk, mk_hbm, osem.at[1])
    out_mk.start()

    me = links.all_me()
    buf1[me, 0:1] = row_sum(acc1[0])
    buf1[me, 1:2] = row_sum(acc1[1])
    n_here = row_sum(acc1[2, :, 0:128])
    buf1[me, 2:3] = wide(n_here, mid // 128)
    buf1[me, 3:4] = jnp.zeros((1, mid), F32)

    prev_dev = (links.i, lax.rem(r + n_row - 1, n_row))
    next_dev = (links.i, lax.rem(r + 1, n_row))
    to_prev = pltpu.make_async_remote_copy(
        src_ref=fp.at[:, 0],
        dst_ref=below,
        send_sem=hsem.at[0],
        recv_sem=hsem.at[1],
        device_id=prev_dev,
        device_id_type=MESH,
    )
    to_next = pltpu.make_async_remote_copy(
        src_ref=bottom,
        dst_ref=above,
        send_sem=hsem.at[2],
        recv_sem=hsem.at[3],
        device_id=next_dev,
        device_id_type=MESH,
    )
    has_prev = r > 0
    has_next = r < n_row - 1

    links.met()
    links.all_start(buf1, sem1)

    @pl.when(has_prev)
    def _():
        to_prev.start()

    @pl.when(has_next)
    def _():
        to_next.start()

    @pl.when(jnp.logical_not(has_prev))
    def _():
        above[...] = jnp.zeros_like(above)

    @pl.when(jnp.logical_not(has_next))
    def _():
        below[...] = jnp.zeros_like(below)

    total = links.all_wait(buf1, sem1)
    n = total[2:3, 0:1]
    mean, factor, scale, offset = norm_terms(total[0:1], total[1:2], n, g1[...], h1[...])
    v1[0:1] = mean
    v1[1:2] = factor
    v1[2:3] = scale
    v1[3:4] = offset
    v1[4:5] = total[2:3]
    v1[5:8] = jnp.zeros((3, mid), F32)

    @pl.when(has_prev)
    def _():
        to_prev.wait_send()
        to_next.wait_recv()

    @pl.when(has_next)
    def _():
        to_next.wait_send()
        to_prev.wait_recv()

    prev_flag = has_prev.astype(F32)
    next_flag = has_next.astype(F32)
    ext = (slots + 2) * cols
    col_index = lax.rem(lax.broadcasted_iota(jnp.int32, (ext, mid), 0), cols)
    acc2[...] = jnp.zeros_like(acc2)

    def a3_copy(b, slot):
        return pltpu.make_async_copy(
            a3.at[slot], a3_hbm.at[pl.ds(b * GROUP, GROUP)], a3sem.at[slot]
        )

    def second(b, c):
        slot = lax.rem(b, 2)

        @pl.when(b >= 2)
        def _():
            a3_copy(b - 2, slot).wait()

        def spread(k, c):
            i = b * GROUP + k
            m = mk[i].reshape(cells, 128)
            cm = wide(m[0:cols], mid // 128)
            z = fp[i].reshape(cells, mid) * v1[2:3] + v1[3:4]
            own = z * sigmoid(z) * wide(m, mid // 128)
            z = above[i] * v1[2:3] + v1[3:4]
            top = z * sigmoid(z) * (cm * prev_flag)
            z = below[i] * v1[2:3] + v1[3:4]
            low = z * sigmoid(z) * (cm * next_flag)
            count = counts[i]
            parts = [top]
            for s in range(slots + 1):
                here = low * jnp.where(count == s, 1.0, 0.0).astype(F32)
                if s < slots:
                    here = here + own[s * cols : (s + 1) * cols]
                parts.append(here)
            full = jnp.concatenate(parts, axis=0)
            left = jnp.where(col_index == 0, 0.0, pltpu.roll(full, 1, 0)).astype(BF16)
            right = jnp.where(col_index == cols - 1, 0.0, pltpu.roll(full, ext - 1, 0)).astype(BF16)
            full = full.astype(BF16)
            pieces = []
            for g in range(2):
                for v in (left, full, right):
                    pieces.append(v[:, g * half : (g + 1) * half])
            a3[slot, k] = jnp.concatenate(pieces, axis=1).reshape(slots + 2, cols, 6 * half)
            return c

        lax.fori_loop(0, GROUP, spread, 0)
        for g in range(2):
            value = None
            for dy in range(3):
                lhs = a3[slot, :, dy : dy + slots, :, g * 3 * half : (g + 1) * 3 * half]
                part = mm(
                    lhs.reshape(GROUP * cells, 3 * half), ws[dy, :, g * mid : (g + 1) * mid]
                )
                value = part if value is None else value + part
            sp[pl.ds(b * GROUP, GROUP), :, :, g * mid : (g + 1) * mid] = value.reshape(
                GROUP, slots, cols, mid
            )
        a3_copy(b, slot).start()
        return c

    lax.fori_loop(0, blocks, second, 0)
    out_sp = pltpu.make_async_copy(sp, sp_hbm, osem.at[2])
    out_sp.start()

    def second_sums(i, c):
        m = wide(mk[i].reshape(cells, 128), mid // 128)
        for g in range(2):
            lanes = slice(g * mid, (g + 1) * mid)
            v = sp[i, :, :, lanes].reshape(cells, mid)
            w = v * m
            acc2[0, :, lanes] += fold(w)
            acc2[1, :, lanes] += fold(w * v)
        return c

    lax.fori_loop(0, images, second_sums, 0)
    buf2[me, 0:1] = row_sum(acc2[0])
    buf2[me, 1:2] = row_sum(acc2[1])
    links.all_start(buf2, sem2)
    total = links.all_wait(buf2, sem2)
    mean, factor, scale, offset = norm_terms(total[0:1], total[1:2], n, g2[...], h2[...])
    v2[0:1] = mean
    v2[1:2] = factor
    v2[2:3] = scale
    v2[3:4] = offset
    v2[4:8] = jnp.zeros((4, 2 * mid), F32)

    def second_act(i, c):
        m = wide(mk[i].reshape(cells, 128), mid // 128)
        both = None
        for g in range(2):
            lanes = slice(g * mid, (g + 1) * mid)
            z = sp[i, :, :, lanes].reshape(cells, mid) * v2[2:3, lanes] + v2[3:4, lanes]
            p = z * sigmoid(z) * m
            pp[i, :, :, lanes] = p.reshape(slots, cols, mid)
            part = fold(p)
            both = part if both is None else both + part
        pooled[pl.ds(i, 1)] = row_sum(both)
        return c

    lax.fori_loop(0, images, second_act, 0)
    pooled[...] = pooled[...] / area[...]
    rbuf3[r] = mm(pooled[...], down[...].astype(F32), HIGH)
    squeeze = links.row_total(rbuf3, rsem3)
    ibuf3[links.i, 0:1] = row_sum(squeeze)
    ibuf3[links.i, 1:2] = row_sum(squeeze * squeeze)
    total = links.img_total(ibuf3, isem3)
    mean, factor, scale, offset = norm_terms(
        total[0:1], total[1:2], float(images * n_img), g_at[...], h_at[...]
    )
    v_at[0:1] = factor
    v_at[1:8] = jnp.zeros((7, v_at.shape[1]), F32)
    at_norm[...] = (squeeze - mean) * factor
    z = at_norm[...] * g_at[...] + h_at[...]
    at_out[...] = z
    attend = z * sigmoid(z)
    upf = up[...].astype(F32)
    lean = mm(attend, upf[:, :mid] - upf[:, mid:], HIGH) + (bias[:, :mid] - bias[:, mid:])
    w0[...] = sigmoid(lean)
    w1[...] = sigmoid(-lean)

    gram[...] = jnp.zeros_like(gram)
    mixed_sum[...] = jnp.zeros_like(mixed_sum)

    def mixing(b, c):
        def one(k, c):
            i = b * GROUP + k
            p0 = pp[i, :, :, 0:mid].reshape(cells, mid)
            p1 = pp[i, :, :, mid:].reshape(cells, mid)
            v = w0[pl.ds(i, 1)] * p0 + w1[pl.ds(i, 1)] * p1
            mx[i] = v.astype(BF16).reshape(slots, cols, mid)
            pd[i] = (p0 - p1).astype(BF16).reshape(slots, cols, mid)
            return c

        lax.fori_loop(0, GROUP, one, 0)
        v = mx[pl.ds(b * GROUP, GROUP)].reshape(GROUP * cells, mid)
        gram[...] += mm_tn(v, v)
        mixed_sum[...] += mm_tn(v, jnp.ones((GROUP * cells, 128), BF16))
        return c

    lax.fori_loop(0, blocks, mixing, 0)
    out_mx = pltpu.make_async_copy(mx, mx_hbm, osem.at[4])
    out_mx.start()
    out_pd = pltpu.make_async_copy(pd, pd_hbm, osem.at[3])
    out_pd.start()
    gw[...] = mm_terms(mm, gram[...], we[...], 3)
    wef = we[...].astype(F32)
    rbuf4[r, 0:1] = row_sum(wide(mixed_sum[...], ch // 128) * wef)
    rbuf4[r, 1:2] = row_sum(gw[...] * wef)
    ibuf4[links.i] = links.row_total(rbuf4, rsem4)
    total = links.img_total(ibuf4, isem4)
    mean, factor, scale, offset = norm_terms(total[0:1], total[1:2], n, g3[...], h3[...])
    v3[0:1] = mean
    v3[1:2] = factor
    v3[2:3] = scale
    v3[3:4] = offset
    v3[4:8] = jnp.zeros((4, ch), F32)

    for slot in range(2):
        a3_copy(0, slot).wait()
    out_fp.wait()
    out_mk.wait()
    out_sp.wait()
    out_pd.wait()
    out_mx.wait()


def sd(shape, dtype=F32):
    return jax.ShapeDtypeStruct(shape, dtype)


def call_forward(n_img, n_row, args, images, slots, cols, ch, mid, inter):
    n = n_img * n_row
    cells = (images, slots, cols)
    outs = [
        (sd(cells + (mid,)), ANY),
        (sd((images, slots + 2, cols, 3 * mid), BF16), ANY),
        (sd(cells + (2 * mid,)), ANY),
        (sd(cells + (mid,), BF16), ANY),
        (sd(cells + (mid,), BF16), ANY),
        (sd(cells + (128,)), ANY),
        (sd((8, mid)), VMEM),
        (sd((8, 2 * mid)), VMEM),
        (sd((8, ch)), VMEM),
        (sd((8, inter)), VMEM),
        (sd((images, inter)), VMEM),
        (sd((images, inter)), VMEM),
        (sd((images, mid)), VMEM),
        (sd((images, mid)), VMEM),
        (sd((images, mid)), VMEM),
        (sd((mid, ch)), VMEM),
        (sd((mid, 128)), VMEM),
    ]
    dma = pltpu.SemaphoreType.DMA
    scratch = [
        pltpu.VMEM(cells + (mid,), F32),
        pltpu.VMEM(cells + (2 * mid,), F32),
        pltpu.VMEM(cells + (2 * mid,), F32),
        pltpu.VMEM(cells + (mid,), BF16),
        pltpu.VMEM(cells + (mid,), BF16),
        pltpu.VMEM(cells + (128,), F32),
        pltpu.VMEM((2, GROUP, slots, cols, ch), BF16),
        pltpu.VMEM((2, GROUP, slots + 2, cols, 3 * mid), BF16),
        pltpu.VMEM((3, 8, mid), F32),
        pltpu.VMEM((2, 8, 2 * mid), F32),
        pltpu.VMEM((mid, mid), F32),
        pltpu.VMEM((images, cols, mid), F32),
        pltpu.VMEM((images, cols, mid), F32),
        pltpu.VMEM((images, cols, mid), F32),
        pltpu.VMEM((n, 4, mid), F32),
        pltpu.VMEM((n, 2, 2 * mid), F32),
        pltpu.VMEM((n_row, images, inter), F32),
        pltpu.VMEM((n_img, 2, inter), F32),
        pltpu.VMEM((n_row, 2, ch), F32),
        pltpu.VMEM((n_img, 2, ch), F32),
        dma((2,)),
        dma((5,)),
        dma((2,)),
        dma((4,)),
        dma((2, n)),
        dma((2, n)),
        dma((2, n_row)),
        dma((2, n_img)),
        dma((2, n_row)),
        dma((2, n_img)),
    ]
    in_specs = [SMEM, SMEM, ANY] + [VMEM] * (len(args) - 3)
    return pl.pallas_call(
        functools.partial(forward_kernel, n_img, n_row),
        out_shape=[o for o, _ in outs],
        in_specs=in_specs,
        out_specs=[s for _, s in outs],
        scratch_shapes=scratch,
        name="forward",
        compiler_params=pltpu.CompilerParams(
            collective_id=0, has_side_effects=True, vmem_limit_bytes=60 * 1024 * 1024
        ),
    )(*args)


def third_kernel(
    counts, x, cot, mx, mk, we, awe, v3, bo, sg, q, m_out, tbuf
):
    step = pl.program_id(0)
    per, slots, cols, ch = x.shape
    mid = mx.shape[-1]
    cells = per * slots * cols
    t = mm(mx[...].reshape(cells, mid), we[...])
    tbuf[...] = t.reshape(tbuf.shape)

    def image(k, c):
        count = counts[step * per + k]
        m = mk[k, 0]
        m = wide(m, ch // 128)

        def row(s, c):
            zh = tbuf[k, s] * v3[0:1] + v3[1:2] + 0.5 * x[k, s].astype(F32)
            th = jnp.tanh(zh)
            up = 1.0 + th
            act = zh * up
            bo[k, s] = (act * m).astype(BF16)
            slope = up + act * (1.0 - th)
            sg[k, s] = (cot[k, s].astype(F32) * (0.5 * m) * slope).astype(BF16)
            return c

        def blank(s, c):
            bo[k, s] = jnp.zeros((cols, ch), BF16)
            sg[k, s] = jnp.zeros((cols, ch), BF16)
            return c

        lax.fori_loop(0, count, row, 0)
        lax.fori_loop(count, slots, blank, 0)
        return c

    lax.fori_loop(0, per, image, 0)
    s = sg[...].reshape(cells, ch)
    q[...] = mm(s, awe[...]).reshape(q.shape)

    @pl.when(step == 0)
    def _():
        m_out[...] = jnp.zeros_like(m_out)

    m_out[0:mid] += mm_tn(mx[...].reshape(cells, mid), s)
    m_out[mid : mid + 16] += mm(jnp.ones((16, cells), BF16), s)


def call_third(counts, x, cot, mx, mk, we, awe, v3):
    images, slots, cols, ch = x.shape
    mid = mx.shape[-1]
    per = 4

    def cells(c):
        return pl.BlockSpec((per, slots, cols, c), lambda b, *_: (b, 0, 0, 0))

    def whole(a):
        return pl.BlockSpec(a.shape, lambda b, *_: (0,) * a.ndim)

    return pl.pallas_call(
        third_kernel,
        out_shape=[
            sd(x.shape, BF16),
            sd(x.shape, BF16),
            sd((images, slots, cols, mid)),
            sd((mid + 16, ch)),
        ],
        grid_spec=pltpu.PrefetchScalarGridSpec(
            num_scalar_prefetch=1,
            grid=(images // per,),
            in_specs=[cells(ch), cells(ch), cells(mid), cells(128), whole(we), whole(awe), whole(v3)],
            out_specs=[
                cells(ch),
                cells(ch),
                cells(mid),
                pl.BlockSpec((mid + 16, ch), lambda b, *_: (0, 0)),
            ],
            scratch_shapes=[pltpu.VMEM((per, slots, cols, ch), F32)],
        ),
        name="third",
        compiler_params=pltpu.CompilerParams(vmem_limit_bytes=48 * 1024 * 1024),
    )(counts, x, cot, mx, mk, we, awe, v3)


def backward_kernel(
    n_img,
    n_row,
    counts,
    q_hbm,
    fp_hbm,
    a3_hbm,
    sp_hbm,
    pd_hbm,
    mx_hbm,
    mk_hbm,
    v1,
    v2,
    v3,
    v_at,
    at_norm,
    at_out,
    w0,
    w1,
    pooled,
    gw,
    mixed_sum,
    m_in,
    area,
    g_at,
    ws,
    down,
    up,
    we,
    awe,
    fu_hbm,
    expand_part,
    split_part,
    down_part,
    up_part,
    bias_part,
    b1,
    b2,
    b3,
    b_at,
    mg,
    fp,
    sp,
    pd,
    ub,
    mx,
    mk,
    a3,
    gpad,
    edge,
    ret,
    acc1,
    acc2,
    mb,
    dpart,
    pgrad,
    ibuf5,
    rbuf5,
    rbuf6,
    ibuf6,
    buf7,
    buf8,
    lsem,
    a3sem,
    hsem,
    rsem5,
    isem5,
    rsem6,
    isem6,
    sem7,
    sem8,
):
    images, slots, cols, mid = q_hbm.shape
    ch = we.shape[1]
    half = mid // 2
    blocks = images // GROUP
    cells = slots * cols
    links = Links(n_img, n_row)
    r, me = links.r, links.all_me()
    links.greet()
    loads = [
        pltpu.make_async_copy(src, dst, lsem.at[k])
        for k, (src, dst) in enumerate(
            [(mx_hbm, mx), (q_hbm, mg), (pd_hbm, pd), (mk_hbm, mk), (sp_hbm, sp), (fp_hbm, fp)]
        )
    ]
    for load in loads:
        load.start()

    n = v1[4:5, 0:1]
    mean3, factor3, scale3 = v3[0:1], v3[1:2], v3[2:3]
    wef = we[...].astype(F32)
    rbuf5[r, 0:1] = m_in[mid : mid + 1]
    rbuf5[r, 1:2] = factor3 * (row_sum(m_in[0:mid] * wef) - mean3 * m_in[mid : mid + 1])
    links.met()
    ibuf5[links.i] = links.row_total(rbuf5, rsem5)
    total = links.img_total(ibuf5, isem5)
    b3[...] = total
    slope3, offset3 = norm_back_terms(mean3, factor3, scale3, n, total[0:1], total[1:2])
    slope = factor3 * (total[1:2] / n)
    mb[...] = mm_terms(mm, wef * slope, awe[...], 2)
    level = total[0:1] / n - slope * mean3
    ev = mm_terms(mm, jnp.broadcast_to(level, (8, ch)), awe[...], 3)[0:1]
    expand_part[...] = (
        m_in[0:mid] * scale3 - wide(mixed_sum[...], ch // 128) * offset3 - gw[...] * slope3
    )

    for load in loads[:4]:
        load.wait()

    def mix_back(b, c):
        v = mx[pl.ds(b * GROUP, GROUP)].reshape(GROUP * cells, mid)
        high = mb[...].astype(BF16)
        fix = mm(v, high) + mm(v, (mb[...] - high.astype(F32)).astype(BF16))
        mg[pl.ds(b * GROUP, GROUP)] -= fix.reshape(GROUP, slots, cols, mid)

        def one(k, c):
            i = b * GROUP + k
            m = wide(mk[i].reshape(cells, 128), mid // 128)
            v = mg[i].reshape(cells, mid) - m * ev
            mg[i] = v.reshape(slots, cols, mid)
            d = pd[i].reshape(cells, mid).astype(F32)
            dpart[pl.ds(i, 1)] = row_sum(fold(v * d))
            return c

        lax.fori_loop(0, GROUP, one, 0)
        return c

    lax.fori_loop(0, blocks, mix_back, 0)

    upf = up[...].astype(F32)
    lean = dpart[...] * w0[...] * w1[...]
    rbuf6[r] = mm_nt(lean, upf[:, :mid] - upf[:, mid:], HIGH)
    z = at_out[...]
    attend = z * sigmoid(z)
    up_part[...] = mm_tn(attend, lean, HIGH)
    bias_part[...] = jnp.broadcast_to(row_sum(lean), bias_part.shape)
    attend_grad = links.row_total(rbuf6, rsem6) * swish_slope(z)
    ibuf6[links.i, 0:1] = row_sum(attend_grad)
    ibuf6[links.i, 1:2] = row_sum(attend_grad * at_norm[...])
    total = links.img_total(ibuf6, isem6)
    b_at[...] = total
    count = float(images * n_img)
    squeeze_grad = (
        g_at[...]
        * v_at[0:1]
        * (attend_grad - total[0:1] / count - at_norm[...] * (total[1:2] / count))
    )
    down_part[...] = mm_tn(pooled[...], squeeze_grad, HIGH)
    pgrad[...] = mm_nt(squeeze_grad, down[...].astype(F32), HIGH) / area[...]

    loads[4].wait()
    acc2[...] = jnp.zeros_like(acc2)

    def second_back(i, c):
        m = wide(mk[i].reshape(cells, 128), mid // 128)
        v = mg[i].reshape(cells, mid)
        for g, w in enumerate((w0, w1)):
            lanes = slice(g * mid, (g + 1) * mid)
            s = sp[i, :, :, lanes].reshape(cells, mid)
            z = s * v2[2:3, lanes] + v2[3:4, lanes]
            grad = (v * w[pl.ds(i, 1)] + pgrad[pl.ds(i, 1)]) * swish_slope(z) * m
            ub[i, :, :, lanes] = grad.reshape(slots, cols, mid)
            acc2[0, :, lanes] += fold(grad)
            acc2[1, :, lanes] += fold(grad * s)
        return c

    lax.fori_loop(0, images, second_back, 0)
    mean2, factor2, scale2 = v2[0:1], v2[1:2], v2[2:3]
    s0 = row_sum(acc2[0])
    buf7[me, 0:1] = s0
    buf7[me, 1:2] = factor2 * (row_sum(acc2[1]) - mean2 * s0)
    links.all_start(buf7, sem7)
    total = links.all_wait(buf7, sem7)
    b2[...] = total
    slope2, offset2 = norm_back_terms(mean2, factor2, scale2, n, total[0:1], total[1:2])

    def second_grad(grad, s, m):
        return (grad * scale2 - m * (offset2 + slope2 * s)).astype(BF16)

    prev_dev = (links.i, lax.rem(r + n_row - 1, n_row))
    next_dev = (links.i, lax.rem(r + 1, n_row))
    has_prev = r > 0
    has_next = r < n_row - 1
    to_prev = pltpu.make_async_remote_copy(
        src_ref=edge.at[0],
        dst_ref=ret.at[1],
        send_sem=hsem.at[0],
        recv_sem=hsem.at[1],
        device_id=prev_dev,
        device_id_type=MESH,
    )
    to_next = pltpu.make_async_remote_copy(
        src_ref=edge.at[1],
        dst_ref=ret.at[0],
        send_sem=hsem.at[2],
        recv_sem=hsem.at[3],
        device_id=next_dev,
        device_id_type=MESH,
    )

    def columns_back(t, lines):
        col = lax.rem(lax.broadcasted_iota(jnp.int32, (lines, half), 0), cols)
        left = jnp.where(col == cols - 1, 0.0, pltpu.roll(t[:, 0:half], lines - 1, 0))
        right = jnp.where(col == 0, 0.0, pltpu.roll(t[:, 2 * half : 3 * half], 1, 0))
        return left + t[:, half : 2 * half] + right

    for side, dy in ((0, 0), (1, 2)):

        def edge_rows(b, c):
            def one(k, c):
                i = b * GROUP + k
                at = 0 if side == 0 else jnp.maximum(counts[i] - 1, 0)
                m = wide(mk[i, 0], 2 * mid // 128)
                gpad[k, 0] = second_grad(ub[i, at], sp[i, at], m)
                return c

            lax.fori_loop(0, GROUP, one, 0)
            for g in range(2):
                v = gpad[:, 0, :, g * mid : (g + 1) * mid].reshape(GROUP * cols, mid)
                t = mm_nt(v, ws[dy, :, g * mid : (g + 1) * mid])
                edge[side, pl.ds(b * GROUP, GROUP), :, g * half : (g + 1) * half] = (
                    columns_back(t, GROUP * cols).astype(BF16).reshape(GROUP, cols, half)
                )
            return c

        lax.fori_loop(0, blocks, edge_rows, 0)
        if side == 0:

            @pl.when(has_prev)
            def _():
                to_prev.start()

        else:

            @pl.when(has_next)
            def _():
                to_next.start()

    @pl.when(jnp.logical_not(has_prev))
    def _():
        ret[0] = jnp.zeros(ret.shape[1:], BF16)

    @pl.when(jnp.logical_not(has_next))
    def _():
        ret[1] = jnp.zeros(ret.shape[1:], BF16)

    def a3_copy(b, slot):
        return pltpu.make_async_copy(
            a3_hbm.at[pl.ds(b * GROUP, GROUP)], a3.at[slot], a3sem.at[slot]
        )

    a3_copy(0, 0).start()
    gpad[:, 0] = jnp.zeros((GROUP, cols, 2 * mid), BF16)
    gpad[:, slots + 1] = jnp.zeros((GROUP, cols, 2 * mid), BF16)
    split_part[...] = jnp.zeros_like(split_part)

    def conv_back(b, c):
        slot = lax.rem(b, 2)

        @pl.when(b + 1 < blocks)
        def _():
            a3_copy(b + 1, 1 - slot).start()

        def one(k, c):
            i = b * GROUP + k
            m = wide(mk[i].reshape(cells, 128), 2 * mid // 128)
            v = second_grad(
                ub[i].reshape(cells, 2 * mid), sp[i].reshape(cells, 2 * mid), m
            )
            gpad[k, 1 : slots + 1] = v.reshape(slots, cols, 2 * mid)
            return c

        lax.fori_loop(0, GROUP, one, 0)
        for g in range(2):
            lanes = slice(g * mid, (g + 1) * mid)
            value = None
            for dy in range(3):
                v = gpad[:, 2 - dy : 2 - dy + slots, :, lanes].reshape(GROUP * cells, mid)
                part = mm_nt(v, ws[dy, :, lanes])
                value = part if value is None else value + part
            mg[pl.ds(b * GROUP, GROUP), :, :, g * half : (g + 1) * half] = columns_back(
                value, GROUP * cells
            ).reshape(GROUP, slots, cols, half)
        a3_copy(b, slot).wait()
        for g in range(2):
            lanes = slice(g * mid, (g + 1) * mid)
            v = gpad[:, 1 : slots + 1, :, lanes].reshape(GROUP * cells, mid)
            for dy in range(3):
                taps = a3[slot, :, dy : dy + slots, :, g * 3 * half : (g + 1) * 3 * half]
                split_part[dy, g] += mm_tn(v, taps.reshape(GROUP * cells, 3 * half))
        return c

    lax.fori_loop(0, blocks, conv_back, 0)

    @pl.when(has_prev)
    def _():
        to_prev.wait_send()
        to_next.wait_recv()

    @pl.when(has_next)
    def _():
        to_next.wait_send()
        to_prev.wait_recv()

    loads[5].wait()
    acc1[...] = jnp.zeros_like(acc1)

    def first_back(i, c):
        m = wide(mk[i].reshape(cells, 128), mid // 128)
        count = counts[i]
        low = ret[1, i].astype(F32)
        parts = []
        for s in range(slots):
            here = mg[i, s] + low * jnp.where(count - 1 == s, 1.0, 0.0).astype(F32)
            if s == 0:
                here = here + ret[0, i].astype(F32)
            parts.append(here)
        v = fp[i].reshape(cells, mid)
        z = v * v1[2:3] + v1[3:4]
        grad = jnp.concatenate(parts, axis=0) * swish_slope(z) * m
        mg[i] = grad.reshape(slots, cols, mid)
        acc1[0] += fold(grad)
        acc1[1] += fold(grad * v)
        return c

    lax.fori_loop(0, images, first_back, 0)
    out_fu = pltpu.make_async_copy(mg, fu_hbm, lsem.at[6])
    out_fu.start()
    s0 = row_sum(acc1[0])
    buf8[me, 0:1] = s0
    buf8[me, 1:2] = v1[1:2] * (row_sum(acc1[1]) - v1[0:1] * s0)
    links.all_start(buf8, sem8)
    total = links.all_wait(buf8, sem8)
    b1[...] = total
    out_fu.wait()


def call_backward(n_img, n_row, args, ch, inter):
    q = args[1]
    images, slots, cols, mid = q.shape
    half = mid // 2
    n = n_img * n_row
    cells = (images, slots, cols)
    outs = [
        (sd(cells + (mid,)), ANY),
        (sd((mid, ch)), VMEM),
        (sd((3, 2, mid, 3 * half)), VMEM),
        (sd((mid, inter)), VMEM),
        (sd((inter, mid)), VMEM),
        (sd((8, mid)), VMEM),
        (sd((2, mid)), VMEM),
        (sd((2, 2 * mid)), VMEM),
        (sd((2, ch)), VMEM),
        (sd((2, inter)), VMEM),
    ]
    dma = pltpu.SemaphoreType.DMA
    scratch = [
        pltpu.VMEM(cells + (mid,), F32),
        pltpu.VMEM(cells + (mid,), F32),
        pltpu.VMEM(cells + (2 * mid,), F32),
        pltpu.VMEM(cells + (mid,), BF16),
        pltpu.VMEM(cells + (2 * mid,), F32),
        pltpu.VMEM(cells + (mid,), BF16),
        pltpu.VMEM(cells + (128,), F32),
        pltpu.VMEM((2, GROUP, slots + 2, cols, 3 * mid), BF16),
        pltpu.VMEM((GROUP, slots + 2, cols, 2 * mid), BF16),
        pltpu.VMEM((2, images, cols, mid), BF16),
        pltpu.VMEM((2, images, cols, mid), BF16),
        pltpu.VMEM((2, 8, mid), F32),
        pltpu.VMEM((2, 8, 2 * mid), F32),
        pltpu.VMEM((mid, mid), F32),
        pltpu.VMEM((images, mid), F32),
        pltpu.VMEM((images, mid), F32),
        pltpu.VMEM((n_img, 2, ch), F32),
        pltpu.VMEM((n_row, 2, ch), F32),
        pltpu.VMEM((n_row, images, inter), F32),
        pltpu.VMEM((n_img, 2, inter), F32),
        pltpu.VMEM((n, 2, 2 * mid), F32),
        pltpu.VMEM((n, 2, mid), F32),
        dma((7,)),
        dma((2,)),
        dma((4,)),
        dma((2, n_row)),
        dma((2, n_img)),
        dma((2, n_row)),
        dma((2, n_img)),
        dma((2, n)),
        dma((2, n)),
    ]
    in_specs = [SMEM] + [ANY] * 7 + [VMEM] * (len(args) - 8)
    return pl.pallas_call(
        functools.partial(backward_kernel, n_img, n_row),
        out_shape=[o for o, _ in outs],
        in_specs=in_specs,
        out_specs=[s for _, s in outs],
        scratch_shapes=scratch,
        name="backward",
        compiler_params=pltpu.CompilerParams(
            collective_id=1, has_side_effects=True, vmem_limit_bytes=60 * 1024 * 1024
        ),
    )(*args)


def input_kernel(fu, fp, mk, x, sg, wr, vec, gi, red):
    per, slots, cols, ch = x.shape
    mid = fp.shape[-1]
    cells = per * slots * cols

    m = wide(mk[...].reshape(cells, 128), mid // 128)
    fg = fu[...].reshape(cells, mid) * vec[0:1] - m * (
        vec[1:2] + vec[2:3] * fp[...].reshape(cells, mid)
    )
    fg = fg.astype(BF16)
    value = mm_nt(fg, wr[...]) + sg[...].reshape(cells, ch).astype(F32)
    gi[...] = value.astype(BF16).reshape(gi.shape)

    @pl.when(pl.program_id(0) == 0)
    def _():
        red[...] = jnp.zeros_like(red)

    red[...] += mm_tn(fg, x[...].reshape(cells, ch))


def call_input(fu, fp, mk, x, sg, wr, vec):
    images, slots, cols, ch = x.shape
    mid = fp.shape[-1]
    per = 4

    def cells(c):
        return pl.BlockSpec((per, slots, cols, c), lambda b: (b, 0, 0, 0))

    def whole(a):
        return pl.BlockSpec(a.shape, lambda b: (0,) * a.ndim)

    return pl.pallas_call(
        input_kernel,
        out_shape=[sd(x.shape, BF16), sd((mid, ch))],
        grid=(images // per,),
        in_specs=[cells(mid), cells(mid), cells(128), cells(ch), cells(ch), whole(wr), whole(vec)],
        out_specs=[cells(ch), pl.BlockSpec((mid, ch), lambda b: (0, 0))],
        name="input_grad",
        compiler_params=pltpu.CompilerParams(vmem_limit_bytes=48 * 1024 * 1024),
    )(fu, fp, mk, x, sg, wr, vec)


def body(
    n_img,
    n_row,
    feature_map,
    image_group,
    row_counts,
    reduce_weight,
    gain_first,
    shift_first,
    split_weight,
    gain_second,
    shift_second,
    attn_down,
    gain_attend,
    shift_attend,
    attn_up,
    attn_bias,
    expand_weight,
    gain_third,
    shift_third,
    cotangent,
):
    images, slots, cols, ch = feature_map.shape
    mid = reduce_weight.shape[1]
    inter = attn_down.shape[1]
    half = mid // 2
    counts = row_counts[:, 0]
    heights = 12 + 2 * image_group
    area = jnp.broadcast_to((heights * heights).astype(F32)[:, None], (images, mid))
    ws = split_weight.reshape(3, 3 * half, 2 * mid)

    def line(v):
        return v[None, :]

    (
        fp, a3, sp, pd, mx, mk, v1, v2, v3, v_at, at_norm, at_out, w0, w1, pooled, gw, mixed_sum,
    ) = call_forward(
        n_img,
        n_row,
        (
            counts,
            heights,
            feature_map,
            area,
            reduce_weight,
            line(gain_first),
            line(shift_first),
            ws,
            line(gain_second),
            line(shift_second),
            attn_down,
            line(gain_attend),
            line(shift_attend),
            attn_up,
            line(attn_bias),
            expand_weight,
            line(gain_third),
            line(shift_third),
        ),
        images, slots, cols, ch, mid, inter,
    )
    awe = (expand_weight.astype(F32) * v3[2:3]).astype(BF16).T
    half_terms = jnp.concatenate([0.5 * v3[2:4], jnp.zeros((6, ch), F32)], axis=0)
    block_out, sg, q, m_sum = call_third(
        counts, feature_map, cotangent, mx, mk, expand_weight, awe, half_terms
    )
    (
        fu, expand_part, split_part, down_part, up_part, bias_part, b1, b2, b3, b_at,
    ) = call_backward(
        n_img,
        n_row,
        (
            counts, q, fp, a3, sp, pd, mx, mk, v1, v2, v3, v_at, at_norm, at_out, w0, w1, pooled,
            gw, mixed_sum, m_sum, area, line(gain_attend), ws, attn_down, attn_up, expand_weight,
            awe,
        ),
        ch, inter,
    )
    slope1, offset1 = norm_back_terms(v1[0:1], v1[1:2], v1[2:3], v1[4, 0], b1[0:1], b1[1:2])
    vec = jnp.concatenate([v1[2:3], offset1, slope1, jnp.zeros((5, mid), F32)], axis=0)
    grad_input, reduce_t = call_input(fu, fp, mk, feature_map, sg, reduce_weight, vec)

    split = split_part.reshape(3, 2, mid, 3, half).transpose(0, 3, 4, 1, 2)
    split = split.reshape(3, 3, half, 2 * mid)

    def shared(v, dim):
        v = lax.psum_scatter(v, "row", scatter_dimension=dim, tiled=True)
        return lax.psum(v, "img")

    grad_reduce = shared(reduce_t.T, 0)
    grad_split = shared(split, 2)
    grad_expand = shared(expand_part, 0)
    grad_down, grad_up, grad_bias = lax.psum((down_part, up_part, bias_part[0]), ("img", "row"))
    return (
        block_out,
        grad_input,
        grad_reduce,
        grad_split,
        grad_expand,
        grad_down,
        jnp.concatenate([grad_up, -grad_up], axis=1),
        jnp.concatenate([grad_bias, -grad_bias]),
        b1[1],
        b1[0],
        b2[1],
        b2[0],
        b_at[1],
        b_at[0],
        b3[1],
        b3[0],
    )


def solution(mesh):
    cells = P("img", "row", None, None)
    in_specs = (cells, P("img"), P("img", "row")) + (P(),) * 14 + (cells,)
    out_specs = (cells, cells, P("row", None), P(None, None, "row", None), P("row", None)) + (P(),) * 11
    return jax.shard_map(
        functools.partial(body, mesh.shape["img"], mesh.shape["row"]),
        mesh=mesh,
        in_specs=in_specs,
        out_specs=out_specs,
        check_vma=False,
    )
```

time: 1070 us -> 568 us (0.53)
  local copies, waits for them, and re-layouts: 348 us -> 28.1 us
  Pallas kernels: 0 us -> 209 us
  blocking collectives: 211 us -> 39.4 us
  other arithmetic: 154 us -> 7.4 us
  matrix products: 109 us -> 0 us
  waiting for transfers between devices: 215 us -> 268 us
    pallas_call x0 -> x4, Pallas kernels: none -> 209 us  [the longest x1 76 us: call_backward(): pl.pallas_call(functools.partial(backward_kernel, n_img, n_row), out_shap...]
    psum x15 -> x1, blocking collectives: 211 us -> 39.4 us  [body(): lax.psum((down_part, up_part, bias_part[0]), ('img', 'row'))]
    slice x5, local copies, waits for them, and re-layouts: 143 us -> 3.84 us  [the longest x1 1.19 us: body(): v1[4, 0]]
    dot_general x18 -> x0, matrix products: 109 us -> none  [the longest x1 13.5 us: body(): jnp.einsum('pm,cm->pc', first_grad, reduce_weight, preferred_element_type...]
    unnamed x230 -> x35, local copies, waits for them, and re-layouts: 95.3 us -> 14.2 us
    reduce_sum x9 -> x0, other arithmetic: 63.7 us -> none  [the longest x1 33.5 us: body(): jnp.sum(summed_grad, axis=0)]
    reshape x4 -> x1, local copies, waits for them, and re-layouts: 63.4 us -> 4.8 us  [body(): split = split.reshape(3, 3, half, 2 * mid)]
    reduce_scatter x0 -> x2, waiting for transfers between devices: none -> 53 us  [shared(): v = lax.psum_scatter(v, 'row', scatter_dimension=dim, tiled=True)]
  transfers between devices with their start and end apart: 7 -> 5, of which waited for: 3 -> 5; matrix products, arithmetic and copies ran while one was open for 5% -> 2% of each run, Pallas kernels for 0% -> 4%
where the time goes in v1:
time: 568 us; the launch traced here: 567 us
  waiting for transfers between devices  268 us (47%)
  Pallas kernels  209 us (37%)
  blocking collectives  39.4 us (7%)
  local copies, waits for them, and re-layouts  28.1 us (5%)
  between operations  14.6 us (3%)
  other arithmetic  7.4 us (1%)
    psum x1, waiting for transfers between devices, body(): lax.psum((down_part, up_part, bias_part[0]), ('img', 'row'))  88.5 us
    psum x1, waiting for transfers between devices, shared(): return lax.psum(v, 'img')  84.3 us
    pallas_call x1, Pallas kernels, call_backward(): pl.pallas_call(functools.partial(backward_kernel, n_img, n_row), out_shap...  76 us
    pallas_call x1, Pallas kernels, call_forward(): pl.pallas_call(functools.partial(forward_kernel, n_img, n_row), out_shape...  75.4 us
    reduce_scatter x2, waiting for transfers between devices, shared(): v = lax.psum_scatter(v, 'row', scatter_dimension=dim, tiled=True)  53 us
    unnamed x6, waiting for transfers between devices  42.2 us
    psum x1, blocking collectives, body(): lax.psum((down_part, up_part, bias_part[0]), ('img', 'row'))  39.4 us
    pallas_call x1, Pallas kernels, call_third(): pl.pallas_call(third_kernel, out_shape=[sd(x.shape, BF16), sd(x.shape, BF...  37.7 us
  transfers between devices with their start and end apart: 5, of which 5 were waited for; matrix products, arithmetic and copies ran while one was open for 2% of the time, Pallas kernels for 4%

profile of v1, /device:TPU:0, one launch (start us, length us, event | category | flops | bytes accessed | tf_op | source)
XLA Modules:
  0.0 567.2 jit_solution(12711989365526197687)
XLA Ops:
  7.2 1.2 multiply_convert_fusion.1
  8.4 1.2 copy.45
  9.6 0.7 broadcast_in_dim.38.area
  10.3 75.4 %forward.1 = (f32[56,6,16,256]{3,2,1,0:T(8,128)}, bf16[56,8,16,768]{3,2,1,0:T(8,128)(2,1)}, f32[56,6,16,512]{3,2,1,0:T(8,128)}, bf16[56,6,16,256]{3,2,1,0:T(8,12...) custom-call(s32[56]{0:T(128)} %bitcast.33, ...), custom_call_target="tpu_custom_call" | custom-call | tf_op jit(solution)/shard_map/forward/pallas_call | solution.py:580
  85.8 0.8 slice.48
  86.5 0.8 slice_multiply_fusion
  87.6 1.9 copy-done.1
  89.5 37.7 %third.1 = (bf16[56,6,16,1024]{3,2,1,0:T(8,128)(2,1)}, bf16[56,6,16,1024]{3,2,1,0:T(8,128)(2,1)}, f32[56,6,16,256]{3,2,1,0:T(8,128)}, f32[272,1024]{1,0:T(8,128)S(1)}) custom-call(s32[56]{0:T(128)S(1)} %bitcast.35, bf16[56,6,16,1024]{3,2,1,0:T(8,128)(2,1)} %x.5, bf16[56,6,16,1024]{3,2,1,0:T(8,128)(2,1)} %cot.1, bf16[56,6,16,256]{3,2,1,0:T(8,128)(2,1)S(1)} %copy-done.1, ...), custom_call_target="tpu_custom_call" | custom-call | tf_op jit(solution)/shard_map/third/pallas_call | solution.py:650
  127.2 1.0 copy-done.5
  128.2 76.0 %backward.1 = (f32[56,6,16,256]{3,2,1,0:T(8,128)}, f32[256,1024]{1,0:T(8,128)}, f32[3,2,256,384]{3,2,1,0:T(8,128)}, f32[256,128]{1,0:T(8,128)}, f32[128,256]{1,0...) custom-call(s32[56]{0:T(128)} %bitcast.34, ...), custom_call_target="tpu_custom_call" | custom-call | tf_op jit(solution)/shard_map/backward/pallas_call | solution.py:1066
  204.2 2.1 copy.46
  206.2 2.0 copy.47
  208.2 4.8 copy.48
  213.1 1.2 slice.52
  214.3 2.0 fusion.1
  216.4 20.4 %input_grad.1 = (bf16[56,6,16,1024]{3,2,1,0:T(8,128)(2,1)}, f32[256,1024]{1,0:T(8,128)S(1)}) custom-call(f32[56,6,16,256]{3,2,1,0:T(8,128)} %get-tuple-element.69.fu, f32[56,6,16,256]{3,2,1,0:T(8,128)} %get-tuple-element.54.fp_hbm.fp, f32[56,6,16,128]{3,2,1,0:T(8,128)S(1)} %copy-done, bf16[56,6,16,1024]{3,2,1,0:T(8,128)(2,1)} %x.5, ...), custom_call_target="tpu_custom_call" | custom-call | tf_op jit(solution)/shard_map/input_grad/pallas_call | solution.py:1110
  236.8 1.0 copy-done.6
  237.9 0.7 reduce-scatter.5.cloned.1.call-update
  240.5 40.9 %all-reduce.8.cloned.1.call-done = f32[3,3,128,512]{3,1,0,2:T(4,128)} async-done(((f32[3,3,128,512]{3,1,0,2:T(4,128)}), f32[3,3,128,512]{3,1,0,2:T(4,128)}) %all-reduce.8.cloned.1.call-update) | async-done | bytes 2359312
  281.4 2.2 constant_dynamic-slice_fusion
  283.6 25.4 %reduce-scatter.3.cloned.1.call-done = f32[256,256]{0,1:T(8,128)} async-done(((f32[1024,256]{0,1:T(8,128)}), f32[256,256]{0,1:T(8,128)}) %reduce-scatter.3.cloned.1.call-update) | async-done | bytes 262160 | tf_op jit(solution)/shard_map/reduce_scatter | solution.py:1207
  309.0 27.6 %reduce-scatter.5.cloned.1.call-done = f32[64,1024]{1,0:T(8,128)} async-done(((f32[256,1024]{1,0:T(8,128)}), f32[64,1024]{1,0:T(8,128)}) %reduce-scatter.5.cloned.1.call-update) | async-done | bytes 262160 | tf_op jit(solution)/shard_map/reduce_scatter | solution.py:1207
  336.6 0.7 slice.56
  337.3 39.4 %psum.47 = f32[256]{0:T(256)S(1)} all-reduce(f32[256]{0:T(256)S(1)} %bitcast.43), channel_id=1, replica_groups=mesh['img'=8,'row'=4] {'img','row'}, use_global_device_ids=true, to_apply=%region_8.0 | all-reduce | flops 256 | bytes 2048 | tf_op jit(solution)/shard_map/psum | solution.py:1213
  379.0 88.5 %all-reduce.10.cloned.1.call-done = (f32[256,128]{1,0:T(8,128)}, f32[128,256]{1,0:T(8,128)}) async-done(((f32[256,128]{1,0:T(8,128)}, f32[128,256]{1,0:T(8,128)}), (f32[256,128]{1,0:T(8,128)}, f32[128,256]{1,0:T(8,128)})) %all-reduce.10.cloned.1.call-update) | async-done | bytes 262160 | tf_op jit(solution)/shard_map/psum | solution.py:1213
  467.5 0.9 neg.6
  468.5 1.6 pad_maximum_fusion
  470.1 84.3 %all-reduce.12.cloned.1.call-done = (f32[256,256]{0,1:T(8,128)}, f32[3,3,32,512]{3,1,0,2:T(4,128)}, f32[64,1024]{1,0:T(8,128)}) async-done(((f32[256,256]{0,1:T(8,128)}, f32[3,3,32,512]{3,1,0,2:T(4,128)}, f32[64,1024]{1,0:T(8,128)}), (f32[256,256]{0,1:T(8,128)}, f32[3,3,32,512]{3,1,0,2:T(4,128)}, f32[64,1024]{1,0:T(8,128)})) %all-reduce.12.cloned.1.call-update) | async-done | bytes 1114128 | tf_op jit(solution)/shard_map/psum | solution.py:1208
  554.5 2.1 copy.50
  556.6 1.8 copy.49
  558.4 1.7 copy.58
  560.1 0.7 copy.59
  (45 shorter events, 4.1 us)
Async XLA Ops:
  7.2 274.2 %all-reduce.8.cloned.1.call-start = ((), (), s32[]{:S(2)}) async-start(), calls=%async_computation.4 | async-start | bytes 6291456
  10.3 77.2 %copy-start.2 = (bf16[256,1024]{1,0:T(8,128)(2,1)S(1)}, bf16[256,1024]{1,0:T(8,128)(2,1)}, u32[]{:S(2)}) copy-start(bf16[256,1024]{1,0:T(8,128)(2,1)} %we.5) | copy-start | bytes 1572868
  10.3 77.2 %copy-start.7 = (s32[56,1]{0,1:T(1,128)S(1)}, s32[56,1]{0,1:T(1,128)}, u32[]{:S(2)}) copy-start(s32[56,1]{0,1:T(1,128)} %param.20) | copy-start | bytes 676
  87.5 39.7 %copy-start.3 = (bf16[1024,256]{1,0:T(8,128)(2,1)}, bf16[1024,256]{1,0:T(8,128)(2,1)S(1)}, u32[]{:S(2)}) copy-start(bf16[1024,256]{1,0:T(8,128)(2,1)S(1)} %fusion.awe) | copy-start | bytes 1572868
  87.6 1.9 copy-start.1
  127.2 1.0 copy-start.5
  208.2 6.1 %copy-start.11 = (f32[2,256]{1,0:T(2,128)S(1)}, f32[2,256]{1,0:T(2,128)}, u32[]{:S(2)}) copy-start(f32[2,256]{1,0:T(2,128)} %get-tuple-element.71) | copy-start | bytes 6148
  208.2 8.2 %copy-start = (f32[56,6,16,128]{3,2,1,0:T(8,128)S(1)}, f32[56,6,16,128]{3,2,1,0:T(8,128)}, u32[]{:S(2)}) copy-start(f32[56,6,16,128]{3,2,1,0:T(8,128)} %get-tuple-element.50.mk.mk_hbm) | copy-start | bytes 8257540
  208.2 8.2 %copy-start.4 = (bf16[1024,256]{1,0:T(8,128)(2,1)S(1)}, bf16[1024,256]{1,0:T(8,128)(2,1)}, u32[]{:S(2)}) copy-start(bf16[1024,256]{1,0:T(8,128)(2,1)} %wr.3) | copy-start | bytes 1572868
  213.0 95.9 %reduce-scatter.3.cloned.1.call-start = ((), (), s32[]{:S(2)}) async-start(), calls=%async_computation.2 | async-start | bytes 1310720 | tf_op jit(solution)/shard_map/reduce_scatter | solution.py:1207
  216.4 22.8 %copy-start.13 = (u32[32]{0:T(128)S(1)}, u32[32]{0:T(128)}, u32[]{:S(2)}) copy-start(u32[32]{0:T(128)} %constant.16) | copy-start | bytes 388
  236.8 1.0 copy-start.6
  237.8 139.5 %copy-start.12 = (f32[2,128]{1,0:T(2,128)S(1)}, f32[2,128]{1,0:T(2,128)}, u32[]{:S(2)}) copy-start(f32[2,128]{1,0:T(2,128)} %get-tuple-element.80) | copy-start | bytes 3076
  237.8 140.0 %copy-start.10 = (f32[2,512]{1,0:T(2,128)S(1)}, f32[2,512]{1,0:T(2,128)}, u32[]{:S(2)}) copy-start(f32[2,512]{1,0:T(2,128)} %get-tuple-element.79) | copy-start | bytes 12292
  237.8 140.6 %copy-start.9 = (f32[2,1024]{1,0:T(2,128)S(1)}, f32[2,1024]{1,0:T(2,128)}, u32[]{:S(2)}) copy-start(f32[2,1024]{1,0:T(2,128)} %get-tuple-element.81) | copy-start | bytes 24580
  237.8 98.8 %reduce-scatter.5.cloned.1.call-start = ((), (), s32[]{:S(2)}) async-start(), calls=%async_computation.3 | async-start | bytes 1310720 | tf_op jit(solution)/shard_map/reduce_scatter | solution.py:1207
  238.6 229.0 %all-reduce.10.cloned.1.call-start = ((), (), s32[]{:S(2)}) async-start(), calls=%async_computation.5 | async-start | bytes 524288 | tf_op jit(solution)/shard_map/psum | solution.py:1213
  239.2 315.3 %all-reduce.12.cloned.1.call-start = ((), (), s32[]{:S(2)}) async-start(), calls=%async_computation.6 | async-start | bytes 2621440 | tf_op jit(solution)/shard_map/psum | solution.py:1208
  467.5 92.5 %copy-start.8 = (f32[256,128]{1,0:T(8,128)S(1)}, f32[256,128]{1,0:T(8,128)}, u32[]{:S(2)}) copy-start(f32[256,128]{1,0:T(8,128)} %get-tuple-element.185) | copy-start | bytes 393220
Sparse Core Ops, SparseCore 0:
  213.1 68.2 all-reduce.7
  283.9 24.9 reduce-scatter.2
  311.7 24.8 reduce-scatter.4
  342.1 125.3 all-reduce.9
  471.3 83.1 all-reduce.11

commit v2 on v1

--- a/solution.py
+++ b/solution.py
@@ -148,6 +148,116 @@
         lax.fori_loop(1, self.ni, go, 0)
         lax.fori_loop(1, self.ni, end, 0)
         return jnp.sum(buf[...], axis=0)
+
+
+class Reducer:
+    @staticmethod
+    def layout(n_img, rows, width, dtype):
+        lane_parts = min(width // 128, n_img)
+        row_parts = n_img // lane_parts
+        tile = 16 if dtype == BF16 else 8
+        share = -(-rows // (row_parts * tile)) * tile
+        return lane_parts, share, share * row_parts
+
+    @staticmethod
+    def scratch(n_img, rows, width, dtype):
+        lane_parts, share, padded = Reducer.layout(n_img, rows, width, dtype)
+        lanes = width // lane_parts
+        return [
+            pltpu.VMEM((2, padded, width), dtype),
+            pltpu.VMEM((2, padded, width), dtype),
+            pltpu.VMEM((padded, width), dtype),
+            pltpu.VMEM((padded, width), dtype),
+            pltpu.VMEM((padded, width), F32),
+            pltpu.VMEM((n_img, share, lanes), dtype),
+            pltpu.VMEM((padded, width), dtype),
+            pltpu.SemaphoreType.DMA((2, 2 + 2 * n_img)),
+        ]
+
+    COUNT = 8
+
+    def __init__(self, links, rows, width, refs):
+        self.links, self.rows, self.width = links, rows, width
+        (self.sb1, self.rb1, self.sb2, self.rb2, self.mine, self.rb3, self.ag, self.sems) = refs
+        self.dtype = self.sb1.dtype
+        self.lane_parts, self.share, self.padded = Reducer.layout(links.ni, rows, width, self.dtype)
+        self.lanes = width // self.lane_parts
+        r = links.r
+        self.one = r + 1 - 2 * lax.rem(r, 2)
+        self.two = lax.rem(r + 2, 4)
+
+    def copy(self, src, dst, k, target):
+        return pltpu.make_async_remote_copy(
+            src_ref=src,
+            dst_ref=dst,
+            send_sem=self.sems.at[0, k],
+            recv_sem=self.sems.at[1, k],
+            device_id=target,
+            device_id_type=MESH,
+        )
+
+    def copy1(self):
+        return self.copy(self.sb1, self.rb1, 0, (self.links.i, self.one))
+
+    def copy2(self):
+        return self.copy(self.sb2, self.rb2, 1, (self.links.i, self.two))
+
+    def part(self, ref, j):
+        row = pl.multiple_of((j // self.lane_parts) * self.share, self.share)
+        lane = pl.multiple_of(lax.rem(j, self.lane_parts) * self.lanes, self.lanes)
+        return ref.at[pl.ds(row, self.share), pl.ds(lane, self.lanes)]
+
+    def peer(self, k):
+        return lax.rem(self.links.i + k, self.links.ni)
+
+    def copy3(self, k):
+        return self.copy(
+            self.part(self.sb2, self.peer(k)), self.rb3.at[self.links.i], 2 + k, (self.peer(k), self.links.r)
+        )
+
+    def copy4(self, k):
+        mine = self.part(self.ag, self.links.i)
+        return self.copy(mine, mine, 2 + self.links.ni + k, (self.peer(k), self.links.r))
+
+    def each(self, make, act):
+        def go(k, c):
+            act(make(k))
+            return c
+
+        lax.fori_loop(1, self.links.ni, go, 0)
+
+    def begin(self, piece):
+        odd = 1 - lax.rem(self.links.r, 2)
+        for k in range(2):
+            self.sb1[k, 0 : self.rows] = piece(odd + 2 * k).astype(self.dtype)
+        self.copy1().start()
+
+    def second(self, piece):
+        self.copy1().wait()
+        r = self.links.r
+        kept = self.rb1[self.two // 2, 0 : self.rows].astype(F32)
+        self.sb2[0 : self.rows] = (piece(self.two) + kept).astype(self.dtype)
+        self.copy2().start()
+        self.mine[0 : self.rows] = piece(r) + self.rb1[r // 2, 0 : self.rows].astype(F32)
+
+    def third(self):
+        self.copy2().wait()
+        total = self.mine[0 : self.rows] + self.rb2[0 : self.rows].astype(F32)
+        self.mine[0 : self.rows] = total
+        self.sb2[0 : self.rows] = total.astype(self.dtype)
+        self.each(self.copy3, lambda c: c.start())
+
+    def fourth(self):
+        self.each(self.copy3, lambda c: c.wait())
+        total = self.part(self.mine, self.links.i)[...]
+        for k in range(1, self.links.ni):
+            total = total + self.rb3[self.peer(k)].astype(F32)
+        self.part(self.ag, self.links.i)[...] = total.astype(self.dtype)
+        self.each(self.copy4, lambda c: c.start())
+
+    def end(self):
+        self.each(self.copy4, lambda c: c.wait())
+        return self.ag[0 : self.rows].astype(F32)
 
 
 def norm_terms(total, square, count, gain, shift):
@@ -189,6 +299,7 @@
     pd_hbm,
     mx_hbm,
     mk_hbm,
+    xt_hbm,
     v1,
     v2,
     v3,
@@ -206,6 +317,7 @@
     pd,
     mx,
     mk,
+    xt,
     xbuf,
     a3,
     acc1,
@@ -246,6 +358,7 @@
         )
 
     x_copy(0, 0).start()
+    pending = []
 
     def first(b, c):
         slot = lax.rem(b, 2)
@@ -262,6 +375,7 @@
     lax.fori_loop(0, blocks, first, 0)
     out_fp = pltpu.make_async_copy(fp, fp_hbm, osem.at[0])
     out_fp.start()
+    pending.append(out_fp)
     acc1[...] = jnp.zeros_like(acc1)
 
     def first_sums(i, c):
@@ -282,6 +396,7 @@
     lax.fori_loop(0, images, first_sums, 0)
     out_mk = pltpu.make_async_copy(mk, mk_hbm, osem.at[1])
     out_mk.start()
+    pending.append(out_mk)
 
     me = links.all_me()
     buf1[me, 0:1] = row_sum(acc1[0])
@@ -330,6 +445,27 @@
     def _():
         below[...] = jnp.zeros_like(below)
 
+    x_copy(0, 0).start()
+    xt[...] = jnp.zeros_like(xt)
+
+    def against_input(b, c):
+        slot = lax.rem(b, 2)
+
+        @pl.when(b + 1 < blocks)
+        def _():
+            x_copy(b + 1, 1 - slot).start()
+
+        m = mk[pl.ds(b * GROUP, GROUP)].reshape(GROUP * cells, 128)
+        v = fp[pl.ds(b * GROUP, GROUP)].reshape(GROUP * cells, mid) * wide(m, mid // 128)
+        v = jnp.concatenate([v.astype(BF16), m.astype(BF16)], axis=1)
+        x_copy(b, slot).wait()
+        xt[...] += mm_tn(v, xbuf[slot].reshape(GROUP * cells, ch))
+        return c
+
+    lax.fori_loop(0, blocks, against_input, 0)
+    out_xt = pltpu.make_async_copy(xt, xt_hbm, osem.at[5])
+    out_xt.start()
+    pending.append(out_xt)
     total = links.all_wait(buf1, sem1)
     n = total[2:3, 0:1]
     mean, factor, scale, offset = norm_terms(total[0:1], total[1:2], n, g1[...], h1[...])
@@ -412,8 +548,10 @@
         return c
 
     lax.fori_loop(0, blocks, second, 0)
+    pending += [a3_copy(0, 0), a3_copy(0, 1)]
     out_sp = pltpu.make_async_copy(sp, sp_hbm, osem.at[2])
     out_sp.start()
+    pending.append(out_sp)
 
     def second_sums(i, c):
         m = wide(mk[i].reshape(cells, 128), mid // 128)
@@ -493,8 +631,10 @@
     lax.fori_loop(0, blocks, mixing, 0)
     out_mx = pltpu.make_async_copy(mx, mx_hbm, osem.at[4])
     out_mx.start()
+    pending.append(out_mx)
     out_pd = pltpu.make_async_copy(pd, pd_hbm, osem.at[3])
     out_pd.start()
+    pending.append(out_pd)
     gw[...] = mm_terms(mm, gram[...], we[...], 3)
     wef = we[...].astype(F32)
     rbuf4[r, 0:1] = row_sum(wide(mixed_sum[...], ch // 128) * wef)
@@ -508,13 +648,8 @@
     v3[3:4] = offset
     v3[4:8] = jnp.zeros((4, ch), F32)
 
-    for slot in range(2):
-        a3_copy(0, slot).wait()
-    out_fp.wait()
-    out_mk.wait()
-    out_sp.wait()
-    out_pd.wait()
-    out_mx.wait()
+    for copy in pending:
+        copy.wait()
 
 
 def sd(shape, dtype=F32):
@@ -531,6 +666,7 @@
         (sd(cells + (mid,), BF16), ANY),
         (sd(cells + (mid,), BF16), ANY),
         (sd(cells + (128,)), ANY),
+        (sd((mid + 128, ch)), ANY),
         (sd((8, mid)), VMEM),
         (sd((8, 2 * mid)), VMEM),
         (sd((8, ch)), VMEM),
@@ -551,6 +687,7 @@
         pltpu.VMEM(cells + (mid,), BF16),
         pltpu.VMEM(cells + (mid,), BF16),
         pltpu.VMEM(cells + (128,), F32),
+        pltpu.VMEM((mid + 128, ch), F32),
         pltpu.VMEM((2, GROUP, slots, cols, ch), BF16),
         pltpu.VMEM((2, GROUP, slots + 2, cols, 3 * mid), BF16),
         pltpu.VMEM((3, 8, mid), F32),
@@ -566,7 +703,7 @@
         pltpu.VMEM((n_row, 2, ch), F32),
         pltpu.VMEM((n_img, 2, ch), F32),
         dma((2,)),
-        dma((5,)),
+        dma((6,)),
         dma((2,)),
         dma((4,)),
         dma((2, n)),
@@ -683,6 +820,8 @@
     pd_hbm,
     mx_hbm,
     mk_hbm,
+    xt_hbm,
+    x_hbm,
     v1,
     v2,
     v3,
@@ -702,25 +841,25 @@
     up,
     we,
     awe,
-    fu_hbm,
-    expand_part,
-    split_part,
-    down_part,
-    up_part,
-    bias_part,
+    fg_hbm,
+    expand_out,
+    split_out,
+    reduce_out,
+    up_out,
+    down_out,
     b1,
     b2,
     b3,
     b_at,
     mg,
-    fp,
     sp,
     pd,
-    ub,
     mx,
     mk,
-    a3,
-    gpad,
+    split_part,
+    small_part,
+    rows_all,
+    geb,
     edge,
     ret,
     acc1,
@@ -736,6 +875,7 @@
     buf8,
     lsem,
     a3sem,
+    xsem,
     hsem,
     rsem5,
     isem5,
@@ -743,23 +883,33 @@
     isem6,
     sem7,
     sem8,
+    rsem9,
+    *reducers,
 ):
     images, slots, cols, mid = q_hbm.shape
     ch = we.shape[1]
+    inter = down.shape[1]
     half = mid // 2
     blocks = images // GROUP
     cells = slots * cols
     links = Links(n_img, n_row)
     r, me = links.r, links.all_me()
     links.greet()
+    sizes = reducer_sizes(n_row, ch, mid, inter)
+    count = Reducer.COUNT
+    expand_red, split_red, reduce_red, small_red = [
+        Reducer(links, rows, width, reducers[k * count : (k + 1) * count])
+        for k, (rows, width, _) in enumerate(sizes)
+    ]
     loads = [
         pltpu.make_async_copy(src, dst, lsem.at[k])
         for k, (src, dst) in enumerate(
-            [(mx_hbm, mx), (q_hbm, mg), (pd_hbm, pd), (mk_hbm, mk), (sp_hbm, sp), (fp_hbm, fp)]
+            [(mx_hbm, mx), (q_hbm, mg), (pd_hbm, pd), (mk_hbm, mk), (sp_hbm, sp)]
         )
     ]
     for load in loads:
         load.start()
+    pending = list(loads)
 
     n = v1[4:5, 0:1]
     mean3, factor3, scale3 = v3[0:1], v3[1:2], v3[2:3]
@@ -775,12 +925,18 @@
     mb[...] = mm_terms(mm, wef * slope, awe[...], 2)
     level = total[0:1] / n - slope * mean3
     ev = mm_terms(mm, jnp.broadcast_to(level, (8, ch)), awe[...], 3)[0:1]
-    expand_part[...] = (
-        m_in[0:mid] * scale3 - wide(mixed_sum[...], ch // 128) * offset3 - gw[...] * slope3
-    )
+
+    def expand_piece(p):
+        rows = pl.ds(pl.multiple_of(p * (mid // n_row), mid // n_row), mid // n_row)
+        return (
+            m_in[rows] * scale3 - wide(mixed_sum[rows], ch // 128) * offset3 - gw[rows] * slope3
+        )
+
+    expand_red.begin(expand_piece)
 
     for load in loads[:4]:
         load.wait()
+    del pending[:4]
 
     def mix_back(b, c):
         v = mx[pl.ds(b * GROUP, GROUP)].reshape(GROUP * cells, mid)
@@ -802,13 +958,14 @@
 
     lax.fori_loop(0, blocks, mix_back, 0)
 
+    expand_red.second(expand_piece)
     upf = up[...].astype(F32)
     lean = dpart[...] * w0[...] * w1[...]
     rbuf6[r] = mm_nt(lean, upf[:, :mid] - upf[:, mid:], HIGH)
     z = at_out[...]
     attend = z * sigmoid(z)
-    up_part[...] = mm_tn(attend, lean, HIGH)
-    bias_part[...] = jnp.broadcast_to(row_sum(lean), bias_part.shape)
+    up_part = mm_tn(attend, lean, HIGH)
+    buf7[me, 2:3] = wide(row_sum(lean), 2)
     attend_grad = links.row_total(rbuf6, rsem6) * swish_slope(z)
     ibuf6[links.i, 0:1] = row_sum(attend_grad)
     ibuf6[links.i, 1:2] = row_sum(attend_grad * at_norm[...])
@@ -820,37 +977,21 @@
         * v_at[0:1]
         * (attend_grad - total[0:1] / count - at_norm[...] * (total[1:2] / count))
     )
-    down_part[...] = mm_tn(pooled[...], squeeze_grad, HIGH)
+    down_part = mm_tn(pooled[...], squeeze_grad, HIGH)
+    up_rows, down_rows = inter // n_row, mid // n_row
+    for p in range(n_row):
+        lines = down_part[p * down_rows : (p + 1) * down_rows]
+        small_part[p, 0:up_rows] = up_part[p * up_rows : (p + 1) * up_rows]
+        small_part[p, up_rows:] = jnp.concatenate(
+            [lines[: down_rows // 2], lines[down_rows // 2 :]], axis=1
+        )
+
+    def small_piece(p):
+        return small_part[p]
+
+    expand_red.third()
+    small_red.begin(small_piece)
     pgrad[...] = mm_nt(squeeze_grad, down[...].astype(F32), HIGH) / area[...]
-
-    loads[4].wait()
-    acc2[...] = jnp.zeros_like(acc2)
-
-    def second_back(i, c):
-        m = wide(mk[i].reshape(cells, 128), mid // 128)
-        v = mg[i].reshape(cells, mid)
-        for g, w in enumerate((w0, w1)):
-            lanes = slice(g * mid, (g + 1) * mid)
-            s = sp[i, :, :, lanes].reshape(cells, mid)
-            z = s * v2[2:3, lanes] + v2[3:4, lanes]
-            grad = (v * w[pl.ds(i, 1)] + pgrad[pl.ds(i, 1)]) * swish_slope(z) * m
-            ub[i, :, :, lanes] = grad.reshape(slots, cols, mid)
-            acc2[0, :, lanes] += fold(grad)
-            acc2[1, :, lanes] += fold(grad * s)
-        return c
-
-    lax.fori_loop(0, images, second_back, 0)
-    mean2, factor2, scale2 = v2[0:1], v2[1:2], v2[2:3]
-    s0 = row_sum(acc2[0])
-    buf7[me, 0:1] = s0
-    buf7[me, 1:2] = factor2 * (row_sum(acc2[1]) - mean2 * s0)
-    links.all_start(buf7, sem7)
-    total = links.all_wait(buf7, sem7)
-    b2[...] = total
-    slope2, offset2 = norm_back_terms(mean2, factor2, scale2, n, total[0:1], total[1:2])
-
-    def second_grad(grad, s, m):
-        return (grad * scale2 - m * (offset2 + slope2 * s)).astype(BF16)
 
     prev_dev = (links.i, lax.rem(r + n_row - 1, n_row))
     next_dev = (links.i, lax.rem(r + 1, n_row))
@@ -879,135 +1020,301 @@
         right = jnp.where(col == 0, 0.0, pltpu.roll(t[:, 2 * half : 3 * half], 1, 0))
         return left + t[:, half : 2 * half] + right
 
-    for side, dy in ((0, 0), (1, 2)):
-
-        def edge_rows(b, c):
+    def to_second_grads(ub, a3):
+        loads[4].wait()
+        del pending[0]
+        acc2[...] = jnp.zeros_like(acc2)
+
+        def second_back(i, c):
+            m = wide(mk[i].reshape(cells, 128), mid // 128)
+            v = mg[i].reshape(cells, mid)
+            for g, w in enumerate((w0, w1)):
+                lanes = slice(g * mid, (g + 1) * mid)
+                s = sp[i, :, :, lanes].reshape(cells, mid)
+                z = s * v2[2:3, lanes] + v2[3:4, lanes]
+                grad = (v * w[pl.ds(i, 1)] + pgrad[pl.ds(i, 1)]) * swish_slope(z) * m
+                ub[i, :, :, lanes] = grad.reshape(slots, cols, mid)
+                acc2[0, :, lanes] += fold(grad)
+                acc2[1, :, lanes] += fold(grad * s)
+            return c
+
+        lax.fori_loop(0, images, second_back, 0)
+        expand_red.fourth()
+        small_red.second(small_piece)
+        mean2, factor2, scale2 = v2[0:1], v2[1:2], v2[2:3]
+        s0 = row_sum(acc2[0])
+        buf7[me, 0:1] = s0
+        buf7[me, 1:2] = factor2 * (row_sum(acc2[1]) - mean2 * s0)
+        links.all_start(buf7, sem7)
+        total = links.all_wait(buf7, sem7)
+        b2[...] = total
+        slope2, offset2 = norm_back_terms(mean2, factor2, scale2, n, total[0:1], total[1:2])
+        expand_out[...] = expand_red.end()
+        small_red.third()
+
+        def second_grad(grad, s, m):
+            return (grad * scale2 - m * (offset2 + slope2 * s)).astype(BF16)
+
+        for side, dy in ((0, 0), (1, 2)):
+
+            def edge_rows(b, c):
+                def one(k, c):
+                    i = b * GROUP + k
+                    at = 0 if side == 0 else jnp.maximum(counts[i] - 1, 0)
+                    m = wide(mk[i, 0], 2 * mid // 128)
+                    geb[k] = second_grad(ub[i, at], sp[i, at], m)
+                    return c
+
+                lax.fori_loop(0, GROUP, one, 0)
+                for g in range(2):
+                    v = geb[:, :, g * mid : (g + 1) * mid].reshape(GROUP * cols, mid)
+                    t = mm_nt(v, ws[dy, :, g * mid : (g + 1) * mid])
+                    edge[side, pl.ds(b * GROUP, GROUP), :, g * half : (g + 1) * half] = (
+                        columns_back(t, GROUP * cols).astype(BF16).reshape(GROUP, cols, half)
+                    )
+                return c
+
+            lax.fori_loop(0, blocks, edge_rows, 0)
+            if side == 0:
+
+                @pl.when(has_prev)
+                def _():
+                    to_prev.start()
+
+            else:
+
+                @pl.when(has_next)
+                def _():
+                    to_next.start()
+
+        @pl.when(jnp.logical_not(has_prev))
+        def _():
+            ret[0] = jnp.zeros(ret.shape[1:], BF16)
+
+        @pl.when(jnp.logical_not(has_next))
+        def _():
+            ret[1] = jnp.zeros(ret.shape[1:], BF16)
+
+        def a3_copy(b, slot):
+            return pltpu.make_async_copy(
+                a3_hbm.at[pl.ds(b * GROUP, GROUP)], a3.at[slot], a3sem.at[slot]
+            )
+
+        a3_copy(0, 0).start()
+        split_part[...] = jnp.zeros_like(split_part)
+
+        def split_grads(b, c):
+            slot = lax.rem(b, 2)
+
+            @pl.when(b + 1 < blocks)
+            def _():
+                a3_copy(b + 1, 1 - slot).start()
+
             def one(k, c):
                 i = b * GROUP + k
-                at = 0 if side == 0 else jnp.maximum(counts[i] - 1, 0)
-                m = wide(mk[i, 0], 2 * mid // 128)
-                gpad[k, 0] = second_grad(ub[i, at], sp[i, at], m)
+                m = wide(mk[i].reshape(cells, 128), 2 * mid // 128)
+                v = second_grad(ub[i].reshape(cells, 2 * mid), sp[i].reshape(cells, 2 * mid), m)
+                mx[i] = v[:, 0:mid].reshape(slots, cols, mid)
+                pd[i] = v[:, mid:].reshape(slots, cols, mid)
                 return c
 
             lax.fori_loop(0, GROUP, one, 0)
-            for g in range(2):
-                v = gpad[:, 0, :, g * mid : (g + 1) * mid].reshape(GROUP * cols, mid)
-                t = mm_nt(v, ws[dy, :, g * mid : (g + 1) * mid])
-                edge[side, pl.ds(b * GROUP, GROUP), :, g * half : (g + 1) * half] = (
-                    columns_back(t, GROUP * cols).astype(BF16).reshape(GROUP, cols, half)
+            a3_copy(b, slot).wait()
+            for g, grads in enumerate((mx, pd)):
+                v = grads[pl.ds(b * GROUP, GROUP)].reshape(GROUP * cells, mid)
+                taps = jnp.concatenate(
+                    [
+                        a3[slot, :, dy : dy + slots, :, g * 3 * half : (g + 1) * 3 * half].reshape(
+                            GROUP * cells, 3 * half
+                        )
+                        for dy in range(3)
+                    ],
+                    axis=1,
                 )
-            return c
-
-        lax.fori_loop(0, blocks, edge_rows, 0)
-        if side == 0:
-
-            @pl.when(has_prev)
+                split_part[g] += mm_tn(v, taps)
+            return c
+
+        lax.fori_loop(0, blocks, split_grads, 0)
+
+    pl.run_scoped(
+        to_second_grads,
+        pltpu.VMEM((images, slots, cols, 2 * mid), F32),
+        pltpu.VMEM((2, GROUP, slots + 2, cols, 3 * mid), BF16),
+    )
+
+    def to_inputs(fp, xbuf, xt, xu, split_rows):
+        loads = [
+            pltpu.make_async_copy(fp_hbm, fp, lsem.at[5]),
+            pltpu.make_async_copy(xt_hbm, xt, lsem.at[6]),
+        ]
+        for load in loads:
+            load.start()
+        small_red.fourth()
+
+        def split_piece(p):
+            lines = []
+            for tap in range(9):
+                at = pl.multiple_of(tap * half + p * (half // n_row), half // n_row)
+                lines.append(split_rows[pl.ds(at, half // n_row)])
+            return jnp.concatenate(lines, axis=0)
+
+        for g in range(2):
+            for tap in range(9):
+                split_rows[tap * half : (tap + 1) * half, g * mid : (g + 1) * mid] = jnp.transpose(
+                    split_part[g, :, tap * half : (tap + 1) * half]
+                )
+        split_red.begin(split_piece)
+
+        def conv_back(b, c):
+            @pl.when(b == 2)
             def _():
-                to_prev.start()
-
-        else:
-
-            @pl.when(has_next)
+                split_red.second(split_piece)
+
+            @pl.when(b == 4)
             def _():
-                to_next.start()
-
-    @pl.when(jnp.logical_not(has_prev))
-    def _():
-        ret[0] = jnp.zeros(ret.shape[1:], BF16)
-
-    @pl.when(jnp.logical_not(has_next))
-    def _():
-        ret[1] = jnp.zeros(ret.shape[1:], BF16)
-
-    def a3_copy(b, slot):
-        return pltpu.make_async_copy(
-            a3_hbm.at[pl.ds(b * GROUP, GROUP)], a3.at[slot], a3sem.at[slot]
-        )
-
-    a3_copy(0, 0).start()
-    gpad[:, 0] = jnp.zeros((GROUP, cols, 2 * mid), BF16)
-    gpad[:, slots + 1] = jnp.zeros((GROUP, cols, 2 * mid), BF16)
-    split_part[...] = jnp.zeros_like(split_part)
-
-    def conv_back(b, c):
-        slot = lax.rem(b, 2)
-
-        @pl.when(b + 1 < blocks)
+                split_red.third()
+
+            blank = jnp.zeros((GROUP, 1, cols, mid), BF16)
+            for g, grads in enumerate((mx, pd)):
+                lanes = slice(g * mid, (g + 1) * mid)
+                v = grads[pl.ds(b * GROUP, GROUP)]
+                moved = (
+                    jnp.concatenate([v[:, 1:], blank], axis=1),
+                    v,
+                    jnp.concatenate([blank, v[:, : slots - 1]], axis=1),
+                )
+                value = None
+                for dy in range(3):
+                    part = mm_nt(moved[dy].reshape(GROUP * cells, mid), ws[dy, :, lanes])
+                    value = part if value is None else value + part
+                mg[pl.ds(b * GROUP, GROUP), :, :, g * half : (g + 1) * half] = columns_back(
+                    value, GROUP * cells
+                ).reshape(GROUP, slots, cols, half)
+            return c
+
+        lax.fori_loop(0, blocks, conv_back, 0)
+        rows_all[r] = small_red.end()
+        rows_copies = links.row_copies(rows_all, rsem9)
+        for copy in rows_copies:
+            copy.start()
+        @pl.when(has_prev)
         def _():
-            a3_copy(b + 1, 1 - slot).start()
-
-        def one(k, c):
-            i = b * GROUP + k
-            m = wide(mk[i].reshape(cells, 128), 2 * mid // 128)
-            v = second_grad(
-                ub[i].reshape(cells, 2 * mid), sp[i].reshape(cells, 2 * mid), m
+            to_prev.wait_send()
+            to_next.wait_recv()
+
+        @pl.when(has_next)
+        def _():
+            to_next.wait_send()
+            to_prev.wait_recv()
+
+        loads[0].wait()
+        acc1[...] = jnp.zeros_like(acc1)
+
+        def first_back(i, c):
+            m = wide(mk[i].reshape(cells, 128), mid // 128)
+            count = counts[i]
+            low = ret[1, i].astype(F32)
+            parts = []
+            for s in range(slots):
+                here = mg[i, s] + low * jnp.where(count - 1 == s, 1.0, 0.0).astype(F32)
+                if s == 0:
+                    here = here + ret[0, i].astype(F32)
+                parts.append(here)
+            v = fp[i].reshape(cells, mid)
+            z = v * v1[2:3] + v1[3:4]
+            grad = jnp.concatenate(parts, axis=0) * swish_slope(z) * m
+            mg[i] = grad.reshape(slots, cols, mid)
+            acc1[0] += fold(grad)
+            acc1[1] += fold(grad * v)
+            return c
+
+        lax.fori_loop(0, images, first_back, 0)
+        s0 = row_sum(acc1[0])
+        buf8[me, 0:1] = s0
+        buf8[me, 1:2] = v1[1:2] * (row_sum(acc1[1]) - v1[0:1] * s0)
+        links.all_start(buf8, sem8)
+        split_red.fourth()
+
+        def x_copy(b, slot):
+            return pltpu.make_async_copy(
+                x_hbm.at[pl.ds(b * GROUP, GROUP)], xbuf.at[slot], xsem.at[slot]
             )
-            gpad[k, 1 : slots + 1] = v.reshape(slots, cols, 2 * mid)
-            return c
-
-        lax.fori_loop(0, GROUP, one, 0)
-        for g in range(2):
-            lanes = slice(g * mid, (g + 1) * mid)
-            value = None
-            for dy in range(3):
-                v = gpad[:, 2 - dy : 2 - dy + slots, :, lanes].reshape(GROUP * cells, mid)
-                part = mm_nt(v, ws[dy, :, lanes])
-                value = part if value is None else value + part
-            mg[pl.ds(b * GROUP, GROUP), :, :, g * half : (g + 1) * half] = columns_back(
-                value, GROUP * cells
-            ).reshape(GROUP, slots, cols, half)
-        a3_copy(b, slot).wait()
-        for g in range(2):
-            lanes = slice(g * mid, (g + 1) * mid)
-            v = gpad[:, 1 : slots + 1, :, lanes].reshape(GROUP * cells, mid)
-            for dy in range(3):
-                taps = a3[slot, :, dy : dy + slots, :, g * 3 * half : (g + 1) * 3 * half]
-                split_part[dy, g] += mm_tn(v, taps.reshape(GROUP * cells, 3 * half))
-        return c
-
-    lax.fori_loop(0, blocks, conv_back, 0)
-
-    @pl.when(has_prev)
-    def _():
-        to_prev.wait_send()
-        to_next.wait_recv()
-
-    @pl.when(has_next)
-    def _():
-        to_next.wait_send()
-        to_prev.wait_recv()
-
-    loads[5].wait()
-    acc1[...] = jnp.zeros_like(acc1)
-
-    def first_back(i, c):
-        m = wide(mk[i].reshape(cells, 128), mid // 128)
-        count = counts[i]
-        low = ret[1, i].astype(F32)
-        parts = []
-        for s in range(slots):
-            here = mg[i, s] + low * jnp.where(count - 1 == s, 1.0, 0.0).astype(F32)
-            if s == 0:
-                here = here + ret[0, i].astype(F32)
-            parts.append(here)
-        v = fp[i].reshape(cells, mid)
-        z = v * v1[2:3] + v1[3:4]
-        grad = jnp.concatenate(parts, axis=0) * swish_slope(z) * m
-        mg[i] = grad.reshape(slots, cols, mid)
-        acc1[0] += fold(grad)
-        acc1[1] += fold(grad * v)
-        return c
-
-    lax.fori_loop(0, images, first_back, 0)
-    out_fu = pltpu.make_async_copy(mg, fu_hbm, lsem.at[6])
-    out_fu.start()
-    s0 = row_sum(acc1[0])
-    buf8[me, 0:1] = s0
-    buf8[me, 1:2] = v1[1:2] * (row_sum(acc1[1]) - v1[0:1] * s0)
-    links.all_start(buf8, sem8)
-    total = links.all_wait(buf8, sem8)
-    b1[...] = total
-    out_fu.wait()
+
+        x_copy(0, 0).start()
+        xu[...] = jnp.zeros_like(xu)
+
+        def against_input(b, c):
+            slot = lax.rem(b, 2)
+
+            @pl.when(b + 1 < blocks)
+            def _():
+                x_copy(b + 1, 1 - slot).start()
+
+            v = mg[pl.ds(b * GROUP, GROUP)].reshape(GROUP * cells, mid).astype(BF16)
+            x_copy(b, slot).wait()
+            xu[...] += mm_tn(v, xbuf[slot].reshape(GROUP * cells, ch))
+            return c
+
+        lax.fori_loop(0, blocks, against_input, 0)
+        loads[1].wait()
+        total = links.all_wait(buf8, sem8)
+        b1[...] = total
+        slope1, offset1 = norm_back_terms(v1[0:1], v1[1:2], v1[2:3], n, total[0:1], total[1:2])
+
+        def reduce_piece(p):
+            lanes = pl.ds(pl.multiple_of(p * (ch // n_row), ch // n_row), ch // n_row)
+            return (
+                jnp.transpose(xu[:, lanes]) * v1[2:3]
+                - jnp.transpose(xt[mid : mid + 128, lanes])[:, 0:1] * offset1
+                - jnp.transpose(xt[0:mid, lanes]) * slope1
+            )
+
+        reduce_red.begin(reduce_piece)
+
+        def first_grad(i, c):
+            m = wide(mk[i].reshape(cells, 128), mid // 128)
+            v = mg[i].reshape(cells, mid) * v1[2:3] - m * (
+                offset1 + slope1 * fp[i].reshape(cells, mid)
+            )
+            mx[i] = v.astype(BF16).reshape(slots, cols, mid)
+            return c
+
+        lax.fori_loop(0, images // 2, first_grad, 0)
+        reduce_red.second(reduce_piece)
+        lax.fori_loop(images // 2, images, first_grad, 0)
+        out_fg = pltpu.make_async_copy(mx, fg_hbm, lsem.at[7])
+        out_fg.start()
+        reduce_red.third()
+        split_out[...] = split_red.end()
+        for copy in rows_copies:
+            copy.wait()
+        for p in range(n_row):
+            up_out[p * up_rows : (p + 1) * up_rows] = rows_all[p, 0:up_rows]
+            lines = rows_all[p, up_rows:]
+            down_out[p * down_rows : (p + 1) * down_rows] = jnp.concatenate(
+                [lines[:, 0:inter], lines[:, inter:]], axis=0
+            )
+        reduce_red.fourth()
+        reduce_out[...] = reduce_red.end()
+        out_fg.wait()
+
+    pl.run_scoped(
+        to_inputs,
+        pltpu.VMEM((images, slots, cols, mid), F32),
+        pltpu.VMEM((2, GROUP, slots, cols, ch), BF16),
+        pltpu.VMEM((mid + 128, ch), F32),
+        pltpu.VMEM((mid, ch), F32),
+        pltpu.VMEM((9 * half, 2 * mid), F32),
+    )
+
+
+def reducer_sizes(n_row, ch, mid, inter):
+    return [
+        (mid // n_row, ch, BF16),
+        (9 * (mid // 2) // n_row, 2 * mid, BF16),
+        (ch // n_row, mid, BF16),
+        (inter // n_row + mid // n_row // 2, mid, F32),
+    ]
 
 
 def call_backward(n_img, n_row, args, ch, inter):
@@ -1016,29 +1323,30 @@
     half = mid // 2
     n = n_img * n_row
     cells = (images, slots, cols)
+    sizes = reducer_sizes(n_row, ch, mid, inter)
     outs = [
-        (sd(cells + (mid,)), ANY),
-        (sd((mid, ch)), VMEM),
-        (sd((3, 2, mid, 3 * half)), VMEM),
+        (sd(cells + (mid,), BF16), ANY),
+        (sd((mid // n_row, ch)), VMEM),
+        (sd((9 * half // n_row, 2 * mid)), VMEM),
+        (sd((ch // n_row, mid)), VMEM),
+        (sd((inter, mid)), VMEM),
         (sd((mid, inter)), VMEM),
-        (sd((inter, mid)), VMEM),
-        (sd((8, mid)), VMEM),
         (sd((2, mid)), VMEM),
-        (sd((2, 2 * mid)), VMEM),
+        (sd((3, 2 * mid)), VMEM),
         (sd((2, ch)), VMEM),
         (sd((2, inter)), VMEM),
     ]
     dma = pltpu.SemaphoreType.DMA
     scratch = [
         pltpu.VMEM(cells + (mid,), F32),
-        pltpu.VMEM(cells + (mid,), F32),
         pltpu.VMEM(cells + (2 * mid,), F32),
         pltpu.VMEM(cells + (mid,), BF16),
-        pltpu.VMEM(cells + (2 * mid,), F32),
         pltpu.VMEM(cells + (mid,), BF16),
         pltpu.VMEM(cells + (128,), F32),
-        pltpu.VMEM((2, GROUP, slots + 2, cols, 3 * mid), BF16),
-        pltpu.VMEM((GROUP, slots + 2, cols, 2 * mid), BF16),
+        pltpu.VMEM((2, mid, 9 * half), F32),
+        pltpu.VMEM((n_row, sizes[3][0], mid), F32),
+        pltpu.VMEM((n_row, sizes[3][0], mid), F32),
+        pltpu.VMEM((GROUP, cols, 2 * mid), BF16),
         pltpu.VMEM((2, images, cols, mid), BF16),
         pltpu.VMEM((2, images, cols, mid), BF16),
         pltpu.VMEM((2, 8, mid), F32),
@@ -1050,9 +1358,10 @@
         pltpu.VMEM((n_row, 2, ch), F32),
         pltpu.VMEM((n_row, images, inter), F32),
         pltpu.VMEM((n_img, 2, inter), F32),
-        pltpu.VMEM((n, 2, 2 * mid), F32),
+        pltpu.VMEM((n, 3, 2 * mid), F32),
         pltpu.VMEM((n, 2, mid), F32),
-        dma((7,)),
+        dma((8,)),
+        dma((2,)),
         dma((2,)),
         dma((4,)),
         dma((2, n_row)),
@@ -1061,8 +1370,11 @@
         dma((2, n_img)),
         dma((2, n)),
         dma((2, n)),
+        dma((2, n_row)),
     ]
-    in_specs = [SMEM] + [ANY] * 7 + [VMEM] * (len(args) - 8)
+    for rows, width, dtype in sizes:
+        scratch += Reducer.scratch(n_img, rows, width, dtype)
+    in_specs = [SMEM] + [ANY] * 9 + [VMEM] * (len(args) - 10)
     return pl.pallas_call(
         functools.partial(backward_kernel, n_img, n_row),
         out_shape=[o for o, _ in outs],
@@ -1071,51 +1383,34 @@
         scratch_shapes=scratch,
         name="backward",
         compiler_params=pltpu.CompilerParams(
-            collective_id=1, has_side_effects=True, vmem_limit_bytes=60 * 1024 * 1024
+            collective_id=1, has_side_effects=True, vmem_limit_bytes=62 * 1024 * 1024
         ),
     )(*args)
 
 
-def input_kernel(fu, fp, mk, x, sg, wr, vec, gi, red):
-    per, slots, cols, ch = x.shape
-    mid = fp.shape[-1]
+def input_kernel(fg, sg, wr, gi):
+    per, slots, cols, ch = sg.shape
     cells = per * slots * cols
-
-    m = wide(mk[...].reshape(cells, 128), mid // 128)
-    fg = fu[...].reshape(cells, mid) * vec[0:1] - m * (
-        vec[1:2] + vec[2:3] * fp[...].reshape(cells, mid)
-    )
-    fg = fg.astype(BF16)
-    value = mm_nt(fg, wr[...]) + sg[...].reshape(cells, ch).astype(F32)
-    gi[...] = value.astype(BF16).reshape(gi.shape)
-
-    @pl.when(pl.program_id(0) == 0)
-    def _():
-        red[...] = jnp.zeros_like(red)
-
-    red[...] += mm_tn(fg, x[...].reshape(cells, ch))
-
-
-def call_input(fu, fp, mk, x, sg, wr, vec):
-    images, slots, cols, ch = x.shape
-    mid = fp.shape[-1]
+    value = mm_nt(fg[...].reshape(cells, fg.shape[-1]), wr[...])
+    gi[...] = (value + sg[...].reshape(cells, ch).astype(F32)).astype(BF16).reshape(gi.shape)
+
+
+def call_input(fg, sg, wr):
+    images, slots, cols, ch = sg.shape
     per = 4
 
     def cells(c):
         return pl.BlockSpec((per, slots, cols, c), lambda b: (b, 0, 0, 0))
 
-    def whole(a):
-        return pl.BlockSpec(a.shape, lambda b: (0,) * a.ndim)
-
     return pl.pallas_call(
         input_kernel,
-        out_shape=[sd(x.shape, BF16), sd((mid, ch))],
+        out_shape=sd(sg.shape, BF16),
         grid=(images // per,),
-        in_specs=[cells(mid), cells(mid), cells(128), cells(ch), cells(ch), whole(wr), whole(vec)],
-        out_specs=[cells(ch), pl.BlockSpec((mid, ch), lambda b: (0, 0))],
+        in_specs=[cells(fg.shape[-1]), cells(ch), pl.BlockSpec(wr.shape, lambda b: (0, 0))],
+        out_specs=cells(ch),
         name="input_grad",
         compiler_params=pltpu.CompilerParams(vmem_limit_bytes=48 * 1024 * 1024),
-    )(fu, fp, mk, x, sg, wr, vec)
+    )(fg, sg, wr)
 
 
 def body(
@@ -1153,7 +1448,7 @@
         return v[None, :]
 
     (
-        fp, a3, sp, pd, mx, mk, v1, v2, v3, v_at, at_norm, at_out, w0, w1, pooled, gw, mixed_sum,
+        fp, a3, sp, pd, mx, mk, xt, v1, v2, v3, v_at, at_norm, at_out, w0, w1, pooled, gw, mixed_sum,
     ) = call_forward(
         n_img,
         n_row,
@@ -1185,32 +1480,20 @@
         counts, feature_map, cotangent, mx, mk, expand_weight, awe, half_terms
     )
     (
-        fu, expand_part, split_part, down_part, up_part, bias_part, b1, b2, b3, b_at,
+        fg, grad_expand, grad_split, grad_reduce, grad_up, grad_down, b1, b2, b3, b_at,
     ) = call_backward(
         n_img,
         n_row,
         (
-            counts, q, fp, a3, sp, pd, mx, mk, v1, v2, v3, v_at, at_norm, at_out, w0, w1, pooled,
+            counts, q, fp, a3, sp, pd, mx, mk, xt, feature_map, v1, v2, v3, v_at, at_norm, at_out, w0, w1, pooled,
             gw, mixed_sum, m_sum, area, line(gain_attend), ws, attn_down, attn_up, expand_weight,
             awe,
         ),
         ch, inter,
     )
-    slope1, offset1 = norm_back_terms(v1[0:1], v1[1:2], v1[2:3], v1[4, 0], b1[0:1], b1[1:2])
-    vec = jnp.concatenate([v1[2:3], offset1, slope1, jnp.zeros((5, mid), F32)], axis=0)
-    grad_input, reduce_t = call_input(fu, fp, mk, feature_map, sg, reduce_weight, vec)
-
-    split = split_part.reshape(3, 2, mid, 3, half).transpose(0, 3, 4, 1, 2)
-    split = split.reshape(3, 3, half, 2 * mid)
-
-    def shared(v, dim):
-        v = lax.psum_scatter(v, "row", scatter_dimension=dim, tiled=True)
-        return lax.psum(v, "img")
-
-    grad_reduce = shared(reduce_t.T, 0)
-    grad_split = shared(split, 2)
-    grad_expand = shared(expand_part, 0)
-    grad_down, grad_up, grad_bias = lax.psum((down_part, up_part, bias_part[0]), ("img", "row"))
+    grad_input = call_input(fg, sg, reduce_weight)
+    grad_split = grad_split.reshape(3, 3, half // n_row, 2 * mid)
+    grad_bias = b2[2, 0:mid]
     return (
         block_out,
         grad_input,

time: 568 us -> 258 us (0.45)
  waiting for transfers between devices: 268 us -> 0 us
  blocking collectives: 39.4 us -> 0 us
  Pallas kernels: 209 us -> 241 us
  local copies, waits for them, and re-layouts: 28.1 us -> 12.5 us
  between operations: 14.6 us -> 0.81 us
    psum x2 -> x0, waiting for transfers between devices: 173 us -> none  [the longest x1 88.5 us: body(): lax.psum((down_part, up_part, bias_part[0]), ('img', 'row'))]
    reduce_scatter x2 -> x0, waiting for transfers between devices: 53 us -> none  [shared(): v = lax.psum_scatter(v, 'row', scatter_dimension=dim, tiled=True)]
    unnamed x6 -> x0, waiting for transfers between devices: 42.2 us -> none
    psum x1 -> x0, blocking collectives: 39.4 us -> none  [body(): lax.psum((down_part, up_part, bias_part[0]), ('img', 'row'))]
    pallas_call x1, Pallas kernels: 76 us -> 112 us  [call_backward(): pl.pallas_call(functools.partial(backward_kernel, n_img, n_row), out_shap...]
    unnamed x35 -> x37, local copies, waits for them, and re-layouts: 14.2 us -> 8.75 us
  transfers between devices with their start and end apart: 5 -> 0, of which waited for: 5 -> 0; matrix products, arithmetic and copies ran while one was open for 2% -> 0% of each run, Pallas kernels for 4% -> 0%
where the time goes in v2:
time: 258 us
  Pallas kernels  241 us (93%)
  local copies, waits for them, and re-layouts  12.5 us (5%)
  other arithmetic  3.49 us (1%)
    pallas_call x1, Pallas kernels, call_backward(): pl.pallas_call(functools.partial(backward_kernel, n_img, n_row), out_shap...  112 us
    pallas_call x1, Pallas kernels, call_forward(): pl.pallas_call(functools.partial(forward_kernel, n_img, n_row), out_shape...  75.5 us
    pallas_call x1, Pallas kernels, call_third(): pl.pallas_call(third_kernel, out_shape=[sd(x.shape, BF16), sd(x.shape, BF...  37.9 us
    pallas_call x1, Pallas kernels, call_input(): pl.pallas_call(input_kernel, out_shape=sd(sg.shape, BF16), grid=(images /...  15.3 us
    unnamed x37, local copies, waits for them, and re-layouts  8.75 us

profile of v2, /device:TPU:0, one launch (start us, length us, event | category | flops | bytes accessed | tf_op | source)
XLA Modules:
  0.0 257.6 jit_solution(12650502502302330022)
XLA Ops:
  0.6 1.2 multiply_convert_fusion.1
  1.8 0.7 broadcast_in_dim.35.area
  2.5 1.2 copy.34
  3.8 0.0 copy-start.1
  3.8 0.0 copy-start.6
  3.8 75.5 %forward.1 = (f32[56,6,16,256]{3,2,1,0:T(8,128)}, bf16[56,8,16,768]{3,2,1,0:T(8,128)(2,1)}, f32[56,6,16,512]{3,2,1,0:T(8,128)}, bf16[56,6,16,256]{3,2,1,0:T(8,12...) custom-call(s32[56]{0:T(128)} %bitcast.26, ...), custom_call_target="tpu_custom_call" | custom-call | tf_op jit(solution)/shard_map/forward/pallas_call | solution.py:717
  79.3 0.8 slice.33
  80.1 0.2 fusion.awe
  80.3 0.0 copy-start.2
  80.3 0.8 slice_multiply_fusion
  81.1 1.8 copy-done
  82.9 37.9 %third.1 = (bf16[56,6,16,1024]{3,2,1,0:T(8,128)(2,1)}, bf16[56,6,16,1024]{3,2,1,0:T(8,128)(2,1)}, f32[56,6,16,256]{3,2,1,0:T(8,128)}, f32[272,1024]{1,0:T(8,128)S(1)}) custom-call(s32[56]{0:T(128)S(1)} %bitcast.28, bf16[56,6,16,1024]{3,2,1,0:T(8,128)(2,1)} %x_hbm.3, bf16[56,6,16,1024]{3,2,1,0:T(8,128)(2,1)} %cot.1, bf16[56,6,16,256]{3,2,1,0:T(8,128)(2,1)S(1)} %copy-done, ...), custom_call_target="tpu_custom_call" | custom-call | tf_op jit(solution)/shard_map/third/pallas_call | solution.py:787
  120.8 1.0 copy-done.5
  121.8 112.1 %backward.1 = (bf16[56,6,16,256]{3,2,1,0:T(8,128)(2,1)}, f32[64,1024]{1,0:T(8,128)}, f32[288,512]{1,0:T(8,128)}, f32[256,256]{1,0:T(8,128)}, f32[128,256]{1,0:T(...) custom-call(s32[56]{0:T(128)} %bitcast.27, ...), custom_call_target="tpu_custom_call" | custom-call | tf_op jit(solution)/shard_map/backward/pallas_call | solution.py:1378
  233.9 0.0 copy-done.4
  233.9 0.0 copy-start.3
  234.0 1.8 copy-done.3
  235.7 0.0 copy-start.8
  235.7 0.0 copy-start.10
  235.8 0.0 copy-start.7
  235.8 0.0 copy-start.9
  235.8 15.3 %input_grad.1 = bf16[56,6,16,1024]{3,2,1,0:T(8,128)(2,1)} custom-call(bf16[56,6,16,256]{3,2,1,0:T(8,128)(2,1)S(1)} %copy-done.3, bf16[56,6,16,1024]{3,2,1,0:T(8,128)(2,1)} %get-tuple-element.70.sg, bf16[1024,256]{1,0:T(8,128)(2,1)S(1)} %copy-done.4), custom_call_target="tpu_custom_call" | custom-call | tf_op jit(solution)/shard_map/input_grad/pallas_call | solution.py:1405
  251.1 0.6 fusion.2
  251.7 0.6 pad_maximum_fusion.1
  252.3 0.5 slice_bitcast_fusion
  252.8 0.6 fusion.3
  253.4 0.6 fusion.1
  254.0 0.7 pad_maximum_fusion
  254.8 0.7 copy.39
  255.5 0.8 copy.40
  256.3 0.7 copy.41
  257.0 0.7 copy.42
  (24 shorter events, 0.1 us)
Async XLA Ops:
  3.8 77.4 %copy-start.1 = (bf16[256,1024]{1,0:T(8,128)(2,1)S(1)}, bf16[256,1024]{1,0:T(8,128)(2,1)}, u32[]{:S(2)}) copy-start(bf16[256,1024]{1,0:T(8,128)(2,1)} %we.5) | copy-start | bytes 1572868
  3.8 77.4 %copy-start.6 = (s32[56,1]{0,1:T(1,128)S(1)}, s32[56,1]{0,1:T(1,128)}, u32[]{:S(2)}) copy-start(s32[56,1]{0,1:T(1,128)} %param.20) | copy-start | bytes 676
  80.3 40.5 %copy-start.2 = (bf16[1024,256]{1,0:T(8,128)(2,1)}, bf16[1024,256]{1,0:T(8,128)(2,1)S(1)}, u32[]{:S(2)}) copy-start(bf16[1024,256]{1,0:T(8,128)(2,1)S(1)} %fusion.awe) | copy-start | bytes 1572868
  81.1 1.8 copy-start
  120.8 1.0 copy-start.5
  121.8 112.1 %copy-start.4 = (bf16[1024,256]{1,0:T(8,128)(2,1)S(1)}, bf16[1024,256]{1,0:T(8,128)(2,1)}, u32[]{:S(2)}) copy-start(bf16[1024,256]{1,0:T(8,128)(2,1)} %wr.3) | copy-start | bytes 1572868
  233.9 1.8 copy-start.3
  235.7 15.4 %copy-start.13 = (f32[3,512]{1,0:T(4,128)S(1)}, f32[3,512]{1,0:T(4,128)}, u32[]{:S(2)}) copy-start(f32[3,512]{1,0:T(4,128)} %get-tuple-element.76) | copy-start | bytes 18436
  235.7 16.6 %copy-start.15 = (f32[2,128]{1,0:T(2,128)S(1)}, f32[2,128]{1,0:T(2,128)}, u32[]{:S(2)}) copy-start(f32[2,128]{1,0:T(2,128)} %get-tuple-element.78) | copy-start | bytes 3076
  235.7 17.1 %copy-start.14 = (f32[2,256]{1,0:T(2,128)S(1)}, f32[2,256]{1,0:T(2,128)}, u32[]{:S(2)}) copy-start(f32[2,256]{1,0:T(2,128)} %get-tuple-element.77) | copy-start | bytes 6148
  235.7 17.7 %copy-start.12 = (f32[2,1024]{1,0:T(2,128)S(1)}, f32[2,1024]{1,0:T(2,128)}, u32[]{:S(2)}) copy-start(f32[2,1024]{1,0:T(2,128)} %get-tuple-element.79) | copy-start | bytes 24580
  235.7 18.3 %copy-start.8 = (f32[128,256]{1,0:T(8,128)S(1)}, f32[128,256]{1,0:T(8,128)}, u32[]{:S(2)}) copy-start(f32[128,256]{1,0:T(8,128)} %get-tuple-element.75) | copy-start | bytes 393220
  235.7 19.0 %copy-start.10 = (f32[256,256]{1,0:T(8,128)S(1)}, f32[256,256]{1,0:T(8,128)}, u32[]{:S(2)}) copy-start(f32[256,256]{1,0:T(8,128)} %get-tuple-element.108) | copy-start | bytes 786436
  235.8 19.7 %copy-start.7 = (f32[288,512]{1,0:T(8,128)S(1)}, f32[288,512]{1,0:T(8,128)}, u32[]{:S(2)}) copy-start(f32[288,512]{1,0:T(8,128)} %get-tuple-element.72) | copy-start | bytes 1769476
  235.8 20.5 %copy-start.9 = (f32[64,1024]{1,0:T(8,128)S(1)}, f32[64,1024]{1,0:T(8,128)}, u32[]{:S(2)}) copy-start(f32[64,1024]{1,0:T(8,128)} %get-tuple-element.110) | copy-start | bytes 786436
  235.8 21.2 %copy-start.11 = (f32[256,128]{1,0:T(8,128)S(1)}, f32[256,128]{1,0:T(8,128)}, u32[]{:S(2)}) copy-start(f32[256,128]{1,0:T(8,128)} %get-tuple-element.111) | copy-start | bytes 393220

commit v3 on v2

--- a/solution.py
+++ b/solution.py
@@ -276,9 +276,8 @@
     n_img,
     n_row,
     counts,
-    heights,
+    group,
     x_hbm,
-    area,
     wr,
     g1,
     h1,
@@ -309,7 +308,10 @@
     w0,
     w1,
     pooled,
+    area,
     gw,
+    awe,
+    wt,
     mixed_sum,
     fp,
     sp,
@@ -379,7 +381,8 @@
     acc1[...] = jnp.zeros_like(acc1)
 
     def first_sums(i, c):
-        count, height = counts[i], heights[i]
+        count, height = counts[i], 12 + 2 * group[i]
+        area[pl.ds(i, 1)] = jnp.full((1, mid), 1, F32) * (height * height).astype(F32)
         rows = lax.broadcasted_iota(jnp.int32, (slots, cols, 128), 0)
         columns = lax.broadcasted_iota(jnp.int32, (slots, cols, 128), 1)
         m = jnp.where((rows < count) & (columns < height), 1.0, 0.0).astype(F32)
@@ -393,7 +396,7 @@
         bottom[i] = fp[i, jnp.maximum(count - 1, 0)]
         return c
 
-    lax.fori_loop(0, images, first_sums, 0)
+    lax.fori_loop(0, images, first_sums, 0, unroll=2)
     out_mk = pltpu.make_async_copy(mk, mk_hbm, osem.at[1])
     out_mk.start()
     pending.append(out_mk)
@@ -534,13 +537,16 @@
 
         lax.fori_loop(0, GROUP, spread, 0)
         for g in range(2):
-            value = None
-            for dy in range(3):
-                lhs = a3[slot, :, dy : dy + slots, :, g * 3 * half : (g + 1) * 3 * half]
-                part = mm(
-                    lhs.reshape(GROUP * cells, 3 * half), ws[dy, :, g * mid : (g + 1) * mid]
-                )
-                value = part if value is None else value + part
+            taps = jnp.concatenate(
+                [
+                    a3[slot, :, dy : dy + slots, :, g * 3 * half : (g + 1) * 3 * half].reshape(
+                        GROUP * cells, 3 * half
+                    )
+                    for dy in range(3)
+                ],
+                axis=1,
+            )
+            value = mm(taps, ws[:, :, g * mid : (g + 1) * mid].reshape(9 * half, mid))
             sp[pl.ds(b * GROUP, GROUP), :, :, g * mid : (g + 1) * mid] = value.reshape(
                 GROUP, slots, cols, mid
             )
@@ -563,10 +569,13 @@
             acc2[1, :, lanes] += fold(w * v)
         return c
 
-    lax.fori_loop(0, images, second_sums, 0)
+    lax.fori_loop(0, images, second_sums, 0, unroll=2)
     buf2[me, 0:1] = row_sum(acc2[0])
     buf2[me, 1:2] = row_sum(acc2[1])
     links.all_start(buf2, sem2)
+    for g in range(2):
+        for dy in range(3):
+            wt[g, dy * mid : (dy + 1) * mid] = jnp.transpose(ws[dy, :, g * mid : (g + 1) * mid])
     total = links.all_wait(buf2, sem2)
     mean, factor, scale, offset = norm_terms(total[0:1], total[1:2], n, g2[...], h2[...])
     v2[0:1] = mean
@@ -588,7 +597,7 @@
         pooled[pl.ds(i, 1)] = row_sum(both)
         return c
 
-    lax.fori_loop(0, images, second_act, 0)
+    lax.fori_loop(0, images, second_act, 0, unroll=2)
     pooled[...] = pooled[...] / area[...]
     rbuf3[r] = mm(pooled[...], down[...].astype(F32), HIGH)
     squeeze = links.row_total(rbuf3, rsem3)
@@ -646,7 +655,10 @@
     v3[1:2] = factor
     v3[2:3] = scale
     v3[3:4] = offset
-    v3[4:8] = jnp.zeros((4, ch), F32)
+    v3[4:5] = 0.5 * scale
+    v3[5:6] = 0.5 * offset
+    v3[6:8] = jnp.zeros((2, ch), F32)
+    awe[...] = (wef * scale).astype(BF16)
 
     for copy in pending:
         copy.wait()
@@ -676,7 +688,10 @@
         (sd((images, mid)), VMEM),
         (sd((images, mid)), VMEM),
         (sd((images, mid)), VMEM),
+        (sd((images, mid)), VMEM),
         (sd((mid, ch)), VMEM),
+        (sd((mid, ch), BF16), VMEM),
+        (sd((2, 3 * mid, 3 * mid // 2), BF16), VMEM),
         (sd((mid, 128)), VMEM),
     ]
     dma = pltpu.SemaphoreType.DMA
@@ -727,62 +742,55 @@
     )(*args)
 
 
-def third_kernel(
-    counts, x, cot, mx, mk, we, awe, v3, bo, sg, q, m_out, tbuf
-):
-    step = pl.program_id(0)
+PART = 2
+
+
+def third_kernel(x, cot, mx, mk, we, awe, v3, bo, sg, q, m_out, *parts):
     per, slots, cols, ch = x.shape
     mid = mx.shape[-1]
-    cells = per * slots * cols
-    t = mm(mx[...].reshape(cells, mid), we[...])
-    tbuf[...] = t.reshape(tbuf.shape)
-
-    def image(k, c):
-        count = counts[step * per + k]
-        m = mk[k, 0]
-        m = wide(m, ch // 128)
-
-        def row(s, c):
-            zh = tbuf[k, s] * v3[0:1] + v3[1:2] + 0.5 * x[k, s].astype(F32)
-            th = jnp.tanh(zh)
-            up = 1.0 + th
-            act = zh * up
-            bo[k, s] = (act * m).astype(BF16)
-            slope = up + act * (1.0 - th)
-            sg[k, s] = (cot[k, s].astype(F32) * (0.5 * m) * slope).astype(BF16)
-            return c
-
-        def blank(s, c):
-            bo[k, s] = jnp.zeros((cols, ch), BF16)
-            sg[k, s] = jnp.zeros((cols, ch), BF16)
-            return c
-
-        lax.fori_loop(0, count, row, 0)
-        lax.fori_loop(count, slots, blank, 0)
-        return c
-
-    lax.fori_loop(0, per, image, 0)
-    s = sg[...].reshape(cells, ch)
-    q[...] = mm(s, awe[...]).reshape(q.shape)
-
-    @pl.when(step == 0)
+    cells = PART * slots * cols
+
+    @pl.when(pl.program_id(0) == 0)
     def _():
         m_out[...] = jnp.zeros_like(m_out)
 
-    m_out[0:mid] += mm_tn(mx[...].reshape(cells, mid), s)
-    m_out[mid : mid + 16] += mm(jnp.ones((16, cells), BF16), s)
-
-
-def call_third(counts, x, cot, mx, mk, we, awe, v3):
+    def product(p):
+        v = mx[p * PART : (p + 1) * PART].reshape(cells, mid)
+        parts[p][...] = mm(v, we[...])
+
+    product(0)
+    for p in range(per // PART):
+        if p + 1 < per // PART:
+            product(p + 1)
+        for k in range(PART):
+            i = p * PART + k
+            for s in range(slots):
+                m = wide(mk[i, s], ch // 128)
+                at = (k * slots + s) * cols
+                half = parts[p][at : at + cols] * v3[4:5] + v3[5:6] + 0.5 * x[i, s].astype(F32)
+                th = jnp.tanh(half)
+                up = 1.0 + th
+                act = half * up
+                bo[i, s] = (act * m).astype(BF16)
+                slope = up + act * (1.0 - th)
+                sg[i, s] = (cot[i, s].astype(F32) * (0.5 * m) * slope).astype(BF16)
+        v = sg[p * PART : (p + 1) * PART].reshape(cells, ch)
+        q[p * PART : (p + 1) * PART] = mm_nt(v, awe[...]).reshape(PART, slots, cols, mid)
+    v = sg[...].reshape(per * slots * cols, ch)
+    m_out[0:mid] += mm_tn(mx[...].reshape(per * slots * cols, mid), v)
+    m_out[mid : mid + 16] += mm(jnp.ones((16, per * slots * cols), BF16), v)
+
+
+def call_third(x, cot, mx, mk, we, awe, v3):
     images, slots, cols, ch = x.shape
     mid = mx.shape[-1]
-    per = 4
+    per = 8
 
     def cells(c):
-        return pl.BlockSpec((per, slots, cols, c), lambda b, *_: (b, 0, 0, 0))
+        return pl.BlockSpec((per, slots, cols, c), lambda b: (b, 0, 0, 0))
 
     def whole(a):
-        return pl.BlockSpec(a.shape, lambda b, *_: (0,) * a.ndim)
+        return pl.BlockSpec(a.shape, lambda b: (0,) * a.ndim)
 
     return pl.pallas_call(
         third_kernel,
@@ -792,21 +800,18 @@
             sd((images, slots, cols, mid)),
             sd((mid + 16, ch)),
         ],
-        grid_spec=pltpu.PrefetchScalarGridSpec(
-            num_scalar_prefetch=1,
-            grid=(images // per,),
-            in_specs=[cells(ch), cells(ch), cells(mid), cells(128), whole(we), whole(awe), whole(v3)],
-            out_specs=[
-                cells(ch),
-                cells(ch),
-                cells(mid),
-                pl.BlockSpec((mid + 16, ch), lambda b, *_: (0, 0)),
-            ],
-            scratch_shapes=[pltpu.VMEM((per, slots, cols, ch), F32)],
-        ),
+        grid=(images // per,),
+        in_specs=[cells(ch), cells(ch), cells(mid), cells(128), whole(we), whole(awe), whole(v3)],
+        out_specs=[
+            cells(ch),
+            cells(ch),
+            cells(mid),
+            pl.BlockSpec((mid + 16, ch), lambda b: (0, 0)),
+        ],
+        scratch_shapes=[pltpu.VMEM((PART * slots * cols, ch), F32)] * (per // PART),
         name="third",
-        compiler_params=pltpu.CompilerParams(vmem_limit_bytes=48 * 1024 * 1024),
-    )(counts, x, cot, mx, mk, we, awe, v3)
+        compiler_params=pltpu.CompilerParams(vmem_limit_bytes=60 * 1024 * 1024),
+    )(x, cot, mx, mk, we, awe, v3)
 
 
 def backward_kernel(
@@ -836,7 +841,7 @@
     m_in,
     area,
     g_at,
-    ws,
+    wt,
     down,
     up,
     we,
@@ -847,19 +852,18 @@
     reduce_out,
     up_out,
     down_out,
+    bias_out,
     b1,
     b2,
     b3,
     b_at,
     mg,
-    sp,
     pd,
     mx,
     mk,
     split_part,
     small_part,
     rows_all,
-    geb,
     edge,
     ret,
     acc1,
@@ -875,7 +879,6 @@
     buf8,
     lsem,
     a3sem,
-    xsem,
     hsem,
     rsem5,
     isem5,
@@ -901,98 +904,8 @@
         Reducer(links, rows, width, reducers[k * count : (k + 1) * count])
         for k, (rows, width, _) in enumerate(sizes)
     ]
-    loads = [
-        pltpu.make_async_copy(src, dst, lsem.at[k])
-        for k, (src, dst) in enumerate(
-            [(mx_hbm, mx), (q_hbm, mg), (pd_hbm, pd), (mk_hbm, mk), (sp_hbm, sp)]
-        )
-    ]
-    for load in loads:
-        load.start()
-    pending = list(loads)
-
     n = v1[4:5, 0:1]
-    mean3, factor3, scale3 = v3[0:1], v3[1:2], v3[2:3]
-    wef = we[...].astype(F32)
-    rbuf5[r, 0:1] = m_in[mid : mid + 1]
-    rbuf5[r, 1:2] = factor3 * (row_sum(m_in[0:mid] * wef) - mean3 * m_in[mid : mid + 1])
-    links.met()
-    ibuf5[links.i] = links.row_total(rbuf5, rsem5)
-    total = links.img_total(ibuf5, isem5)
-    b3[...] = total
-    slope3, offset3 = norm_back_terms(mean3, factor3, scale3, n, total[0:1], total[1:2])
-    slope = factor3 * (total[1:2] / n)
-    mb[...] = mm_terms(mm, wef * slope, awe[...], 2)
-    level = total[0:1] / n - slope * mean3
-    ev = mm_terms(mm, jnp.broadcast_to(level, (8, ch)), awe[...], 3)[0:1]
-
-    def expand_piece(p):
-        rows = pl.ds(pl.multiple_of(p * (mid // n_row), mid // n_row), mid // n_row)
-        return (
-            m_in[rows] * scale3 - wide(mixed_sum[rows], ch // 128) * offset3 - gw[rows] * slope3
-        )
-
-    expand_red.begin(expand_piece)
-
-    for load in loads[:4]:
-        load.wait()
-    del pending[:4]
-
-    def mix_back(b, c):
-        v = mx[pl.ds(b * GROUP, GROUP)].reshape(GROUP * cells, mid)
-        high = mb[...].astype(BF16)
-        fix = mm(v, high) + mm(v, (mb[...] - high.astype(F32)).astype(BF16))
-        mg[pl.ds(b * GROUP, GROUP)] -= fix.reshape(GROUP, slots, cols, mid)
-
-        def one(k, c):
-            i = b * GROUP + k
-            m = wide(mk[i].reshape(cells, 128), mid // 128)
-            v = mg[i].reshape(cells, mid) - m * ev
-            mg[i] = v.reshape(slots, cols, mid)
-            d = pd[i].reshape(cells, mid).astype(F32)
-            dpart[pl.ds(i, 1)] = row_sum(fold(v * d))
-            return c
-
-        lax.fori_loop(0, GROUP, one, 0)
-        return c
-
-    lax.fori_loop(0, blocks, mix_back, 0)
-
-    expand_red.second(expand_piece)
-    upf = up[...].astype(F32)
-    lean = dpart[...] * w0[...] * w1[...]
-    rbuf6[r] = mm_nt(lean, upf[:, :mid] - upf[:, mid:], HIGH)
-    z = at_out[...]
-    attend = z * sigmoid(z)
-    up_part = mm_tn(attend, lean, HIGH)
-    buf7[me, 2:3] = wide(row_sum(lean), 2)
-    attend_grad = links.row_total(rbuf6, rsem6) * swish_slope(z)
-    ibuf6[links.i, 0:1] = row_sum(attend_grad)
-    ibuf6[links.i, 1:2] = row_sum(attend_grad * at_norm[...])
-    total = links.img_total(ibuf6, isem6)
-    b_at[...] = total
-    count = float(images * n_img)
-    squeeze_grad = (
-        g_at[...]
-        * v_at[0:1]
-        * (attend_grad - total[0:1] / count - at_norm[...] * (total[1:2] / count))
-    )
-    down_part = mm_tn(pooled[...], squeeze_grad, HIGH)
     up_rows, down_rows = inter // n_row, mid // n_row
-    for p in range(n_row):
-        lines = down_part[p * down_rows : (p + 1) * down_rows]
-        small_part[p, 0:up_rows] = up_part[p * up_rows : (p + 1) * up_rows]
-        small_part[p, up_rows:] = jnp.concatenate(
-            [lines[: down_rows // 2], lines[down_rows // 2 :]], axis=1
-        )
-
-    def small_piece(p):
-        return small_part[p]
-
-    expand_red.third()
-    small_red.begin(small_piece)
-    pgrad[...] = mm_nt(squeeze_grad, down[...].astype(F32), HIGH) / area[...]
-
     prev_dev = (links.i, lax.rem(r + n_row - 1, n_row))
     next_dev = (links.i, lax.rem(r + 1, n_row))
     has_prev = r > 0
@@ -1020,132 +933,223 @@
         right = jnp.where(col == 0, 0.0, pltpu.roll(t[:, 2 * half : 3 * half], 1, 0))
         return left + t[:, half : 2 * half] + right
 
-    def to_second_grads(ub, a3):
-        loads[4].wait()
-        del pending[0]
-        acc2[...] = jnp.zeros_like(acc2)
-
-        def second_back(i, c):
-            m = wide(mk[i].reshape(cells, 128), mid // 128)
-            v = mg[i].reshape(cells, mid)
-            for g, w in enumerate((w0, w1)):
-                lanes = slice(g * mid, (g + 1) * mid)
-                s = sp[i, :, :, lanes].reshape(cells, mid)
-                z = s * v2[2:3, lanes] + v2[3:4, lanes]
-                grad = (v * w[pl.ds(i, 1)] + pgrad[pl.ds(i, 1)]) * swish_slope(z) * m
-                ub[i, :, :, lanes] = grad.reshape(slots, cols, mid)
-                acc2[0, :, lanes] += fold(grad)
-                acc2[1, :, lanes] += fold(grad * s)
+    def small_piece(p):
+        return small_part[p]
+
+    def to_second_grads(sp):
+        loads = [
+            pltpu.make_async_copy(src, dst, lsem.at[k])
+            for k, (src, dst) in enumerate(
+                [(mx_hbm, mx), (q_hbm, mg), (pd_hbm, pd), (mk_hbm, mk), (sp_hbm, sp)]
+            )
+        ]
+        for load in loads:
+            load.start()
+        pending = list(loads)
+
+        mean3, factor3, scale3 = v3[0:1], v3[1:2], v3[2:3]
+        wef = we[...].astype(F32)
+        rbuf5[r, 0:1] = m_in[mid : mid + 1]
+        rbuf5[r, 1:2] = factor3 * (row_sum(m_in[0:mid] * wef) - mean3 * m_in[mid : mid + 1])
+        links.met()
+        ibuf5[links.i] = links.row_total(rbuf5, rsem5)
+        total = links.img_total(ibuf5, isem5)
+        b3[...] = total
+        slope3, offset3 = norm_back_terms(mean3, factor3, scale3, n, total[0:1], total[1:2])
+        slope = factor3 * (total[1:2] / n)
+        mb[...] = mm_terms(mm_nt, wef * slope, awe[...], 2)
+        level = total[0:1] / n - slope * mean3
+        ev = mm_terms(mm_nt, jnp.broadcast_to(level, (8, ch)), awe[...], 3)[0:1]
+
+        def expand_piece(p):
+            rows = pl.ds(pl.multiple_of(p * (mid // n_row), mid // n_row), mid // n_row)
+            return (
+                m_in[rows] * scale3 - wide(mixed_sum[rows], ch // 128) * offset3 - gw[rows] * slope3
+            )
+
+        expand_red.begin(expand_piece)
+
+        for load in loads[:4]:
+            load.wait()
+        del pending[:4]
+
+        def mix_back(b, c):
+            v = mx[pl.ds(b * GROUP, GROUP)].reshape(GROUP * cells, mid)
+            high = mb[...].astype(BF16)
+            fix = mm(v, high) + mm(v, (mb[...] - high.astype(F32)).astype(BF16))
+            mg[pl.ds(b * GROUP, GROUP)] -= fix.reshape(GROUP, slots, cols, mid)
+
+            def one(k, c):
+                i = b * GROUP + k
+                m = wide(mk[i].reshape(cells, 128), mid // 128)
+                v = mg[i].reshape(cells, mid) - m * ev
+                mg[i] = v.reshape(slots, cols, mid)
+                d = pd[i].reshape(cells, mid).astype(F32)
+                dpart[pl.ds(i, 1)] = row_sum(fold(v * d))
+                return c
+
+            lax.fori_loop(0, GROUP, one, 0)
             return c
 
-        lax.fori_loop(0, images, second_back, 0)
-        expand_red.fourth()
-        small_red.second(small_piece)
-        mean2, factor2, scale2 = v2[0:1], v2[1:2], v2[2:3]
-        s0 = row_sum(acc2[0])
-        buf7[me, 0:1] = s0
-        buf7[me, 1:2] = factor2 * (row_sum(acc2[1]) - mean2 * s0)
-        links.all_start(buf7, sem7)
-        total = links.all_wait(buf7, sem7)
-        b2[...] = total
-        slope2, offset2 = norm_back_terms(mean2, factor2, scale2, n, total[0:1], total[1:2])
-        expand_out[...] = expand_red.end()
-        small_red.third()
-
-        def second_grad(grad, s, m):
-            return (grad * scale2 - m * (offset2 + slope2 * s)).astype(BF16)
-
-        for side, dy in ((0, 0), (1, 2)):
-
-            def edge_rows(b, c):
+        lax.fori_loop(0, blocks, mix_back, 0)
+
+        expand_red.second(expand_piece)
+        upf = up[...].astype(F32)
+        lean = dpart[...] * w0[...] * w1[...]
+        rbuf6[r] = mm_nt(lean, upf[:, :mid] - upf[:, mid:], HIGH)
+        z = at_out[...]
+        attend = z * sigmoid(z)
+        up_part = mm_tn(attend, lean, HIGH)
+        bias_part = row_sum(lean)
+        attend_grad = links.row_total(rbuf6, rsem6) * swish_slope(z)
+        ibuf6[links.i, 0:1] = row_sum(attend_grad)
+        ibuf6[links.i, 1:2] = row_sum(attend_grad * at_norm[...])
+        total = links.img_total(ibuf6, isem6)
+        b_at[...] = total
+        count = float(images * n_img)
+        squeeze_grad = (
+            g_at[...]
+            * v_at[0:1]
+            * (attend_grad - total[0:1] / count - at_norm[...] * (total[1:2] / count))
+        )
+        down_part = mm_tn(pooled[...], squeeze_grad, HIGH)
+        for p in range(n_row):
+            lines = down_part[p * down_rows : (p + 1) * down_rows]
+            small_part[p, 0:up_rows] = up_part[p * up_rows : (p + 1) * up_rows]
+            small_part[p, up_rows : up_rows + down_rows // 2] = jnp.concatenate(
+                [lines[: down_rows // 2], lines[down_rows // 2 :]], axis=1
+            )
+            small_part[p, up_rows + down_rows // 2 :] = jnp.broadcast_to(bias_part, (8, mid))
+
+        expand_red.third()
+        small_red.begin(small_piece)
+        pgrad[...] = mm_nt(squeeze_grad, down[...].astype(F32), HIGH) / area[...]
+
+        def with_second_grads(ub, a3, geb):
+            loads[4].wait()
+            del pending[0]
+            acc2[...] = jnp.zeros_like(acc2)
+
+            def second_back(i, c):
+                m = wide(mk[i].reshape(cells, 128), mid // 128)
+                v = mg[i].reshape(cells, mid)
+                for g, w in enumerate((w0, w1)):
+                    lanes = slice(g * mid, (g + 1) * mid)
+                    s = sp[i, :, :, lanes].reshape(cells, mid)
+                    z = s * v2[2:3, lanes] + v2[3:4, lanes]
+                    grad = (v * w[pl.ds(i, 1)] + pgrad[pl.ds(i, 1)]) * swish_slope(z) * m
+                    ub[i, :, :, lanes] = grad.reshape(slots, cols, mid)
+                    acc2[0, :, lanes] += fold(grad)
+                    acc2[1, :, lanes] += fold(grad * s)
+                return c
+
+            lax.fori_loop(0, images, second_back, 0, unroll=2)
+            expand_red.fourth()
+            small_red.second(small_piece)
+            mean2, factor2, scale2 = v2[0:1], v2[1:2], v2[2:3]
+            s0 = row_sum(acc2[0])
+            buf7[me, 0:1] = s0
+            buf7[me, 1:2] = factor2 * (row_sum(acc2[1]) - mean2 * s0)
+            links.all_start(buf7, sem7)
+            total = links.all_wait(buf7, sem7)
+            b2[...] = total
+            slope2, offset2 = norm_back_terms(mean2, factor2, scale2, n, total[0:1], total[1:2])
+            expand_out[...] = expand_red.end()
+            small_red.third()
+
+            def second_grad(grad, s, m):
+                return (grad * scale2 - m * (offset2 + slope2 * s)).astype(BF16)
+
+            for side, dy in ((0, 0), (1, 2)):
+
+                def edge_rows(i, c):
+                    at = 0 if side == 0 else jnp.maximum(counts[i] - 1, 0)
+                    m = wide(mk[i, 0], 2 * mid // 128)
+                    geb[i] = second_grad(ub[i, at], sp[i, at], m)
+                    return c
+
+                lax.fori_loop(0, images, edge_rows, 0, unroll=2)
+                for g in range(2):
+                    v = geb[:, :, g * mid : (g + 1) * mid].reshape(images * cols, mid)
+                    t = mm(v, wt[g, dy * mid : (dy + 1) * mid])
+                    edge[side, :, :, g * half : (g + 1) * half] = (
+                        columns_back(t, images * cols).astype(BF16).reshape(images, cols, half)
+                    )
+                if side == 0:
+
+                    @pl.when(has_prev)
+                    def _():
+                        to_prev.start()
+
+                else:
+
+                    @pl.when(has_next)
+                    def _():
+                        to_next.start()
+
+            @pl.when(jnp.logical_not(has_prev))
+            def _():
+                ret[0] = jnp.zeros(ret.shape[1:], BF16)
+
+            @pl.when(jnp.logical_not(has_next))
+            def _():
+                ret[1] = jnp.zeros(ret.shape[1:], BF16)
+
+            def a3_copy(b, slot):
+                return pltpu.make_async_copy(
+                    a3_hbm.at[pl.ds(b * GROUP, GROUP)], a3.at[slot], a3sem.at[slot]
+                )
+
+            a3_copy(0, 0).start()
+            split_part[...] = jnp.zeros_like(split_part)
+
+            def split_grads(b, c):
+                slot = lax.rem(b, 2)
+
+                @pl.when(b + 1 < blocks)
+                def _():
+                    a3_copy(b + 1, 1 - slot).start()
+
                 def one(k, c):
                     i = b * GROUP + k
-                    at = 0 if side == 0 else jnp.maximum(counts[i] - 1, 0)
-                    m = wide(mk[i, 0], 2 * mid // 128)
-                    geb[k] = second_grad(ub[i, at], sp[i, at], m)
+                    m = wide(mk[i].reshape(cells, 128), 2 * mid // 128)
+                    v = second_grad(ub[i].reshape(cells, 2 * mid), sp[i].reshape(cells, 2 * mid), m)
+                    mx[i] = v[:, 0:mid].reshape(slots, cols, mid)
+                    pd[i] = v[:, mid:].reshape(slots, cols, mid)
                     return c
 
                 lax.fori_loop(0, GROUP, one, 0)
-                for g in range(2):
-                    v = geb[:, :, g * mid : (g + 1) * mid].reshape(GROUP * cols, mid)
-                    t = mm_nt(v, ws[dy, :, g * mid : (g + 1) * mid])
-                    edge[side, pl.ds(b * GROUP, GROUP), :, g * half : (g + 1) * half] = (
-                        columns_back(t, GROUP * cols).astype(BF16).reshape(GROUP, cols, half)
+                a3_copy(b, slot).wait()
+                for g, grads in enumerate((mx, pd)):
+                    v = grads[pl.ds(b * GROUP, GROUP)].reshape(GROUP * cells, mid)
+                    taps = jnp.concatenate(
+                        [
+                            a3[slot, :, dy : dy + slots, :, g * 3 * half : (g + 1) * 3 * half].reshape(
+                                GROUP * cells, 3 * half
+                            )
+                            for dy in range(3)
+                        ],
+                        axis=1,
                     )
+                    split_part[g] += mm_tn(v, taps)
                 return c
 
-            lax.fori_loop(0, blocks, edge_rows, 0)
-            if side == 0:
-
-                @pl.when(has_prev)
-                def _():
-                    to_prev.start()
-
-            else:
-
-                @pl.when(has_next)
-                def _():
-                    to_next.start()
-
-        @pl.when(jnp.logical_not(has_prev))
-        def _():
-            ret[0] = jnp.zeros(ret.shape[1:], BF16)
-
-        @pl.when(jnp.logical_not(has_next))
-        def _():
-            ret[1] = jnp.zeros(ret.shape[1:], BF16)
-
-        def a3_copy(b, slot):
-            return pltpu.make_async_copy(
-                a3_hbm.at[pl.ds(b * GROUP, GROUP)], a3.at[slot], a3sem.at[slot]
-            )
-
-        a3_copy(0, 0).start()
-        split_part[...] = jnp.zeros_like(split_part)
-
-        def split_grads(b, c):
-            slot = lax.rem(b, 2)
-
-            @pl.when(b + 1 < blocks)
-            def _():
-                a3_copy(b + 1, 1 - slot).start()
-
-            def one(k, c):
-                i = b * GROUP + k
-                m = wide(mk[i].reshape(cells, 128), 2 * mid // 128)
-                v = second_grad(ub[i].reshape(cells, 2 * mid), sp[i].reshape(cells, 2 * mid), m)
-                mx[i] = v[:, 0:mid].reshape(slots, cols, mid)
-                pd[i] = v[:, mid:].reshape(slots, cols, mid)
-                return c
-
-            lax.fori_loop(0, GROUP, one, 0)
-            a3_copy(b, slot).wait()
-            for g, grads in enumerate((mx, pd)):
-                v = grads[pl.ds(b * GROUP, GROUP)].reshape(GROUP * cells, mid)
-                taps = jnp.concatenate(
-                    [
-                        a3[slot, :, dy : dy + slots, :, g * 3 * half : (g + 1) * 3 * half].reshape(
-                            GROUP * cells, 3 * half
-                        )
-                        for dy in range(3)
-                    ],
-                    axis=1,
-                )
-                split_part[g] += mm_tn(v, taps)
-            return c
-
-        lax.fori_loop(0, blocks, split_grads, 0)
-
-    pl.run_scoped(
-        to_second_grads,
-        pltpu.VMEM((images, slots, cols, 2 * mid), F32),
-        pltpu.VMEM((2, GROUP, slots + 2, cols, 3 * mid), BF16),
-    )
-
-    def to_inputs(fp, xbuf, xt, xu, split_rows):
+            lax.fori_loop(0, blocks, split_grads, 0)
+
+        pl.run_scoped(
+            with_second_grads,
+            pltpu.VMEM((images, slots, cols, 2 * mid), F32),
+            pltpu.VMEM((2, GROUP, slots + 2, cols, 3 * mid), BF16),
+            pltpu.VMEM((images, cols, 2 * mid), BF16),
+        )
+
+    pl.run_scoped(to_second_grads, pltpu.VMEM((images, slots, cols, 2 * mid), F32))
+
+    def to_inputs(fp, xs, xt, xu, split_rows):
         loads = [
             pltpu.make_async_copy(fp_hbm, fp, lsem.at[5]),
             pltpu.make_async_copy(xt_hbm, xt, lsem.at[6]),
+            pltpu.make_async_copy(x_hbm, xs, lsem.at[4]),
         ]
         for load in loads:
             load.start()
@@ -1156,12 +1160,12 @@
             for tap in range(9):
                 at = pl.multiple_of(tap * half + p * (half // n_row), half // n_row)
                 lines.append(split_rows[pl.ds(at, half // n_row)])
-            return jnp.concatenate(lines, axis=0)
+            return jnp.concatenate(lines, axis=0).astype(F32)
 
         for g in range(2):
             for tap in range(9):
                 split_rows[tap * half : (tap + 1) * half, g * mid : (g + 1) * mid] = jnp.transpose(
-                    split_part[g, :, tap * half : (tap + 1) * half]
+                    split_part[g, :, tap * half : (tap + 1) * half].astype(BF16)
                 )
         split_red.begin(split_piece)
 
@@ -1170,23 +1174,22 @@
             def _():
                 split_red.second(split_piece)
 
-            @pl.when(b == 4)
+            @pl.when(b == 5)
             def _():
                 split_red.third()
 
             blank = jnp.zeros((GROUP, 1, cols, mid), BF16)
             for g, grads in enumerate((mx, pd)):
-                lanes = slice(g * mid, (g + 1) * mid)
                 v = grads[pl.ds(b * GROUP, GROUP)]
                 moved = (
                     jnp.concatenate([v[:, 1:], blank], axis=1),
                     v,
                     jnp.concatenate([blank, v[:, : slots - 1]], axis=1),
                 )
-                value = None
-                for dy in range(3):
-                    part = mm_nt(moved[dy].reshape(GROUP * cells, mid), ws[dy, :, lanes])
-                    value = part if value is None else value + part
+                v = jnp.concatenate(
+                    [moved[dy].reshape(GROUP * cells, mid) for dy in range(3)], axis=1
+                )
+                value = mm(v, wt[g])
                 mg[pl.ds(b * GROUP, GROUP), :, :, g * half : (g + 1) * half] = columns_back(
                     value, GROUP * cells
                 ).reshape(GROUP, slots, cols, half)
@@ -1224,52 +1227,40 @@
             z = v * v1[2:3] + v1[3:4]
             grad = jnp.concatenate(parts, axis=0) * swish_slope(z) * m
             mg[i] = grad.reshape(slots, cols, mid)
+            pd[i] = grad.astype(BF16).reshape(slots, cols, mid)
             acc1[0] += fold(grad)
             acc1[1] += fold(grad * v)
             return c
 
-        lax.fori_loop(0, images, first_back, 0)
+        lax.fori_loop(0, images, first_back, 0, unroll=2)
         s0 = row_sum(acc1[0])
         buf8[me, 0:1] = s0
         buf8[me, 1:2] = v1[1:2] * (row_sum(acc1[1]) - v1[0:1] * s0)
         links.all_start(buf8, sem8)
-        split_red.fourth()
-
-        def x_copy(b, slot):
-            return pltpu.make_async_copy(
-                x_hbm.at[pl.ds(b * GROUP, GROUP)], xbuf.at[slot], xsem.at[slot]
+        loads[2].wait()
+        lines = images * cells
+        width = ch // 2
+        for k in range(2):
+            xu[:, k * width : (k + 1) * width] = mm_tn(
+                pd[...].reshape(lines, mid), xs[:, :, :, k * width : (k + 1) * width].reshape(lines, width)
             )
-
-        x_copy(0, 0).start()
-        xu[...] = jnp.zeros_like(xu)
-
-        def against_input(b, c):
-            slot = lax.rem(b, 2)
-
-            @pl.when(b + 1 < blocks)
-            def _():
-                x_copy(b + 1, 1 - slot).start()
-
-            v = mg[pl.ds(b * GROUP, GROUP)].reshape(GROUP * cells, mid).astype(BF16)
-            x_copy(b, slot).wait()
-            xu[...] += mm_tn(v, xbuf[slot].reshape(GROUP * cells, ch))
-            return c
-
-        lax.fori_loop(0, blocks, against_input, 0)
         loads[1].wait()
         total = links.all_wait(buf8, sem8)
         b1[...] = total
         slope1, offset1 = norm_back_terms(v1[0:1], v1[1:2], v1[2:3], n, total[0:1], total[1:2])
 
+        def column(v):
+            return wide(jnp.transpose(jnp.broadcast_to(v, (128, mid))), ch // n_row // 128)
+
+        scale_c, slope_c, offset_c = column(v1[2:3]), column(slope1), column(offset1)
+
         def reduce_piece(p):
             lanes = pl.ds(pl.multiple_of(p * (ch // n_row), ch // n_row), ch // n_row)
-            return (
-                jnp.transpose(xu[:, lanes]) * v1[2:3]
-                - jnp.transpose(xt[mid : mid + 128, lanes])[:, 0:1] * offset1
-                - jnp.transpose(xt[0:mid, lanes]) * slope1
-            )
+            v = xu[:, lanes] * scale_c - xt[mid : mid + 1, lanes] * offset_c - xt[0:mid, lanes] * slope_c
+            return jnp.transpose(v.astype(BF16)).astype(F32)
 
         reduce_red.begin(reduce_piece)
+        split_red.fourth()
 
         def first_grad(i, c):
             m = wide(mk[i].reshape(cells, 128), mid // 128)
@@ -1290,10 +1281,11 @@
             copy.wait()
         for p in range(n_row):
             up_out[p * up_rows : (p + 1) * up_rows] = rows_all[p, 0:up_rows]
-            lines = rows_all[p, up_rows:]
+            lines = rows_all[p, up_rows : up_rows + down_rows // 2]
             down_out[p * down_rows : (p + 1) * down_rows] = jnp.concatenate(
                 [lines[:, 0:inter], lines[:, inter:]], axis=0
             )
+        bias_out[...] = rows_all[0, up_rows + down_rows // 2 :]
         reduce_red.fourth()
         reduce_out[...] = reduce_red.end()
         out_fg.wait()
@@ -1301,10 +1293,10 @@
     pl.run_scoped(
         to_inputs,
         pltpu.VMEM((images, slots, cols, mid), F32),
-        pltpu.VMEM((2, GROUP, slots, cols, ch), BF16),
+        pltpu.VMEM((images, slots, cols, ch), BF16),
         pltpu.VMEM((mid + 128, ch), F32),
         pltpu.VMEM((mid, ch), F32),
-        pltpu.VMEM((9 * half, 2 * mid), F32),
+        pltpu.VMEM((9 * half, 2 * mid), BF16),
     )
 
 
@@ -1313,7 +1305,7 @@
         (mid // n_row, ch, BF16),
         (9 * (mid // 2) // n_row, 2 * mid, BF16),
         (ch // n_row, mid, BF16),
-        (inter // n_row + mid // n_row // 2, mid, F32),
+        (inter // n_row + mid // n_row // 2 + 8, mid, F32),
     ]
 
 
@@ -1331,22 +1323,21 @@
         (sd((ch // n_row, mid)), VMEM),
         (sd((inter, mid)), VMEM),
         (sd((mid, inter)), VMEM),
+        (sd((8, mid)), VMEM),
         (sd((2, mid)), VMEM),
-        (sd((3, 2 * mid)), VMEM),
+        (sd((2, 2 * mid)), VMEM),
         (sd((2, ch)), VMEM),
         (sd((2, inter)), VMEM),
     ]
     dma = pltpu.SemaphoreType.DMA
     scratch = [
         pltpu.VMEM(cells + (mid,), F32),
-        pltpu.VMEM(cells + (2 * mid,), F32),
         pltpu.VMEM(cells + (mid,), BF16),
         pltpu.VMEM(cells + (mid,), BF16),
         pltpu.VMEM(cells + (128,), F32),
         pltpu.VMEM((2, mid, 9 * half), F32),
         pltpu.VMEM((n_row, sizes[3][0], mid), F32),
         pltpu.VMEM((n_row, sizes[3][0], mid), F32),
-        pltpu.VMEM((GROUP, cols, 2 * mid), BF16),
         pltpu.VMEM((2, images, cols, mid), BF16),
         pltpu.VMEM((2, images, cols, mid), BF16),
         pltpu.VMEM((2, 8, mid), F32),
@@ -1358,10 +1349,9 @@
         pltpu.VMEM((n_row, 2, ch), F32),
         pltpu.VMEM((n_row, images, inter), F32),
         pltpu.VMEM((n_img, 2, inter), F32),
-        pltpu.VMEM((n, 3, 2 * mid), F32),
+        pltpu.VMEM((n, 2, 2 * mid), F32),
         pltpu.VMEM((n, 2, mid), F32),
         dma((8,)),
-        dma((2,)),
         dma((2,)),
         dma((4,)),
         dma((2, n_row)),
@@ -1388,29 +1378,56 @@
     )(*args)
 
 
-def input_kernel(fg, sg, wr, gi):
+def input_kernel(
+    fg, sg, wr, expand, split, reduce, up, down, bias, b1, b2, b3, b_at,
+    gi, expand_out, split_out, reduce_out, up_out, down_out, bias_out, *lines,
+):
     per, slots, cols, ch = sg.shape
     cells = per * slots * cols
-    value = mm_nt(fg[...].reshape(cells, fg.shape[-1]), wr[...])
+    mid = fg.shape[-1]
+    value = mm_nt(fg[...].reshape(cells, mid), wr[...])
     gi[...] = (value + sg[...].reshape(cells, ch).astype(F32)).astype(BF16).reshape(gi.shape)
 
-
-def call_input(fg, sg, wr):
+    @pl.when(pl.program_id(0) == 0)
+    def _():
+        expand_out[...] = expand[...]
+        split_out[...] = split[...]
+        reduce_out[...] = reduce[...]
+        down_out[...] = down[...]
+        up_out[:, 0:mid] = up[...]
+        up_out[:, mid:] = -up[...]
+        bias_out[:, 0:mid] = bias[0:1]
+        bias_out[:, mid:] = -bias[0:1]
+        for k, v in enumerate((b1, b2, b_at, b3)):
+            lines[2 * k][...] = v[1:2]
+            lines[2 * k + 1][...] = v[0:1]
+
+
+def call_input(fg, sg, wr, *small):
     images, slots, cols, ch = sg.shape
-    per = 4
+    mid = fg.shape[-1]
+    expand, split, reduce, up, down, _, b1, b2, b3, b_at = small
+    per = 14
 
     def cells(c):
         return pl.BlockSpec((per, slots, cols, c), lambda b: (b, 0, 0, 0))
 
+    def whole(a):
+        return pl.BlockSpec(a.shape, lambda b: (0,) * len(a.shape))
+
+    outs = [sd(a.shape) for a in (expand, split, reduce)]
+    outs += [sd((up.shape[0], 2 * mid)), sd(down.shape), sd((1, 2 * mid))]
+    for v in (b1, b2, b_at, b3):
+        outs += [sd((1, v.shape[1]))] * 2
     return pl.pallas_call(
         input_kernel,
-        out_shape=sd(sg.shape, BF16),
+        out_shape=[sd(sg.shape, BF16)] + outs,
         grid=(images // per,),
-        in_specs=[cells(fg.shape[-1]), cells(ch), pl.BlockSpec(wr.shape, lambda b: (0, 0))],
-        out_specs=cells(ch),
+        in_specs=[cells(mid), cells(ch), whole(wr)] + [whole(a) for a in small],
+        out_specs=[cells(ch)] + [whole(a) for a in outs],
         name="input_grad",
-        compiler_params=pltpu.CompilerParams(vmem_limit_bytes=48 * 1024 * 1024),
-    )(fg, sg, wr)
+        compiler_params=pltpu.CompilerParams(vmem_limit_bytes=60 * 1024 * 1024),
+    )(fg, sg, wr, *small)
 
 
 def body(
@@ -1440,23 +1457,21 @@
     inter = attn_down.shape[1]
     half = mid // 2
     counts = row_counts[:, 0]
-    heights = 12 + 2 * image_group
-    area = jnp.broadcast_to((heights * heights).astype(F32)[:, None], (images, mid))
     ws = split_weight.reshape(3, 3 * half, 2 * mid)
 
     def line(v):
         return v[None, :]
 
     (
-        fp, a3, sp, pd, mx, mk, xt, v1, v2, v3, v_at, at_norm, at_out, w0, w1, pooled, gw, mixed_sum,
+        fp, a3, sp, pd, mx, mk, xt, v1, v2, v3, v_at, at_norm, at_out, w0, w1, pooled, area,
+        gw, awe, wt, mixed_sum,
     ) = call_forward(
         n_img,
         n_row,
         (
             counts,
-            heights,
+            image_group,
             feature_map,
-            area,
             reduce_weight,
             line(gain_first),
             line(shift_first),
@@ -1474,44 +1489,35 @@
         ),
         images, slots, cols, ch, mid, inter,
     )
-    awe = (expand_weight.astype(F32) * v3[2:3]).astype(BF16).T
-    half_terms = jnp.concatenate([0.5 * v3[2:4], jnp.zeros((6, ch), F32)], axis=0)
     block_out, sg, q, m_sum = call_third(
-        counts, feature_map, cotangent, mx, mk, expand_weight, awe, half_terms
+        feature_map, cotangent, mx, mk, expand_weight, awe, v3
     )
     (
-        fg, grad_expand, grad_split, grad_reduce, grad_up, grad_down, b1, b2, b3, b_at,
+        fg, grad_expand, grad_split, grad_reduce, grad_up, grad_down, bias, b1, b2, b3, b_at,
     ) = call_backward(
         n_img,
         n_row,
         (
             counts, q, fp, a3, sp, pd, mx, mk, xt, feature_map, v1, v2, v3, v_at, at_norm, at_out, w0, w1, pooled,
-            gw, mixed_sum, m_sum, area, line(gain_attend), ws, attn_down, attn_up, expand_weight,
+            gw, mixed_sum, m_sum, area, line(gain_attend), wt, attn_down, attn_up, expand_weight,
             awe,
         ),
         ch, inter,
     )
-    grad_input = call_input(fg, sg, reduce_weight)
-    grad_split = grad_split.reshape(3, 3, half // n_row, 2 * mid)
-    grad_bias = b2[2, 0:mid]
+    small = call_input(
+        fg, sg, reduce_weight, grad_expand, grad_split, grad_reduce, grad_up, grad_down, bias,
+        b1, b2, b3, b_at,
+    )
+    grad_input, grad_expand, grad_split, grad_reduce, grad_up, grad_down = small[:6]
     return (
         block_out,
         grad_input,
         grad_reduce,
-        grad_split,
+        grad_split.reshape(3, 3, half // n_row, 2 * mid),
         grad_expand,
         grad_down,
-        jnp.concatenate([grad_up, -grad_up], axis=1),
-        jnp.concatenate([grad_bias, -grad_bias]),
-        b1[1],
-        b1[0],
-        b2[1],
-        b2[0],
-        b_at[1],
-        b_at[0],
-        b3[1],
-        b3[0],
-    )
+        grad_up,
+    ) + tuple(v.reshape(-1) for v in small[6:])
 
 
 def solution(mesh):

time: 258 us -> 213 us (0.83)
  Pallas kernels: 241 us -> 212 us
  local copies, waits for them, and re-layouts: 12.5 us -> 0 us
  other arithmetic: 3.49 us -> 0 us
    pallas_call x1, Pallas kernels: 37.9 us -> 25.5 us  [call_third(): pl.pallas_call(third_kernel, out_shape=[sd(x.shape, BF16), sd(x.shape, BF...]
    pallas_call x1, Pallas kernels: 112 us -> 101 us  [call_backward(): pl.pallas_call(functools.partial(backward_kernel, n_img, n_row), out_shap...]
    unnamed x37 -> x0, local copies, waits for them, and re-layouts: 8.75 us -> none
    pallas_call x1, Pallas kernels: 15.3 us -> 11.6 us  [call_input(): pl.pallas_call(input_kernel, out_shape=[sd(sg.shape, BF16)] + outs, grid=...]
where the time goes in v3:
time: 213 us
  Pallas kernels  212 us (100%)
    pallas_call x1, Pallas kernels, call_backward(): pl.pallas_call(functools.partial(backward_kernel, n_img, n_row), out_shap...  101 us
    pallas_call x1, Pallas kernels, call_forward(): pl.pallas_call(functools.partial(forward_kernel, n_img, n_row), out_shape...  73.8 us
    pallas_call x1, Pallas kernels, call_third(): pl.pallas_call(third_kernel, out_shape=[sd(x.shape, BF16), sd(x.shape, BF...  25.5 us
    pallas_call x1, Pallas kernels, call_input(): pl.pallas_call(input_kernel, out_shape=[sd(sg.shape, BF16)] + outs, grid=...  11.6 us

profile of v3, /device:TPU:0, one launch (start us, length us, event | category | flops | bytes accessed | tf_op | source)
XLA Modules:
  0.0 212.9 jit_solution(558417322139038915)
XLA Ops:
  0.7 73.8 %forward.1 = (f32[56,6,16,256]{3,2,1,0:T(8,128)}, bf16[56,8,16,768]{3,2,1,0:T(8,128)(2,1)}, f32[56,6,16,512]{3,2,1,0:T(8,128)}, bf16[56,6,16,256]{3,2,1,0:T(8,12...) custom-call(s32[56]{0:T(128)} %bitcast.27, ...), custom_call_target="tpu_custom_call" | custom-call | tf_op jit(solution)/shard_map/forward/pallas_call | solution.py:732
  74.5 25.5 %third.1 = (bf16[56,6,16,1024]{3,2,1,0:T(8,128)(2,1)}, bf16[56,6,16,1024]{3,2,1,0:T(8,128)(2,1)}, f32[56,6,16,256]{3,2,1,0:T(8,128)}, f32[272,1024]{1,0:T(8,128)}) custom-call(bf16[56,6,16,1024]{3,2,1,0:T(8,128)(2,1)} %x_hbm.3, bf16[56,6,16,1024]{3,2,1,0:T(8,128)(2,1)} %cot.1, bf16[56,6,16,256]{3,2,1,0:T(8,128)(2,1)} %get-tuple-element.67.mx.mx_hbm, ...), custom_call_target="tpu_custom_call" | custom-call | tf_op jit(solution)/shard_map/third/pallas_call | solution.py:795
  100.0 101.1 %backward.1 = (bf16[56,6,16,256]{3,2,1,0:T(8,128)(2,1)}, f32[64,1024]{1,0:T(8,128)}, f32[288,512]{1,0:T(8,128)}, f32[256,256]{1,0:T(8,128)}, f32[128,256]{1,0:T(...) custom-call(s32[56]{0:T(128)} %bitcast.28, ...), custom_call_target="tpu_custom_call" | custom-call | tf_op jit(solution)/shard_map/backward/pallas_call | solution.py:1368
  201.1 11.6 %input_grad.1 = (bf16[56,6,16,1024]{3,2,1,0:T(8,128)(2,1)}, f32[64,1024]{1,0:T(8,128)}, f32[288,512]{1,0:T(8,128)}, f32[256,256]{1,0:T(8,128)}, f32[128,512]{1,0...) custom-call(bf16[56,6,16,256]{3,2,1,0:T(8,128)(2,1)} %get-tuple-elem, ...), custom_call_target="tpu_custom_call" | custom-call | tf_op jit(solution)/shard_map/input_grad/pallas_call | solution.py:1422

commit v4 on v3

--- a/solution.py
+++ b/solution.py
@@ -281,7 +281,7 @@
     wr,
     g1,
     h1,
-    ws,
+    ws_hbm,
     g2,
     h2,
     down,
@@ -289,7 +289,7 @@
     h_at,
     up,
     bias,
-    we,
+    we_hbm,
     g3,
     h3,
     fp_hbm,
@@ -309,9 +309,9 @@
     w1,
     pooled,
     area,
-    gw,
-    awe,
-    wt,
+    gw_hbm,
+    awe_hbm,
+    wt_hbm,
     mixed_sum,
     fp,
     sp,
@@ -320,8 +320,13 @@
     mx,
     mk,
     xt,
-    xbuf,
+    xs,
     a3,
+    a3b,
+    ws,
+    we,
+    awe,
+    wt,
     acc1,
     acc2,
     gram,
@@ -354,52 +359,58 @@
     r = links.r
     links.greet()
 
-    def x_copy(b, slot):
-        return pltpu.make_async_copy(
-            x_hbm.at[pl.ds(b * GROUP, GROUP)], xbuf.at[slot], xsem.at[slot]
-        )
-
-    x_copy(0, 0).start()
+    def x_copy(b):
+        at = pl.ds(b * GROUP, GROUP)
+        return pltpu.make_async_copy(x_hbm.at[at], xs.at[at], xsem.at[b])
+
+    def x_start(b, c):
+        x_copy(b).start()
+        return c
+
+    lax.fori_loop(0, blocks, x_start, 0)
     pending = []
+    in_ws = pltpu.make_async_copy(ws_hbm, ws, osem.at[6])
+    in_we = pltpu.make_async_copy(we_hbm, we, osem.at[7])
+    in_ws.start()
+    in_we.start()
+    pending += [in_ws, in_we]
+
+    def masks(i, c):
+        count, height = counts[i], 12 + 2 * group[i]
+        area[pl.ds(i, 1)] = jnp.full((1, mid), 1, F32) * (height * height).astype(F32)
+        rows = lax.broadcasted_iota(jnp.int32, (slots, cols, 128), 0)
+        columns = lax.broadcasted_iota(jnp.int32, (slots, cols, 128), 1)
+        mk[i] = jnp.where((rows < count) & (columns < height), 1.0, 0.0).astype(F32)
+        return c
+
+    lax.fori_loop(0, images, masks, 0)
+    out_mk = pltpu.make_async_copy(mk, mk_hbm, osem.at[1])
+    out_mk.start()
+    pending.append(out_mk)
+    acc1[...] = jnp.zeros_like(acc1)
+    lines = GROUP * cells
 
     def first(b, c):
-        slot = lax.rem(b, 2)
-
-        @pl.when(b + 1 < blocks)
-        def _():
-            x_copy(b + 1, 1 - slot).start()
-
-        x_copy(b, slot).wait()
-        pre = mm(xbuf[slot].reshape(GROUP * cells, ch), wr[...])
-        fp[pl.ds(b * GROUP, GROUP)] = pre.reshape(GROUP, slots, cols, mid)
+        x_copy(b).wait()
+        at = pl.ds(b * GROUP, GROUP)
+        v = mm(xs[at].reshape(lines, ch), wr[...])
+        fp[at] = v.reshape(GROUP, slots, cols, mid)
+        m = mk[at].reshape(lines, 128)
+        w = v * wide(m, mid // 128)
+        mx[at] = w.astype(BF16).reshape(GROUP, slots, cols, mid)
+        pd[at, :, :, 0:128] = mk[at].astype(BF16)
+        acc1[0] += fold(w)
+        acc1[1] += fold(w * v)
+        acc1[2, :, 0:128] += fold(m)
+        for k in range(GROUP):
+            i = b * GROUP + k
+            bottom[i] = fp[i, jnp.maximum(counts[i] - 1, 0)]
         return c
 
     lax.fori_loop(0, blocks, first, 0)
     out_fp = pltpu.make_async_copy(fp, fp_hbm, osem.at[0])
     out_fp.start()
     pending.append(out_fp)
-    acc1[...] = jnp.zeros_like(acc1)
-
-    def first_sums(i, c):
-        count, height = counts[i], 12 + 2 * group[i]
-        area[pl.ds(i, 1)] = jnp.full((1, mid), 1, F32) * (height * height).astype(F32)
-        rows = lax.broadcasted_iota(jnp.int32, (slots, cols, 128), 0)
-        columns = lax.broadcasted_iota(jnp.int32, (slots, cols, 128), 1)
-        m = jnp.where((rows < count) & (columns < height), 1.0, 0.0).astype(F32)
-        mk[i] = m
-        m = m.reshape(cells, 128)
-        v = fp[i].reshape(cells, mid)
-        w = v * wide(m, mid // 128)
-        acc1[0] += fold(w)
-        acc1[1] += fold(w * v)
-        acc1[2, :, 0:128] += fold(m)
-        bottom[i] = fp[i, jnp.maximum(count - 1, 0)]
-        return c
-
-    lax.fori_loop(0, images, first_sums, 0, unroll=2)
-    out_mk = pltpu.make_async_copy(mk, mk_hbm, osem.at[1])
-    out_mk.start()
-    pending.append(out_mk)
 
     me = links.all_me()
     buf1[me, 0:1] = row_sum(acc1[0])
@@ -448,24 +459,14 @@
     def _():
         below[...] = jnp.zeros_like(below)
 
-    x_copy(0, 0).start()
-    xt[...] = jnp.zeros_like(xt)
-
-    def against_input(b, c):
-        slot = lax.rem(b, 2)
-
-        @pl.when(b + 1 < blocks)
-        def _():
-            x_copy(b + 1, 1 - slot).start()
-
-        m = mk[pl.ds(b * GROUP, GROUP)].reshape(GROUP * cells, 128)
-        v = fp[pl.ds(b * GROUP, GROUP)].reshape(GROUP * cells, mid) * wide(m, mid // 128)
-        v = jnp.concatenate([v.astype(BF16), m.astype(BF16)], axis=1)
-        x_copy(b, slot).wait()
-        xt[...] += mm_tn(v, xbuf[slot].reshape(GROUP * cells, ch))
-        return c
-
-    lax.fori_loop(0, blocks, against_input, 0)
+    v = jnp.concatenate(
+        [mx[...].reshape(images * cells, mid), pd[:, :, :, 0:128].reshape(images * cells, 128)], axis=1
+    )
+    width = ch // 2
+    for k in range(2):
+        xt[:, k * width : (k + 1) * width] = mm_tn(
+            v, xs[:, :, :, k * width : (k + 1) * width].reshape(images * cells, width)
+        )[0 : mid + 8]
     out_xt = pltpu.make_async_copy(xt, xt_hbm, osem.at[5])
     out_xt.start()
     pending.append(out_xt)
@@ -495,19 +496,18 @@
     col_index = lax.rem(lax.broadcasted_iota(jnp.int32, (ext, mid), 0), cols)
     acc2[...] = jnp.zeros_like(acc2)
 
+    in_ws.wait()
+    in_we.wait()
+    del pending[:2]
+    buffers = (a3, a3b)
+
     def a3_copy(b, slot):
         return pltpu.make_async_copy(
-            a3.at[slot], a3_hbm.at[pl.ds(b * GROUP, GROUP)], a3sem.at[slot]
+            buffers[slot], a3_hbm.at[pl.ds(b * GROUP, GROUP)], a3sem.at[slot]
         )
 
-    def second(b, c):
-        slot = lax.rem(b, 2)
-
-        @pl.when(b >= 2)
-        def _():
-            a3_copy(b - 2, slot).wait()
-
-        def spread(k, c):
+    def spread(b, slot):
+        for k in range(GROUP):
             i = b * GROUP + k
             m = mk[i].reshape(cells, 128)
             cm = wide(m[0:cols], mid // 128)
@@ -528,48 +528,61 @@
             left = jnp.where(col_index == 0, 0.0, pltpu.roll(full, 1, 0)).astype(BF16)
             right = jnp.where(col_index == cols - 1, 0.0, pltpu.roll(full, ext - 1, 0)).astype(BF16)
             full = full.astype(BF16)
-            pieces = []
             for g in range(2):
-                for v in (left, full, right):
-                    pieces.append(v[:, g * half : (g + 1) * half])
-            a3[slot, k] = jnp.concatenate(pieces, axis=1).reshape(slots + 2, cols, 6 * half)
-            return c
-
-        lax.fori_loop(0, GROUP, spread, 0)
+                for d, v in enumerate((left, full, right)):
+                    lanes = slice((3 * g + d) * half, (3 * g + d + 1) * half)
+                    buffers[slot][k, :, :, lanes] = v[:, g * half : (g + 1) * half].reshape(
+                        slots + 2, cols, half
+                    )
+
+    def convolve(b, slot):
+        m = wide(mk[pl.ds(b * GROUP, GROUP)].reshape(lines, 128), mid // 128)
         for g in range(2):
+            lanes = slice(g * mid, (g + 1) * mid)
             taps = jnp.concatenate(
                 [
-                    a3[slot, :, dy : dy + slots, :, g * 3 * half : (g + 1) * 3 * half].reshape(
-                        GROUP * cells, 3 * half
+                    buffers[slot][:, dy : dy + slots, :, g * 3 * half : (g + 1) * 3 * half].reshape(
+                        lines, 3 * half
                     )
                     for dy in range(3)
                 ],
                 axis=1,
             )
-            value = mm(taps, ws[:, :, g * mid : (g + 1) * mid].reshape(9 * half, mid))
-            sp[pl.ds(b * GROUP, GROUP), :, :, g * mid : (g + 1) * mid] = value.reshape(
-                GROUP, slots, cols, mid
-            )
+            v = mm(taps, ws[:, :, lanes].reshape(9 * half, mid))
+            sp[pl.ds(b * GROUP, GROUP), :, :, lanes] = v.reshape(GROUP, slots, cols, mid)
+            w = v * m
+            acc2[0, :, lanes] += fold(w)
+            acc2[1, :, lanes] += fold(w * v)
+
+    def second(b, slot, more):
         a3_copy(b, slot).start()
+        convolve(b, slot)
+        if more:
+
+            @pl.when(b >= 1)
+            def _():
+                a3_copy(b - 1, 1 - slot).wait()
+
+            spread(b + 1, 1 - slot)
+
+    spread(0, 0)
+
+    def pair(j, c):
+        second(2 * j, 0, True)
+        second(2 * j + 1, 1, True)
         return c
 
-    lax.fori_loop(0, blocks, second, 0)
+    pairs = (blocks - 1) // 2
+    lax.fori_loop(0, pairs, pair, 0)
+    rest = blocks - 2 * pairs
+    second(2 * pairs, 0, rest == 2)
+    if rest == 2:
+        second(2 * pairs + 1, 1, False)
     pending += [a3_copy(0, 0), a3_copy(0, 1)]
     out_sp = pltpu.make_async_copy(sp, sp_hbm, osem.at[2])
     out_sp.start()
     pending.append(out_sp)
 
-    def second_sums(i, c):
-        m = wide(mk[i].reshape(cells, 128), mid // 128)
-        for g in range(2):
-            lanes = slice(g * mid, (g + 1) * mid)
-            v = sp[i, :, :, lanes].reshape(cells, mid)
-            w = v * m
-            acc2[0, :, lanes] += fold(w)
-            acc2[1, :, lanes] += fold(w * v)
-        return c
-
-    lax.fori_loop(0, images, second_sums, 0, unroll=2)
     buf2[me, 0:1] = row_sum(acc2[0])
     buf2[me, 1:2] = row_sum(acc2[1])
     links.all_start(buf2, sem2)
@@ -618,32 +631,29 @@
     w0[...] = sigmoid(lean)
     w1[...] = sigmoid(-lean)
 
-    gram[...] = jnp.zeros_like(gram)
-    mixed_sum[...] = jnp.zeros_like(mixed_sum)
-
-    def mixing(b, c):
-        def one(k, c):
-            i = b * GROUP + k
-            p0 = pp[i, :, :, 0:mid].reshape(cells, mid)
-            p1 = pp[i, :, :, mid:].reshape(cells, mid)
-            v = w0[pl.ds(i, 1)] * p0 + w1[pl.ds(i, 1)] * p1
-            mx[i] = v.astype(BF16).reshape(slots, cols, mid)
-            pd[i] = (p0 - p1).astype(BF16).reshape(slots, cols, mid)
-            return c
-
-        lax.fori_loop(0, GROUP, one, 0)
-        v = mx[pl.ds(b * GROUP, GROUP)].reshape(GROUP * cells, mid)
-        gram[...] += mm_tn(v, v)
-        mixed_sum[...] += mm_tn(v, jnp.ones((GROUP * cells, 128), BF16))
+
+    def mixing(i, c):
+        p0 = pp[i, :, :, 0:mid].reshape(cells, mid)
+        p1 = pp[i, :, :, mid:].reshape(cells, mid)
+        v = w0[pl.ds(i, 1)] * p0 + w1[pl.ds(i, 1)] * p1
+        mx[i] = v.astype(BF16).reshape(slots, cols, mid)
+        pd[i] = (p0 - p1).astype(BF16).reshape(slots, cols, mid)
         return c
 
-    lax.fori_loop(0, blocks, mixing, 0)
+    lax.fori_loop(0, images, mixing, 0, unroll=2)
+    v = mx[...].reshape(images * cells, mid)
+    v = mm_tn(v, jnp.concatenate([v, jnp.ones((images * cells, 128), BF16)], axis=1))
+    gram[...] = v[:, 0:mid]
+    mixed_sum[...] = v[:, mid:]
     out_mx = pltpu.make_async_copy(mx, mx_hbm, osem.at[4])
     out_mx.start()
     pending.append(out_mx)
     out_pd = pltpu.make_async_copy(pd, pd_hbm, osem.at[3])
     out_pd.start()
     pending.append(out_pd)
+    out_xt.wait()
+    pending = [c for c in pending if c is not out_xt]
+    gw = xt.at[0:mid]
     gw[...] = mm_terms(mm, gram[...], we[...], 3)
     wef = we[...].astype(F32)
     rbuf4[r, 0:1] = row_sum(wide(mixed_sum[...], ch // 128) * wef)
@@ -659,6 +669,10 @@
     v3[5:6] = 0.5 * offset
     v3[6:8] = jnp.zeros((2, ch), F32)
     awe[...] = (wef * scale).astype(BF16)
+    for k, (src, dst) in enumerate([(gw, gw_hbm), (awe, awe_hbm), (wt, wt_hbm)]):
+        copy = pltpu.make_async_copy(src, dst, osem.at[6 + k])
+        copy.start()
+        pending.append(copy)
 
     for copy in pending:
         copy.wait()
@@ -678,7 +692,7 @@
         (sd(cells + (mid,), BF16), ANY),
         (sd(cells + (mid,), BF16), ANY),
         (sd(cells + (128,)), ANY),
-        (sd((mid + 128, ch)), ANY),
+        (sd((mid + 8, ch)), ANY),
         (sd((8, mid)), VMEM),
         (sd((8, 2 * mid)), VMEM),
         (sd((8, ch)), VMEM),
@@ -689,9 +703,9 @@
         (sd((images, mid)), VMEM),
         (sd((images, mid)), VMEM),
         (sd((images, mid)), VMEM),
-        (sd((mid, ch)), VMEM),
-        (sd((mid, ch), BF16), VMEM),
-        (sd((2, 3 * mid, 3 * mid // 2), BF16), VMEM),
+        (sd((mid, ch)), ANY),
+        (sd((mid, ch), BF16), ANY),
+        (sd((2, 3 * mid, 3 * mid // 2), BF16), ANY),
         (sd((mid, 128)), VMEM),
     ]
     dma = pltpu.SemaphoreType.DMA
@@ -702,9 +716,14 @@
         pltpu.VMEM(cells + (mid,), BF16),
         pltpu.VMEM(cells + (mid,), BF16),
         pltpu.VMEM(cells + (128,), F32),
-        pltpu.VMEM((mid + 128, ch), F32),
-        pltpu.VMEM((2, GROUP, slots, cols, ch), BF16),
-        pltpu.VMEM((2, GROUP, slots + 2, cols, 3 * mid), BF16),
+        pltpu.VMEM((mid + 8, ch), F32),
+        pltpu.VMEM((images, slots, cols, ch), BF16),
+        pltpu.VMEM((GROUP, slots + 2, cols, 3 * mid), BF16),
+        pltpu.VMEM((GROUP, slots + 2, cols, 3 * mid), BF16),
+        pltpu.VMEM(args[6].shape, BF16),
+        pltpu.VMEM((mid, ch), BF16),
+        pltpu.VMEM((mid, ch), BF16),
+        pltpu.VMEM((2, 3 * mid, 3 * mid // 2), BF16),
         pltpu.VMEM((3, 8, mid), F32),
         pltpu.VMEM((2, 8, 2 * mid), F32),
         pltpu.VMEM((mid, mid), F32),
@@ -717,8 +736,8 @@
         pltpu.VMEM((n_img, 2, inter), F32),
         pltpu.VMEM((n_row, 2, ch), F32),
         pltpu.VMEM((n_img, 2, ch), F32),
-        dma((2,)),
-        dma((6,)),
+        dma((images // GROUP,)),
+        dma((9,)),
         dma((2,)),
         dma((4,)),
         dma((2, n)),
@@ -729,6 +748,8 @@
         dma((2, n_img)),
     ]
     in_specs = [SMEM, SMEM, ANY] + [VMEM] * (len(args) - 3)
+    for k in (6, 14):
+        in_specs[k] = ANY
     return pl.pallas_call(
         functools.partial(forward_kernel, n_img, n_row),
         out_shape=[o for o, _ in outs],
@@ -737,7 +758,7 @@
         scratch_shapes=scratch,
         name="forward",
         compiler_params=pltpu.CompilerParams(
-            collective_id=0, has_side_effects=True, vmem_limit_bytes=60 * 1024 * 1024
+            collective_id=0, has_side_effects=True, vmem_limit_bytes=62 * 1024 * 1024
         ),
     )(*args)
 
@@ -745,10 +766,11 @@
 PART = 2
 
 
-def third_kernel(x, cot, mx, mk, we, awe, v3, bo, sg, q, m_out, *parts):
+def third_kernel(counts, group, x, cot, mx, we, awe, v3, bo, sg, q, m_out, *parts):
     per, slots, cols, ch = x.shape
     mid = mx.shape[-1]
     cells = PART * slots * cols
+    columns = lax.broadcasted_iota(jnp.int32, (cols, 128), 0)
 
     @pl.when(pl.program_id(0) == 0)
     def _():
@@ -764,8 +786,11 @@
             product(p + 1)
         for k in range(PART):
             i = p * PART + k
+            image = pl.program_id(0) * per + i
+            inside = jnp.where(columns < 12 + 2 * group[image], 1.0, 0.0).astype(F32)
             for s in range(slots):
-                m = wide(mk[i, s], ch // 128)
+                held = jnp.where(s < counts[image], 1.0, 0.0).astype(F32)
+                m = wide(inside * held, ch // 128)
                 at = (k * slots + s) * cols
                 half = parts[p][at : at + cols] * v3[4:5] + v3[5:6] + 0.5 * x[i, s].astype(F32)
                 th = jnp.tanh(half)
@@ -781,7 +806,7 @@
     m_out[mid : mid + 16] += mm(jnp.ones((16, per * slots * cols), BF16), v)
 
 
-def call_third(x, cot, mx, mk, we, awe, v3):
+def call_third(counts, group, x, cot, mx, we, awe, v3):
     images, slots, cols, ch = x.shape
     mid = mx.shape[-1]
     per = 8
@@ -801,7 +826,7 @@
             sd((mid + 16, ch)),
         ],
         grid=(images // per,),
-        in_specs=[cells(ch), cells(ch), cells(mid), cells(128), whole(we), whole(awe), whole(v3)],
+        in_specs=[SMEM, SMEM, cells(ch), cells(ch), cells(mid), whole(we), whole(awe), whole(v3)],
         out_specs=[
             cells(ch),
             cells(ch),
@@ -811,7 +836,7 @@
         scratch_shapes=[pltpu.VMEM((PART * slots * cols, ch), F32)] * (per // PART),
         name="third",
         compiler_params=pltpu.CompilerParams(vmem_limit_bytes=60 * 1024 * 1024),
-    )(x, cot, mx, mk, we, awe, v3)
+    )(counts, group, x, cot, mx, we, awe, v3)
 
 
 def backward_kernel(
@@ -836,12 +861,12 @@
     w0,
     w1,
     pooled,
-    gw,
+    gw_hbm,
     mixed_sum,
     m_in,
     area,
     g_at,
-    wt,
+    wt_hbm,
     down,
     up,
     we,
@@ -861,6 +886,8 @@
     pd,
     mx,
     mk,
+    gw,
+    wt,
     split_part,
     small_part,
     rows_all,
@@ -943,8 +970,12 @@
                 [(mx_hbm, mx), (q_hbm, mg), (pd_hbm, pd), (mk_hbm, mk), (sp_hbm, sp)]
             )
         ]
+        load_gw = pltpu.make_async_copy(gw_hbm, gw, lsem.at[5])
+        load_wt = pltpu.make_async_copy(wt_hbm, wt, lsem.at[6])
+        load_gw.start()
         for load in loads:
             load.start()
+        load_wt.start()
         pending = list(loads)
 
         mean3, factor3, scale3 = v3[0:1], v3[1:2], v3[2:3]
@@ -957,9 +988,18 @@
         b3[...] = total
         slope3, offset3 = norm_back_terms(mean3, factor3, scale3, n, total[0:1], total[1:2])
         slope = factor3 * (total[1:2] / n)
-        mb[...] = mm_terms(mm_nt, wef * slope, awe[...], 2)
-        level = total[0:1] / n - slope * mean3
-        ev = mm_terms(mm_nt, jnp.broadcast_to(level, (8, ch)), awe[...], 3)[0:1]
+        level = jnp.broadcast_to(total[0:1] / n - slope * mean3, (16, ch))
+        lefts = []
+        for v, terms in ((wef * slope, 2), (level, 3)):
+            for _ in range(terms):
+                lefts.append(v.astype(BF16))
+                v = v - lefts[-1].astype(F32)
+        v = mm_nt(jnp.concatenate(lefts, axis=0), awe[...])
+        fix = v[0:mid] + v[mid : 2 * mid]
+        ev = v[2 * mid : 2 * mid + 1] + v[2 * mid + 16 : 2 * mid + 17] + v[2 * mid + 32 : 2 * mid + 33]
+        high = fix.astype(BF16)
+        mb[0:mid] = high
+        mb[mid:] = (fix - high.astype(F32)).astype(BF16)
 
         def expand_piece(p):
             rows = pl.ds(pl.multiple_of(p * (mid // n_row), mid // n_row), mid // n_row)
@@ -967,6 +1007,7 @@
                 m_in[rows] * scale3 - wide(mixed_sum[rows], ch // 128) * offset3 - gw[rows] * slope3
             )
 
+        load_gw.wait()
         expand_red.begin(expand_piece)
 
         for load in loads[:4]:
@@ -975,25 +1016,17 @@
 
         def mix_back(b, c):
             v = mx[pl.ds(b * GROUP, GROUP)].reshape(GROUP * cells, mid)
-            high = mb[...].astype(BF16)
-            fix = mm(v, high) + mm(v, (mb[...] - high.astype(F32)).astype(BF16))
-            mg[pl.ds(b * GROUP, GROUP)] -= fix.reshape(GROUP, slots, cols, mid)
-
-            def one(k, c):
+            v = mm(jnp.concatenate([v, v], axis=1), mb[...])
+            for k in range(GROUP):
                 i = b * GROUP + k
                 m = wide(mk[i].reshape(cells, 128), mid // 128)
-                v = mg[i].reshape(cells, mid) - m * ev
-                mg[i] = v.reshape(slots, cols, mid)
-                d = pd[i].reshape(cells, mid).astype(F32)
-                dpart[pl.ds(i, 1)] = row_sum(fold(v * d))
-                return c
-
-            lax.fori_loop(0, GROUP, one, 0)
+                w = mg[i].reshape(cells, mid) - v[k * cells : (k + 1) * cells] - m * ev
+                mg[i] = w.reshape(slots, cols, mid)
+                dpart[pl.ds(i, 1)] = row_sum(fold(w * pd[i].reshape(cells, mid).astype(F32)))
             return c
 
         lax.fori_loop(0, blocks, mix_back, 0)
 
-        expand_red.second(expand_piece)
         upf = up[...].astype(F32)
         lean = dpart[...] * w0[...] * w1[...]
         rbuf6[r] = mm_nt(lean, upf[:, :mid] - upf[:, mid:], HIGH)
@@ -1021,12 +1054,13 @@
             )
             small_part[p, up_rows + down_rows // 2 :] = jnp.broadcast_to(bias_part, (8, mid))
 
-        expand_red.third()
         small_red.begin(small_piece)
+        expand_red.second(expand_piece)
         pgrad[...] = mm_nt(squeeze_grad, down[...].astype(F32), HIGH) / area[...]
 
         def with_second_grads(ub, a3, geb):
             loads[4].wait()
+            load_wt.wait()
             del pending[0]
             acc2[...] = jnp.zeros_like(acc2)
 
@@ -1044,8 +1078,6 @@
                 return c
 
             lax.fori_loop(0, images, second_back, 0, unroll=2)
-            expand_red.fourth()
-            small_red.second(small_piece)
             mean2, factor2, scale2 = v2[0:1], v2[1:2], v2[2:3]
             s0 = row_sum(acc2[0])
             buf7[me, 0:1] = s0
@@ -1054,8 +1086,7 @@
             total = links.all_wait(buf7, sem7)
             b2[...] = total
             slope2, offset2 = norm_back_terms(mean2, factor2, scale2, n, total[0:1], total[1:2])
-            expand_out[...] = expand_red.end()
-            small_red.third()
+            expand_red.third()
 
             def second_grad(grad, s, m):
                 return (grad * scale2 - m * (offset2 + slope2 * s)).astype(BF16)
@@ -1109,6 +1140,18 @@
                 @pl.when(b + 1 < blocks)
                 def _():
                     a3_copy(b + 1, 1 - slot).start()
+
+                @pl.when(b == 2)
+                def _():
+                    small_red.second(small_piece)
+
+                @pl.when(b == 4)
+                def _():
+                    expand_red.fourth()
+
+                @pl.when(b == 6)
+                def _():
+                    small_red.third()
 
                 def one(k, c):
                     i = b * GROUP + k
@@ -1153,7 +1196,6 @@
         ]
         for load in loads:
             load.start()
-        small_red.fourth()
 
         def split_piece(p):
             lines = []
@@ -1168,11 +1210,27 @@
                     split_part[g, :, tap * half : (tap + 1) * half].astype(BF16)
                 )
         split_red.begin(split_piece)
+        @pl.when(has_prev)
+        def _():
+            to_prev.wait_send()
+            to_next.wait_recv()
+
+        @pl.when(has_next)
+        def _():
+            to_next.wait_send()
+            to_prev.wait_recv()
+
+        loads[0].wait()
+        acc1[...] = jnp.zeros_like(acc1)
 
         def conv_back(b, c):
-            @pl.when(b == 2)
+            @pl.when(b == 1)
             def _():
                 split_red.second(split_piece)
+
+            @pl.when(b == 3)
+            def _():
+                small_red.fourth()
 
             @pl.when(b == 5)
             def _():
@@ -1190,53 +1248,41 @@
                     [moved[dy].reshape(GROUP * cells, mid) for dy in range(3)], axis=1
                 )
                 value = mm(v, wt[g])
-                mg[pl.ds(b * GROUP, GROUP), :, :, g * half : (g + 1) * half] = columns_back(
-                    value, GROUP * cells
-                ).reshape(GROUP, slots, cols, half)
+                back = columns_back(value, GROUP * cells)
+                lanes = slice(g * half, (g + 1) * half)
+                for k in range(GROUP):
+                    i = b * GROUP + k
+                    m = mk[i].reshape(cells, 128)
+                    low = ret[1, i, :, lanes].astype(F32)
+                    parts = []
+                    for s in range(slots):
+                        at = k * cells + s * cols
+                        here = back[at : at + cols] + low * jnp.where(counts[i] - 1 == s, 1.0, 0.0).astype(F32)
+                        if s == 0:
+                            here = here + ret[0, i, :, lanes].astype(F32)
+                        parts.append(here)
+                    v = fp[i, :, :, lanes].reshape(cells, half)
+                    z = v * v1[2:3, lanes] + v1[3:4, lanes]
+                    grad = jnp.concatenate(parts, axis=0) * swish_slope(z) * wide(m, half // 128)
+                    mg[i, :, :, lanes] = grad.reshape(slots, cols, half)
+                    acc1[0, :, lanes] += fold(grad)
+                    acc1[1, :, lanes] += fold(grad * v)
             return c
 
         lax.fori_loop(0, blocks, conv_back, 0)
+        expand_out[...] = expand_red.end()
         rows_all[r] = small_red.end()
         rows_copies = links.row_copies(rows_all, rsem9)
-        for copy in rows_copies:
-            copy.start()
-        @pl.when(has_prev)
-        def _():
-            to_prev.wait_send()
-            to_next.wait_recv()
-
-        @pl.when(has_next)
-        def _():
-            to_next.wait_send()
-            to_prev.wait_recv()
-
-        loads[0].wait()
-        acc1[...] = jnp.zeros_like(acc1)
-
-        def first_back(i, c):
-            m = wide(mk[i].reshape(cells, 128), mid // 128)
-            count = counts[i]
-            low = ret[1, i].astype(F32)
-            parts = []
-            for s in range(slots):
-                here = mg[i, s] + low * jnp.where(count - 1 == s, 1.0, 0.0).astype(F32)
-                if s == 0:
-                    here = here + ret[0, i].astype(F32)
-                parts.append(here)
-            v = fp[i].reshape(cells, mid)
-            z = v * v1[2:3] + v1[3:4]
-            grad = jnp.concatenate(parts, axis=0) * swish_slope(z) * m
-            mg[i] = grad.reshape(slots, cols, mid)
-            pd[i] = grad.astype(BF16).reshape(slots, cols, mid)
-            acc1[0] += fold(grad)
-            acc1[1] += fold(grad * v)
-            return c
-
-        lax.fori_loop(0, images, first_back, 0, unroll=2)
         s0 = row_sum(acc1[0])
         buf8[me, 0:1] = s0
         buf8[me, 1:2] = v1[1:2] * (row_sum(acc1[1]) - v1[0:1] * s0)
         links.all_start(buf8, sem8)
+
+        def narrow(i, c):
+            pd[i] = mg[i].astype(BF16)
+            return c
+
+        lax.fori_loop(0, images, narrow, 0, unroll=4)
         loads[2].wait()
         lines = images * cells
         width = ch // 2
@@ -1260,6 +1306,8 @@
             return jnp.transpose(v.astype(BF16)).astype(F32)
 
         reduce_red.begin(reduce_piece)
+        for copy in rows_copies:
+            copy.start()
         split_red.fourth()
 
         def first_grad(i, c):
@@ -1294,7 +1342,7 @@
         to_inputs,
         pltpu.VMEM((images, slots, cols, mid), F32),
         pltpu.VMEM((images, slots, cols, ch), BF16),
-        pltpu.VMEM((mid + 128, ch), F32),
+        pltpu.VMEM((mid + 8, ch), F32),
         pltpu.VMEM((mid, ch), F32),
         pltpu.VMEM((9 * half, 2 * mid), BF16),
     )
@@ -1309,7 +1357,7 @@
     ]
 
 
-def call_backward(n_img, n_row, args, ch, inter):
+def call_backward(n_img, n_row, args, gw, wt, ch, inter):
     q = args[1]
     images, slots, cols, mid = q.shape
     half = mid // 2
@@ -1335,6 +1383,8 @@
         pltpu.VMEM(cells + (mid,), BF16),
         pltpu.VMEM(cells + (mid,), BF16),
         pltpu.VMEM(cells + (128,), F32),
+        pltpu.VMEM((mid, ch), F32),
+        pltpu.VMEM((2, 3 * mid, 3 * half), BF16),
         pltpu.VMEM((2, mid, 9 * half), F32),
         pltpu.VMEM((n_row, sizes[3][0], mid), F32),
         pltpu.VMEM((n_row, sizes[3][0], mid), F32),
@@ -1342,7 +1392,7 @@
         pltpu.VMEM((2, images, cols, mid), BF16),
         pltpu.VMEM((2, 8, mid), F32),
         pltpu.VMEM((2, 8, 2 * mid), F32),
-        pltpu.VMEM((mid, mid), F32),
+        pltpu.VMEM((2 * mid, mid), BF16),
         pltpu.VMEM((images, mid), F32),
         pltpu.VMEM((images, mid), F32),
         pltpu.VMEM((n_img, 2, ch), F32),
@@ -1365,6 +1415,9 @@
     for rows, width, dtype in sizes:
         scratch += Reducer.scratch(n_img, rows, width, dtype)
     in_specs = [SMEM] + [ANY] * 9 + [VMEM] * (len(args) - 10)
+    for k, a in enumerate(args):
+        if a is gw or a is wt:
+            in_specs[k] = ANY
     return pl.pallas_call(
         functools.partial(backward_kernel, n_img, n_row),
         out_shape=[o for o, _ in outs],
@@ -1490,7 +1543,7 @@
         images, slots, cols, ch, mid, inter,
     )
     block_out, sg, q, m_sum = call_third(
-        feature_map, cotangent, mx, mk, expand_weight, awe, v3
+        counts, image_group, feature_map, cotangent, mx, expand_weight, awe, v3
     )
     (
         fg, grad_expand, grad_split, grad_reduce, grad_up, grad_down, bias, b1, b2, b3, b_at,
@@ -1502,7 +1555,7 @@
             gw, mixed_sum, m_sum, area, line(gain_attend), wt, attn_down, attn_up, expand_weight,
             awe,
         ),
-        ch, inter,
+        gw, wt, ch, inter,
     )
     small = call_input(
         fg, sg, reduce_weight, grad_expand, grad_split, grad_reduce, grad_up, grad_down, bias,

time: 213 us -> 201 us (0.944)
  Pallas kernels: 212 us -> 200 us
    pallas_call x1, Pallas kernels: 73.8 us -> 67.5 us  [call_forward(): pl.pallas_call(functools.partial(forward_kernel, n_img, n_row), out_shape...]
    pallas_call x1, Pallas kernels: 101 us -> 95.3 us  [call_backward(): pl.pallas_call(functools.partial(backward_kernel, n_img, n_row), out_shap...]
where the time goes in v4:
time: 201 us
  Pallas kernels  200 us (100%)
    pallas_call x1, Pallas kernels, call_backward(): pl.pallas_call(functools.partial(backward_kernel, n_img, n_row), out_shap...  95.3 us
    pallas_call x1, Pallas kernels, call_forward(): pl.pallas_call(functools.partial(forward_kernel, n_img, n_row), out_shape...  67.5 us
    pallas_call x1, Pallas kernels, call_third(): pl.pallas_call(third_kernel, out_shape=[sd(x.shape, BF16), sd(x.shape, BF...  25.6 us
    pallas_call x1, Pallas kernels, call_input(): pl.pallas_call(input_kernel, out_shape=[sd(sg.shape, BF16)] + outs, grid=...  11.6 us

profile of v4, /device:TPU:0, one launch (start us, length us, event | category | flops | bytes accessed | tf_op | source)
XLA Modules:
  0.0 200.9 jit_solution(1441468947811984413)
XLA Ops:
  0.7 67.5 %forward.1 = (f32[56,6,16,256]{3,2,1,0:T(8,128)}, bf16[56,8,16,768]{3,2,1,0:T(8,128)(2,1)}, f32[56,6,16,512]{3,2,1,0:T(8,128)}, bf16[56,6,16,256]{3,2,1,0:T(8,12...) custom-call(s32[56]{0:T(128)} %bitcast.22, ...), custom_call_target="tpu_custom_call" | custom-call | tf_op jit(solution)/shard_map/forward/pallas_call | solution.py:753
  68.2 25.6 %third.1 = (bf16[56,6,16,1024]{3,2,1,0:T(8,128)(2,1)}, bf16[56,6,16,1024]{3,2,1,0:T(8,128)(2,1)}, f32[56,6,16,256]{3,2,1,0:T(8,128)}, f32[272,1024]{1,0:T(8,128)}) custom-call(s32[56]{0:T(128)} %bitcast.23, s32[56]{0:T(128)} %group.3, bf16[56,6,16,1024]{3,2,1,0:T(8,128)(2,1)} %x_hbm.3, bf16[56,6,16,1024]{3,2,1,0:T(8,128)(2,1)} %cot.1, ...), custom_call_target="tpu_custom_call" | custom-call | tf_op jit(solution)/shard_map/third/pallas_call | solution.py:820
  93.8 95.3 %backward.1 = (bf16[56,6,16,256]{3,2,1,0:T(8,128)(2,1)}, f32[64,1024]{1,0:T(8,128)}, f32[288,512]{1,0:T(8,128)}, f32[256,256]{1,0:T(8,128)}, f32[128,256]{1,0:T(...) custom-call(s32[56]{0:T(128)} %bitcast.24, ...), custom_call_target="tpu_custom_call" | custom-call | tf_op jit(solution)/shard_map/backward/pallas_call | solution.py:1421
  189.1 11.6 %input_grad.1 = (bf16[56,6,16,1024]{3,2,1,0:T(8,128)(2,1)}, f32[64,1024]{1,0:T(8,128)}, f32[288,512]{1,0:T(8,128)}, f32[256,256]{1,0:T(8,128)}, f32[128,512]{1,0...) custom-call(bf16[56,6,16,256]{3,2,1,0:T(8,128)(2,1)} %get-tuple-elem, ...), custom_call_target="tpu_custom_call" | custom-call | tf_op jit(solution)/shard_map/input_grad/pallas_call | solution.py:1475

commit v5 on v4

--- a/solution.py
+++ b/solution.py
@@ -128,26 +128,38 @@
             buf, sems.at[0], sems.at[1], self.i, k, (lax.rem(self.i + k, self.ni), self.r)
         )
 
-    def row_total(self, buf, sems):
+    def row_start(self, buf, sems):
         copies = self.row_copies(buf, sems)
         for c in copies:
             c.start()
+        return copies
+
+    def row_end(self, buf, copies):
         for c in copies:
             c.wait()
         return jnp.sum(buf[...], axis=0)
 
-    def img_total(self, buf, sems):
+    def row_total(self, buf, sems):
+        return self.row_end(buf, self.row_start(buf, sems))
+
+    def img_start(self, buf, sems):
         def go(k, c):
             self.img_copy(buf, sems, k).start()
             return c
 
+        lax.fori_loop(1, self.ni, go, 0)
+
+    def img_end(self, buf, sems):
         def end(k, c):
             self.img_copy(buf, sems, k).wait()
             return c
 
-        lax.fori_loop(1, self.ni, go, 0)
         lax.fori_loop(1, self.ni, end, 0)
         return jnp.sum(buf[...], axis=0)
+
+    def img_total(self, buf, sems):
+        self.img_start(buf, sems)
+        return self.img_end(buf, sems)
 
 
 class Reducer:
@@ -371,9 +383,6 @@
     pending = []
     in_ws = pltpu.make_async_copy(ws_hbm, ws, osem.at[6])
     in_we = pltpu.make_async_copy(we_hbm, we, osem.at[7])
-    in_ws.start()
-    in_we.start()
-    pending += [in_ws, in_we]
 
     def masks(i, c):
         count, height = counts[i], 12 + 2 * group[i]
@@ -384,9 +393,6 @@
         return c
 
     lax.fori_loop(0, images, masks, 0)
-    out_mk = pltpu.make_async_copy(mk, mk_hbm, osem.at[1])
-    out_mk.start()
-    pending.append(out_mk)
     acc1[...] = jnp.zeros_like(acc1)
     lines = GROUP * cells
 
@@ -408,6 +414,12 @@
         return c
 
     lax.fori_loop(0, blocks, first, 0)
+    in_ws.start()
+    in_we.start()
+    pending += [in_ws, in_we]
+    out_mk = pltpu.make_async_copy(mk, mk_hbm, osem.at[1])
+    out_mk.start()
+    pending.append(out_mk)
     out_fp = pltpu.make_async_copy(fp, fp_hbm, osem.at[0])
     out_fp.start()
     pending.append(out_fp)
@@ -599,21 +611,30 @@
 
     def second_act(i, c):
         m = wide(mk[i].reshape(cells, 128), mid // 128)
-        both = None
+        acts = []
         for g in range(2):
             lanes = slice(g * mid, (g + 1) * mid)
             z = sp[i, :, :, lanes].reshape(cells, mid) * v2[2:3, lanes] + v2[3:4, lanes]
-            p = z * sigmoid(z) * m
-            pp[i, :, :, lanes] = p.reshape(slots, cols, mid)
-            part = fold(p)
-            both = part if both is None else both + part
-        pooled[pl.ds(i, 1)] = row_sum(both)
+            acts.append(z * sigmoid(z) * m)
+        pp[i, :, :, 0:mid] = (acts[0] - acts[1]).reshape(slots, cols, mid)
+        pp[i, :, :, mid:] = acts[1].reshape(slots, cols, mid)
+        pooled[pl.ds(i, 1)] = row_sum(fold(acts[0] + acts[1]))
         return c
 
     lax.fori_loop(0, images, second_act, 0, unroll=2)
     pooled[...] = pooled[...] / area[...]
     rbuf3[r] = mm(pooled[...], down[...].astype(F32), HIGH)
-    squeeze = links.row_total(rbuf3, rsem3)
+    copies = links.row_start(rbuf3, rsem3)
+
+    def difference(i, c):
+        pd[i] = pp[i, :, :, 0:mid].astype(BF16)
+        return c
+
+    lax.fori_loop(0, images, difference, 0, unroll=4)
+    out_pd = pltpu.make_async_copy(pd, pd_hbm, osem.at[3])
+    out_pd.start()
+    pending.append(out_pd)
+    squeeze = links.row_end(rbuf3, copies)
     ibuf3[links.i, 0:1] = row_sum(squeeze)
     ibuf3[links.i, 1:2] = row_sum(squeeze * squeeze)
     total = links.img_total(ibuf3, isem3)
@@ -633,11 +654,9 @@
 
 
     def mixing(i, c):
-        p0 = pp[i, :, :, 0:mid].reshape(cells, mid)
-        p1 = pp[i, :, :, mid:].reshape(cells, mid)
-        v = w0[pl.ds(i, 1)] * p0 + w1[pl.ds(i, 1)] * p1
+        v = w0[pl.ds(i, 1)] * pp[i, :, :, 0:mid].reshape(cells, mid)
+        v = v + pp[i, :, :, mid:].reshape(cells, mid)
         mx[i] = v.astype(BF16).reshape(slots, cols, mid)
-        pd[i] = (p0 - p1).astype(BF16).reshape(slots, cols, mid)
         return c
 
     lax.fori_loop(0, images, mixing, 0, unroll=2)
@@ -648,9 +667,6 @@
     out_mx = pltpu.make_async_copy(mx, mx_hbm, osem.at[4])
     out_mx.start()
     pending.append(out_mx)
-    out_pd = pltpu.make_async_copy(pd, pd_hbm, osem.at[3])
-    out_pd.start()
-    pending.append(out_pd)
     out_xt.wait()
     pending = [c for c in pending if c is not out_xt]
     gw = xt.at[0:mid]
@@ -963,7 +979,7 @@
     def small_piece(p):
         return small_part[p]
 
-    def to_second_grads(sp):
+    def to_second_grads(sp, ub):
         loads = [
             pltpu.make_async_copy(src, dst, lsem.at[k])
             for k, (src, dst) in enumerate(
@@ -1030,14 +1046,29 @@
         upf = up[...].astype(F32)
         lean = dpart[...] * w0[...] * w1[...]
         rbuf6[r] = mm_nt(lean, upf[:, :mid] - upf[:, mid:], HIGH)
+        copies = links.row_start(rbuf6, rsem6)
         z = at_out[...]
         attend = z * sigmoid(z)
         up_part = mm_tn(attend, lean, HIGH)
         bias_part = row_sum(lean)
-        attend_grad = links.row_total(rbuf6, rsem6) * swish_slope(z)
+        loads[4].wait()
+        del pending[0]
+
+        def slopes(i, c):
+            m = wide(mk[i].reshape(cells, 128), mid // 128)
+            for g in range(2):
+                lanes = slice(g * mid, (g + 1) * mid)
+                v = sp[i, :, :, lanes].reshape(cells, mid) * v2[2:3, lanes] + v2[3:4, lanes]
+                ub[i, :, :, lanes] = (swish_slope(v) * m).reshape(slots, cols, mid)
+            return c
+
+        lax.fori_loop(0, images * 2 // 5, slopes, 0, unroll=2)
+        attend_grad = links.row_end(rbuf6, copies) * swish_slope(z)
         ibuf6[links.i, 0:1] = row_sum(attend_grad)
         ibuf6[links.i, 1:2] = row_sum(attend_grad * at_norm[...])
-        total = links.img_total(ibuf6, isem6)
+        links.img_start(ibuf6, isem6)
+        lax.fori_loop(images * 2 // 5, images, slopes, 0, unroll=2)
+        total = links.img_end(ibuf6, isem6)
         b_at[...] = total
         count = float(images * n_img)
         squeeze_grad = (
@@ -1058,20 +1089,17 @@
         expand_red.second(expand_piece)
         pgrad[...] = mm_nt(squeeze_grad, down[...].astype(F32), HIGH) / area[...]
 
-        def with_second_grads(ub, a3, geb):
-            loads[4].wait()
+        def with_second_grads(a3, geb):
             load_wt.wait()
-            del pending[0]
             acc2[...] = jnp.zeros_like(acc2)
 
             def second_back(i, c):
-                m = wide(mk[i].reshape(cells, 128), mid // 128)
                 v = mg[i].reshape(cells, mid)
                 for g, w in enumerate((w0, w1)):
                     lanes = slice(g * mid, (g + 1) * mid)
                     s = sp[i, :, :, lanes].reshape(cells, mid)
-                    z = s * v2[2:3, lanes] + v2[3:4, lanes]
-                    grad = (v * w[pl.ds(i, 1)] + pgrad[pl.ds(i, 1)]) * swish_slope(z) * m
+                    grad = v * w[pl.ds(i, 1)] + pgrad[pl.ds(i, 1)]
+                    grad = grad * ub[i, :, :, lanes].reshape(cells, mid)
                     ub[i, :, :, lanes] = grad.reshape(slots, cols, mid)
                     acc2[0, :, lanes] += fold(grad)
                     acc2[1, :, lanes] += fold(grad * s)
@@ -1181,12 +1209,15 @@
 
         pl.run_scoped(
             with_second_grads,
-            pltpu.VMEM((images, slots, cols, 2 * mid), F32),
             pltpu.VMEM((2, GROUP, slots + 2, cols, 3 * mid), BF16),
             pltpu.VMEM((images, cols, 2 * mid), BF16),
         )
 
-    pl.run_scoped(to_second_grads, pltpu.VMEM((images, slots, cols, 2 * mid), F32))
+    pl.run_scoped(
+        to_second_grads,
+        pltpu.VMEM((images, slots, cols, 2 * mid), F32),
+        pltpu.VMEM((images, slots, cols, 2 * mid), F32),
+    )
 
     def to_inputs(fp, xs, xt, xu, split_rows):
         loads = [

time: 201 us -> 196 us (0.975)
  Pallas kernels: 200 us -> 195 us
    pallas_call x1, Pallas kernels: 95.3 us -> 91.3 us  [call_backward(): pl.pallas_call(functools.partial(backward_kernel, n_img, n_row), out_shap...]
where the time goes in v5:
time: 196 us
  Pallas kernels  195 us (99%)
    pallas_call x1, Pallas kernels, call_backward(): pl.pallas_call(functools.partial(backward_kernel, n_img, n_row), out_shap...  91.3 us
    pallas_call x1, Pallas kernels, call_forward(): pl.pallas_call(functools.partial(forward_kernel, n_img, n_row), out_shape...  66.7 us
    pallas_call x1, Pallas kernels, call_third(): pl.pallas_call(third_kernel, out_shape=[sd(x.shape, BF16), sd(x.shape, BF...  25.7 us
    pallas_call x1, Pallas kernels, call_input(): pl.pallas_call(input_kernel, out_shape=[sd(sg.shape, BF16)] + outs, grid=...  11.6 us

profile of v5, /device:TPU:0, one launch (start us, length us, event | category | flops | bytes accessed | tf_op | source)
XLA Modules:
  0.0 196.1 jit_solution(5452405042292473645)
XLA Ops:
  0.7 66.7 %forward.1 = (f32[56,6,16,256]{3,2,1,0:T(8,128)}, bf16[56,8,16,768]{3,2,1,0:T(8,128)(2,1)}, f32[56,6,16,512]{3,2,1,0:T(8,128)}, bf16[56,6,16,256]{3,2,1,0:T(8,12...) custom-call(s32[56]{0:T(128)} %bitcast.22, ...), custom_call_target="tpu_custom_call" | custom-call | tf_op jit(solution)/shard_map/forward/pallas_call | solution.py:769
  67.3 25.7 %third.1 = (bf16[56,6,16,1024]{3,2,1,0:T(8,128)(2,1)}, bf16[56,6,16,1024]{3,2,1,0:T(8,128)(2,1)}, f32[56,6,16,256]{3,2,1,0:T(8,128)}, f32[272,1024]{1,0:T(8,128)}) custom-call(s32[56]{0:T(128)} %bitcast.23, s32[56]{0:T(128)} %group.3, bf16[56,6,16,1024]{3,2,1,0:T(8,128)(2,1)} %x_hbm.3, bf16[56,6,16,1024]{3,2,1,0:T(8,128)(2,1)} %cot.1, ...), custom_call_target="tpu_custom_call" | custom-call | tf_op jit(solution)/shard_map/third/pallas_call | solution.py:836
  93.0 91.3 %backward.1 = (bf16[56,6,16,256]{3,2,1,0:T(8,128)(2,1)}, f32[64,1024]{1,0:T(8,128)}, f32[288,512]{1,0:T(8,128)}, f32[256,256]{1,0:T(8,128)}, f32[128,256]{1,0:T(...) custom-call(s32[56]{0:T(128)} %bitcast.24, ...), custom_call_target="tpu_custom_call" | custom-call | tf_op jit(solution)/shard_map/backward/pallas_call | solution.py:1452
  184.3 11.6 %input_grad.1 = (bf16[56,6,16,1024]{3,2,1,0:T(8,128)(2,1)}, f32[64,1024]{1,0:T(8,128)}, f32[288,512]{1,0:T(8,128)}, f32[256,256]{1,0:T(8,128)}, f32[128,512]{1,0...) custom-call(bf16[56,6,16,256]{3,2,1,0:T(8,128)(2,1)} %get-tuple-elem, ...), custom_call_target="tpu_custom_call" | custom-call | tf_op jit(solution)/shard_map/input_grad/pallas_call | solution.py:1506

commit v6 on v5

--- a/solution.py
+++ b/solution.py
@@ -779,7 +779,7 @@
     )(*args)
 
 
-PART = 2
+PART = 4
 
 
 def third_kernel(counts, group, x, cot, mx, we, awe, v3, bo, sg, q, m_out, *parts):
@@ -1076,17 +1076,6 @@
             * v_at[0:1]
             * (attend_grad - total[0:1] / count - at_norm[...] * (total[1:2] / count))
         )
-        down_part = mm_tn(pooled[...], squeeze_grad, HIGH)
-        for p in range(n_row):
-            lines = down_part[p * down_rows : (p + 1) * down_rows]
-            small_part[p, 0:up_rows] = up_part[p * up_rows : (p + 1) * up_rows]
-            small_part[p, up_rows : up_rows + down_rows // 2] = jnp.concatenate(
-                [lines[: down_rows // 2], lines[down_rows // 2 :]], axis=1
-            )
-            small_part[p, up_rows + down_rows // 2 :] = jnp.broadcast_to(bias_part, (8, mid))
-
-        small_red.begin(small_piece)
-        expand_red.second(expand_piece)
         pgrad[...] = mm_nt(squeeze_grad, down[...].astype(F32), HIGH) / area[...]
 
         def with_second_grads(a3, geb):
@@ -1111,10 +1100,20 @@
             buf7[me, 0:1] = s0
             buf7[me, 1:2] = factor2 * (row_sum(acc2[1]) - mean2 * s0)
             links.all_start(buf7, sem7)
+            down_part = mm_tn(pooled[...], squeeze_grad, HIGH)
+            for p in range(n_row):
+                lines = down_part[p * down_rows : (p + 1) * down_rows]
+                small_part[p, 0:up_rows] = up_part[p * up_rows : (p + 1) * up_rows]
+                small_part[p, up_rows : up_rows + down_rows // 2] = jnp.concatenate(
+                    [lines[: down_rows // 2], lines[down_rows // 2 :]], axis=1
+                )
+                small_part[p, up_rows + down_rows // 2 :] = jnp.broadcast_to(bias_part, (8, mid))
+
+            small_red.begin(small_piece)
             total = links.all_wait(buf7, sem7)
+            expand_red.second(expand_piece)
             b2[...] = total
             slope2, offset2 = norm_back_terms(mean2, factor2, scale2, n, total[0:1], total[1:2])
-            expand_red.third()
 
             def second_grad(grad, s, m):
                 return (grad * scale2 - m * (offset2 + slope2 * s)).astype(BF16)
@@ -1173,7 +1172,11 @@
                 def _():
                     small_red.second(small_piece)
 
-                @pl.when(b == 4)
+                @pl.when(b == 1)
+                def _():
+                    expand_red.third()
+
+                @pl.when(b == 5)
                 def _():
                     expand_red.fourth()
 

time: 196 us -> 195 us (level)
  no operation moved by 1% of the time
where the time goes in v6:
time: 195 us
  Pallas kernels  194 us (99%)
    pallas_call x1, Pallas kernels, call_backward(): pl.pallas_call(functools.partial(backward_kernel, n_img, n_row), out_shap...  90.9 us
    pallas_call x1, Pallas kernels, call_forward(): pl.pallas_call(functools.partial(forward_kernel, n_img, n_row), out_shape...  66.7 us
    pallas_call x1, Pallas kernels, call_third(): pl.pallas_call(third_kernel, out_shape=[sd(x.shape, BF16), sd(x.shape, BF...  25.3 us
    pallas_call x1, Pallas kernels, call_input(): pl.pallas_call(input_kernel, out_shape=[sd(sg.shape, BF16)] + outs, grid=...  11.6 us

profile of v6, /device:TPU:0, one launch (start us, length us, event | category | flops | bytes accessed | tf_op | source)
XLA Modules:
  0.0 195.3 jit_solution(1784665848820436459)
XLA Ops:
  0.7 66.7 %forward.1 = (f32[56,6,16,256]{3,2,1,0:T(8,128)}, bf16[56,8,16,768]{3,2,1,0:T(8,128)(2,1)}, f32[56,6,16,512]{3,2,1,0:T(8,128)}, bf16[56,6,16,256]{3,2,1,0:T(8,12...) custom-call(s32[56]{0:T(128)} %bitcast.22, ...), custom_call_target="tpu_custom_call" | custom-call | tf_op jit(solution)/shard_map/forward/pallas_call | solution.py:769
  67.3 25.3 %third.1 = (bf16[56,6,16,1024]{3,2,1,0:T(8,128)(2,1)}, bf16[56,6,16,1024]{3,2,1,0:T(8,128)(2,1)}, f32[56,6,16,256]{3,2,1,0:T(8,128)}, f32[272,1024]{1,0:T(8,128)}) custom-call(s32[56]{0:T(128)} %bitcast.23, s32[56]{0:T(128)} %group.3, bf16[56,6,16,1024]{3,2,1,0:T(8,128)(2,1)} %x_hbm.3, bf16[56,6,16,1024]{3,2,1,0:T(8,128)(2,1)} %cot.1, ...), custom_call_target="tpu_custom_call" | custom-call | tf_op jit(solution)/shard_map/third/pallas_call | solution.py:836
  92.7 90.9 %backward.1 = (bf16[56,6,16,256]{3,2,1,0:T(8,128)(2,1)}, f32[64,1024]{1,0:T(8,128)}, f32[288,512]{1,0:T(8,128)}, f32[256,256]{1,0:T(8,128)}, f32[128,256]{1,0:T(...) custom-call(s32[56]{0:T(128)} %bitcast.24, ...), custom_call_target="tpu_custom_call" | custom-call | tf_op jit(solution)/shard_map/backward/pallas_call | solution.py:1455
  183.5 11.6 %input_grad.1 = (bf16[56,6,16,1024]{3,2,1,0:T(8,128)(2,1)}, f32[64,1024]{1,0:T(8,128)}, f32[288,512]{1,0:T(8,128)}, f32[256,256]{1,0:T(8,128)}, f32[128,512]{1,0...) custom-call(bf16[56,6,16,256]{3,2,1,0:T(8,128)(2,1)} %get-tuple-elem, ...), custom_call_target="tpu_custom_call" | custom-call | tf_op jit(solution)/shard_map/input_grad/pallas_call | solution.py:1509

commit v7 on v6

--- a/solution.py
+++ b/solution.py
@@ -392,7 +392,7 @@
         mk[i] = jnp.where((rows < count) & (columns < height), 1.0, 0.0).astype(F32)
         return c
 
-    lax.fori_loop(0, images, masks, 0)
+    lax.fori_loop(0, images, masks, 0, unroll=4)
     acc1[...] = jnp.zeros_like(acc1)
     lines = GROUP * cells
 
@@ -1126,7 +1126,7 @@
                     geb[i] = second_grad(ub[i, at], sp[i, at], m)
                     return c
 
-                lax.fori_loop(0, images, edge_rows, 0, unroll=2)
+                lax.fori_loop(0, images, edge_rows, 0, unroll=4)
                 for g in range(2):
                     v = geb[:, :, g * mid : (g + 1) * mid].reshape(images * cols, mid)
                     t = mm(v, wt[g, dy * mid : (dy + 1) * mid])
@@ -1352,9 +1352,9 @@
             mx[i] = v.astype(BF16).reshape(slots, cols, mid)
             return c
 
-        lax.fori_loop(0, images // 2, first_grad, 0)
+        lax.fori_loop(0, images // 2, first_grad, 0, unroll=2)
         reduce_red.second(reduce_piece)
-        lax.fori_loop(images // 2, images, first_grad, 0)
+        lax.fori_loop(images // 2, images, first_grad, 0, unroll=2)
         out_fg = pltpu.make_async_copy(mx, fg_hbm, lsem.at[7])
         out_fg.start()
         reduce_red.third()

time: 195 us -> 195 us (level)
  no operation moved by 1% of the time
where the time goes in v7:
time: 195 us
  Pallas kernels  194 us (99%)
    pallas_call x1, Pallas kernels, call_backward(): pl.pallas_call(functools.partial(backward_kernel, n_img, n_row), out_shap...  90.5 us
    pallas_call x1, Pallas kernels, call_forward(): pl.pallas_call(functools.partial(forward_kernel, n_img, n_row), out_shape...  66.7 us
    pallas_call x1, Pallas kernels, call_third(): pl.pallas_call(third_kernel, out_shape=[sd(x.shape, BF16), sd(x.shape, BF...  25.3 us
    pallas_call x1, Pallas kernels, call_input(): pl.pallas_call(input_kernel, out_shape=[sd(sg.shape, BF16)] + outs, grid=...  11.6 us

profile of v7, /device:TPU:0, one launch (start us, length us, event | category | flops | bytes accessed | tf_op | source)
XLA Modules:
  0.0 195.0 jit_solution(319238862025348421)
XLA Ops:
  0.7 66.7 %forward.1 = (f32[56,6,16,256]{3,2,1,0:T(8,128)}, bf16[56,8,16,768]{3,2,1,0:T(8,128)(2,1)}, f32[56,6,16,512]{3,2,1,0:T(8,128)}, bf16[56,6,16,256]{3,2,1,0:T(8,12...) custom-call(s32[56]{0:T(128)} %bitcast.22, ...), custom_call_target="tpu_custom_call" | custom-call | tf_op jit(solution)/shard_map/forward/pallas_call | solution.py:769
  67.3 25.3 %third.1 = (bf16[56,6,16,1024]{3,2,1,0:T(8,128)(2,1)}, bf16[56,6,16,1024]{3,2,1,0:T(8,128)(2,1)}, f32[56,6,16,256]{3,2,1,0:T(8,128)}, f32[272,1024]{1,0:T(8,128)}) custom-call(s32[56]{0:T(128)} %bitcast.23, s32[56]{0:T(128)} %group.3, bf16[56,6,16,1024]{3,2,1,0:T(8,128)(2,1)} %x_hbm.3, bf16[56,6,16,1024]{3,2,1,0:T(8,128)(2,1)} %cot.1, ...), custom_call_target="tpu_custom_call" | custom-call | tf_op jit(solution)/shard_map/third/pallas_call | solution.py:836
  92.7 90.5 %backward.1 = (bf16[56,6,16,256]{3,2,1,0:T(8,128)(2,1)}, f32[64,1024]{1,0:T(8,128)}, f32[288,512]{1,0:T(8,128)}, f32[256,256]{1,0:T(8,128)}, f32[128,256]{1,0:T(...) custom-call(s32[56]{0:T(128)} %bitcast.24, ...), custom_call_target="tpu_custom_call" | custom-call | tf_op jit(solution)/shard_map/backward/pallas_call | solution.py:1455
  183.2 11.6 %input_grad.1 = (bf16[56,6,16,1024]{3,2,1,0:T(8,128)(2,1)}, f32[64,1024]{1,0:T(8,128)}, f32[288,512]{1,0:T(8,128)}, f32[256,256]{1,0:T(8,128)}, f32[128,512]{1,0...) custom-call(bf16[56,6,16,256]{3,2,1,0:T(8,128)(2,1)} %get-tuple-elem, ...), custom_call_target="tpu_custom_call" | custom-call | tf_op jit(solution)/shard_map/input_grad/pallas_call | solution.py:1509
